TPU v7x, 256 devices: a whole 4x4x8 slice. The times are simulated.
256 devices in a mesh: freq: 4 (over x_hi, core), strip: 64 (over z, y, x_lo).
Axes of the slice: x: 4 (x_hi: 2, x_lo: 2; x = x_hi * 2 + x_lo), y: 4, z: 8, core: 2. Of those that a mesh axis runs over, the one named last changes fastest.
Arguments:
- source_field: bfloat16 [2, 4, 2, 2048, 2048], P(None, 'freq', None, 'strip'), may hold values from -6 to 6
- recorded: bfloat16 [2, 4, 2, 2048, 2048], P(None, 'freq', None, 'strip'), may hold values from -6 to 6
- phase_index: int32 [1, 2, 4], replicated, may hold values from 0 to 7
- slowness: float32 [16, 2048, 2048], P(None, 'strip'), may hold values from 0.8 to 1.2
- slice_index: int32 [4], replicated, may hold values from 0 to 15
Outputs:
- images: float32 [4, 2048, 2048], P(None, 'strip', 'freq')
All inputs are finite; a program needn't handle non-finite values.
Results may differ from a plain program's by a relative error of at most 0.0003.
Values sent between devices are 32-bit elements; how exact they have to be, the bound alone decides.
No kernel may reach another device: no remote copies, remote signals or barrier semaphores. Data moves between devices by JAX's collectives and lax.ppermute only.
A program may use at most 128 MiB of HBM per device.

v0:
```python
import math

import jax
import jax.numpy as jnp
from jax import lax
from jax.sharding import PartitionSpec as P

FACTOR = 16
DEPTHS = 4
PHASES = 8


grid_step = 4.0
depth_step = 8.0
highest = lax.Precision.HIGHEST


def permuted_waves(positions, total_count):
    inner_size = total_count // FACTOR
    natural = positions % inner_size * FACTOR + positions // inner_size
    signed = jnp.where(natural < total_count // 2, natural, natural - total_count).astype(
        jnp.float32
    )
    return signed * (2.0 * math.pi / (total_count * grid_step))


def frequencies(first_index, local_count, total_count):
    position = (first_index + jnp.arange(local_count, dtype=jnp.int32)).astype(jnp.float32)
    return 0.5 + 1.5 * (position + 0.5) / total_count


def propagator(angular, wave_x, wave_y):
    vertical_sq = angular * angular - wave_x * wave_x - wave_y * wave_y
    vertical = jnp.sqrt(jnp.abs(vertical_sq))
    propagating = vertical_sq > 0
    real_part = jnp.where(
        propagating, jnp.cos(depth_step * vertical), jnp.exp(-depth_step * vertical)
    )
    imag_part = jnp.where(propagating, jnp.sin(depth_step * vertical), 0.0)
    return (real_part, imag_part)


def encode(wavefield, encode_angle):
    turn_cos = jnp.cos(encode_angle)[:, :, :, None, None]
    turn_sin = jnp.sin(encode_angle)[:, :, :, None, None]
    real_part = wavefield[:, :, 0].astype(jnp.float32)[None]
    imag_part = wavefield[:, :, 1].astype(jnp.float32)[None]
    return (
        jnp.sum(turn_cos * real_part - turn_sin * imag_part, axis=1),
        jnp.sum(turn_cos * imag_part + turn_sin * real_part, axis=1),
    )


def section_table(first_count, second_count, modulus, direction):
    first_range = jnp.arange(first_count, dtype=jnp.int32)
    second_range = jnp.arange(second_count, dtype=jnp.int32)
    angle = (first_range[:, None] * second_range[None, :] % modulus).astype(jnp.float32) * (
        direction * 2.0 * math.pi / modulus
    )
    cosine = jnp.cos(angle)
    sine = jnp.sin(angle)
    return jnp.stack([jnp.stack([cosine, sine]), jnp.stack([-sine, cosine])])


def twist(field, length, direction):
    inner_size = length // FACTOR
    short_range = jnp.arange(FACTOR, dtype=jnp.int32)
    long_range = jnp.arange(inner_size, dtype=jnp.int32)
    angle = (short_range[:, None] * long_range[None, :] % length).astype(jnp.float32) * (
        direction * 2.0 * math.pi / length
    )
    cosine = jnp.cos(angle)
    sine = jnp.sin(angle)
    return jnp.stack([field[0] * cosine - field[1] * sine, field[0] * sine + field[1] * cosine])


def forward_transform(field, transposed):
    length = field.shape[-1]
    inner_size = length // FACTOR
    lead = field.shape[:-1]
    parts = field.reshape(lead + (FACTOR, inner_size))
    first = jnp.einsum(
        "t...ab,tuak->u...kb", parts, section_table(FACTOR, FACTOR, FACTOR, -1.0), precision=highest
    )
    turned = twist(first, length, -1.0)
    second_table = section_table(inner_size, inner_size, inner_size, -1.0)
    if transposed:
        result = jnp.einsum("t...qkb,tubm->u...kmq", turned, second_table, precision=highest)
        return result.reshape(lead[:-1] + (length, lead[-1]))
    result = jnp.einsum("t...kb,tubm->u...km", turned, second_table, precision=highest)
    return result.reshape(lead + (length,))


def inverse_transform(field, transposed):
    if transposed:
        length = field.shape[-2]
        inner_size = length // FACTOR
        parts = field.reshape(field.shape[:-2] + (FACTOR, inner_size, field.shape[-1]))
        first = jnp.einsum(
            "t...kmq,tumb->u...qkb",
            parts,
            section_table(inner_size, inner_size, inner_size, 1.0),
            precision=highest,
        )
    else:
        length = field.shape[-1]
        inner_size = length // FACTOR
        parts = field.reshape(field.shape[:-1] + (FACTOR, inner_size))
        first = jnp.einsum(
            "t...km,tumb->u...kb",
            parts,
            section_table(inner_size, inner_size, inner_size, 1.0),
            precision=highest,
        )
    turned = twist(first, length, 1.0)
    result = jnp.einsum(
        "t...kb,tuka->u...ab", turned, section_table(FACTOR, FACTOR, FACTOR, 1.0), precision=highest
    )
    return result.reshape(result.shape[:-2] + (length,)) / length


def shift_phase(turned, factor_real, factor_imag):
    spectra = forward_transform(turned, False)
    shifted = jnp.stack(
        [
            spectra[0] * factor_real - spectra[1] * factor_imag,
            spectra[0] * factor_imag + spectra[1] * factor_real,
        ]
    )
    return inverse_transform(shifted, False)


def per_device(source_field, recorded, phase_index, slowness, slice_index):
    freq_local = source_field.shape[1]
    row_count = source_field.shape[3]
    grid_width = source_field.shape[4]
    strips = lax.axis_size("strip")
    columns = grid_width // strips
    height = row_count * strips
    first_freq = lax.axis_index("freq") * freq_local
    total_freq = freq_local * lax.axis_size("freq")
    encode_angle = lax.dynamic_slice_in_dim(phase_index, first_freq, freq_local, 2).astype(
        jnp.float32
    ) * (2.0 * math.pi / PHASES)
    source_real, source_imag = encode(source_field, encode_angle)
    receiver_real, receiver_imag = encode(recorded, encode_angle)
    real_stack = jnp.stack([source_real, receiver_real]).transpose(2, 0, 1, 3, 4)
    imag_stack = jnp.stack([source_imag, receiver_imag]).transpose(2, 0, 1, 3, 4)
    wavefields = jnp.stack([real_stack, imag_stack])
    angular = frequencies(first_freq, freq_local, total_freq)
    column_positions = lax.axis_index("strip") * columns + jnp.arange(columns, dtype=jnp.int32)
    wave_y = permuted_waves(column_positions, grid_width)
    wave_x = permuted_waves(jnp.arange(height, dtype=jnp.int32), height)
    kind_sign = jnp.array([1.0, -1.0], jnp.float32)
    prop_real, prop_imag = propagator(
        angular[:, None, None], wave_y[None, :, None], wave_x[None, None, :]
    )
    factor_real = prop_real[:, None, None]
    factor_imag = prop_imag[:, None, None] * kind_sign[None, :, None, None, None]
    pictures = []
    for descent in range(DEPTHS):
        spectra = forward_transform(wavefields, True)
        turned = lax.all_to_all(spectra[:, 0], "strip", split_axis=3, concat_axis=4, tiled=True)
        turned = shift_phase(turned, factor_real[0], factor_imag[0])
        pieces = [lax.all_to_all(turned, "strip", split_axis=4, concat_axis=3, tiled=True)]
        spectra = jnp.stack(pieces, axis=1)
        spatial = inverse_transform(spectra, True)
        slow_slice = lax.dynamic_index_in_dim(slowness, slice_index[descent], 0, keepdims=False)
        rotation = depth_step * angular[:, None, None] * (slow_slice[None] - 1.0)
        rotate_cos = jnp.cos(rotation)[:, None, None]
        rotate_sin = jnp.sin(rotation)[:, None, None] * kind_sign[None, :, None, None, None]
        wavefields = jnp.stack(
            [
                spatial[0] * rotate_cos - spatial[1] * rotate_sin,
                spatial[0] * rotate_sin + spatial[1] * rotate_cos,
            ]
        )
        product = jnp.sum(wavefields[:, :, 0] * wavefields[:, :, 1], axis=(0, 1, 2)) / total_freq
        pictures.append(lax.psum_scatter(product, "freq", scatter_dimension=1, tiled=True))
    return jnp.stack(pictures)


def solution(mesh):
    placed = (
        P(None, "freq", None, "strip", None),
        P(None, "freq", None, "strip", None),
        P(),
        P(None, "strip", None),
        P(),
    )
    return jax.shard_map(
        per_device, mesh=mesh, in_specs=placed, out_specs=P(None, "strip", "freq"), check_vma=False
    )
```

profile of v0, /device:TPU:1, one launch (start us, length us, event | category | flops | bytes accessed | tf_op | source)
XLA Modules:
  0.0 704.5 jit_solution(10505301404214607464)
XLA Ops:
  17.8 6.5 reshape.1694
  24.3 14.0 %all-to-all-start = ((f32[64,1,4096]{2,1,0:T(1,128)}), f32[64,1,4096]{2,1,0:T(1,128)S(1)}, u32[]{:S(2)}, u32[]{:S(2)}) async-start(f32[64,1,4096]{2,1,0:T(1,128)} %reshape.1694), calls=%async_computation | async-start | bytes 2097152 | tf_op jit(solution)/shard_map/all_to_all | solution.py:163
  40.3 24.1 %all-to-all-done = f32[64,1,4096]{2,1,0:T(1,128)S(1)} async-done(((f32[64,1,4096]{2,1,0:T(1,128)}), f32[64,1,4096]{2,1,0:T(1,128)S(1)}, u32[]{:S(2)}, u32[]{:S(2)}) %all-to-all-start) | async-done | bytes 1048608 | tf_op jit(solution)/shard_map/all_to_all | solution.py:163
  73.1 6.6 copy.537
  92.0 6.5 reshape.1696
  98.6 8.1 %all-to-all-start.1 = ((f32[64,1,4096]{2,1,0:T(1,128)}), f32[64,1,4096]{2,1,0:T(1,128)S(1)}, u32[]{:S(2)}, u32[]{:S(2)}) async-start(f32[64,1,4096]{2,1,0:T(1,128)} %reshape.1696), calls=%async_computation.1 | async-start | bytes 2097152 | tf_op jit(solution)/shard_map/all_to_all | solution.py:165
  120.4 12.1 %all-to-all-done.1 = f32[64,1,4096]{2,1,0:T(1,128)S(1)} async-done(((f32[64,1,4096]{2,1,0:T(1,128)}), f32[64,1,4096]{2,1,0:T(1,128)S(1)}, u32[]{:S(2)}, u32[]{:S(2)}) %all-to-all-start.1) | async-done | bytes 1048608 | tf_op jit(solution)/shard_map/all_to_all | solution.py:165
  140.6 6.6 copy.536
  169.0 33.3 %all_to_all.120 = f32[64,1,4096]{2,1,0:T(1,128)} all-to-all(f32[64,1,4096]{2,1,0:T(1,128)S(1)} %reshape.1698), channel_id=1, replica_groups=mesh['freq'=4,'strip'=64] {'strip'}, dimensions={0} | all-to-all | bytes 2097152 | tf_op jit(solution)/shard_map/all_to_all | solution.py:163
  211.5 6.6 copy.535
  236.3 33.5 %all_to_all.121 = f32[64,1,4096]{2,1,0:T(1,128)} all-to-all(f32[64,1,4096]{2,1,0:T(1,128)S(1)} %reshape.1700), channel_id=1, replica_groups=mesh['freq'=4,'strip'=64] {'strip'}, dimensions={0} | all-to-all | bytes 2097152 | tf_op jit(solution)/shard_map/all_to_all | solution.py:165
  279.0 6.6 copy.534
  300.0 6.5 copy.229
  306.5 6.5 reshape.1702
  313.0 33.8 %all_to_all.122 = f32[64,1,4096]{2,1,0:T(1,128)} all-to-all(f32[64,1,4096]{2,1,0:T(1,128)} %reshape.1702), channel_id=1, replica_groups=mesh['freq'=4,'strip'=64] {'strip'}, dimensions={0} | all-to-all | bytes 2097152 | tf_op jit(solution)/shard_map/all_to_all | solution.py:163
  352.1 5.9 reshape.1703
  357.9 6.6 copy.533
  381.3 6.5 reshape.1704
  387.8 33.2 %all_to_all.123 = f32[64,1,4096]{2,1,0:T(1,128)} all-to-all(f32[64,1,4096]{2,1,0:T(1,128)} %reshape.1704), channel_id=1, replica_groups=mesh['freq'=4,'strip'=64] {'strip'}, dimensions={0} | all-to-all | bytes 2097152 | tf_op jit(solution)/shard_map/all_to_all | solution.py:165
  426.3 5.9 reshape.1705
  432.2 6.6 copy.532
  458.3 6.5 copy.247
  464.8 6.5 reshape.1706
  471.3 33.4 %all_to_all.124 = f32[64,1,4096]{2,1,0:T(1,128)} all-to-all(f32[64,1,4096]{2,1,0:T(1,128)} %reshape.1706), channel_id=1, replica_groups=mesh['freq'=4,'strip'=64] {'strip'}, dimensions={0} | all-to-all | bytes 2097152 | tf_op jit(solution)/shard_map/all_to_all | solution.py:163
  515.9 6.6 copy.531
  539.3 6.5 reshape.1708
  545.8 8.5 %all-to-all-start.7 = ((f32[64,1,4096]{2,1,0:T(1,128)}), f32[64,1,4096]{2,1,0:T(1,128)}, u32[]{:S(2)}, u32[]{:S(2)}) async-start(f32[64,1,4096]{2,1,0:T(1,128)} %reshape.1708), calls=%async_computation.10 | async-start | bytes 2097152 | tf_op jit(solution)/shard_map/all_to_all | solution.py:165
  558.2 20.6 %all-to-all-done.7 = f32[64,1,4096]{2,1,0:T(1,128)} async-done(((f32[64,1,4096]{2,1,0:T(1,128)}), f32[64,1,4096]{2,1,0:T(1,128)}, u32[]{:S(2)}, u32[]{:S(2)}) %all-to-all-start.7) | async-done | bytes 1048608 | tf_op jit(solution)/shard_map/all_to_all | solution.py:165
  588.1 6.6 copy.530
  602.4 24.9 %reduce-scatter.7.cloned.1.call-done = f32[32,512]{1,0:T(8,128)} async-done(((f32[32,2048]{1,0:T(8,128)}), f32[32,512]{1,0:T(8,128)}) %reduce-scatter.7.cloned.1.call-update) | async-done | bytes 65552 | tf_op jit(solution)/shard_map/reduce_scatter | solution.py:179
  627.3 34.3 %reduce-scatter.9.cloned.1.call-done = f32[32,512]{1,0:T(8,128)} async-done(((f32[32,2048]{1,0:T(8,128)}), f32[32,512]{1,0:T(8,128)}) %reduce-scatter.9.cloned.1.call-update) | async-done | bytes 65552 | tf_op jit(solution)/shard_map/reduce_scatter | solution.py:179
  661.6 34.3 %reduce-scatter.11.cloned.1.call-done = f32[32,512]{1,0:T(8,128)} async-done(((f32[32,2048]{1,0:T(8,128)}), f32[32,512]{1,0:T(8,128)}) %reduce-scatter.11.cloned.1.call-update) | async-done | bytes 65552 | tf_op jit(solution)/shard_map/reduce_scatter | solution.py:179
  (180 shorter events, 217.8 us)
Async XLA Ops:
  24.3 40.1 %all-to-all-start = ((f32[64,1,4096]{2,1,0:T(1,128)}), f32[64,1,4096]{2,1,0:T(1,128)S(1)}, u32[]{:S(2)}, u32[]{:S(2)}) async-start(f32[64,1,4096]{2,1,0:T(1,128)} %reshape.1694), calls=%async_computation | async-start | bytes 2097152 | tf_op jit(solution)/shard_map/all_to_all | solution.py:163
  83.1 2.5 copy-start.4
  92.0 14.7 %copy-start.5 = (s32[4]{0:T(128)S(1)}, s32[4]{0:T(128)}, u32[]{:S(2)}) copy-start(s32[4]{0:T(128)} %param.10) | copy-start | bytes 52
  98.6 34.0 %all-to-all-start.1 = ((f32[64,1,4096]{2,1,0:T(1,128)}), f32[64,1,4096]{2,1,0:T(1,128)S(1)}, u32[]{:S(2)}, u32[]{:S(2)}) async-start(f32[64,1,4096]{2,1,0:T(1,128)} %reshape.1696), calls=%async_computation.1 | async-start | bytes 2097152 | tf_op jit(solution)/shard_map/all_to_all | solution.py:165
  454.0 1.5 copy-start
  454.0 1.5 copy-start.2
  545.8 10.3 %copy-start.1 = (f32[1,1,2,1,32,2048]{5,4,2,3,1,0:T(8,128)S(1)}, f32[1,1,2,1,32,2048]{5,4,2,3,1,0:T(8,128)}, u32[]{:S(2)}) copy-start(f32[1,1,2,1,32,2048]{5,4,2,3,1,0:T(8,128)} %copy-done) | copy-start | bytes 1572868
  545.8 33.1 %all-to-all-start.7 = ((f32[64,1,4096]{2,1,0:T(1,128)}), f32[64,1,4096]{2,1,0:T(1,128)}, u32[]{:S(2)}, u32[]{:S(2)}) async-start(f32[64,1,4096]{2,1,0:T(1,128)} %reshape.1708), calls=%async_computation.10 | async-start | bytes 2097152 | tf_op jit(solution)/shard_map/all_to_all | solution.py:165
  554.3 48.1 %reduce-scatter.5.cloned.1.call-start = ((), (), s32[]{:S(2)}) async-start(), calls=%async_computation.12 | async-start | bytes 327680 | tf_op jit(solution)/shard_map/reduce_scatter | solution.py:179
  555.1 72.2 %reduce-scatter.7.cloned.1.call-start = ((), (), s32[]{:S(2)}) async-start(), calls=%async_computation.13 | async-start | bytes 327680 | tf_op jit(solution)/shard_map/reduce_scatter | solution.py:179
  556.0 105.6 %reduce-scatter.9.cloned.1.call-start = ((), (), s32[]{:S(2)}) async-start(), calls=%async_computation.14 | async-start | bytes 327680 | tf_op jit(solution)/shard_map/reduce_scatter | solution.py:179
  557.9 138.0 %reduce-scatter.11.cloned.1.call-start = ((), (), s32[]{:S(2)}) async-start(), calls=%async_computation.15 | async-start | bytes 327680 | tf_op jit(solution)/shard_map/reduce_scatter | solution.py:179
  599.3 1.9 copy-start.3
Sparse Core Ops, SparseCore 0:
  557.8 34.9 reduce-scatter.4
  595.7 31.5 reduce-scatter.6
  630.0 31.5 reduce-scatter.8
  664.3 31.5 reduce-scatter.10
where the time goes:
time: 714 us; the launch traced here: 705 us
  local copies, waits for them, and re-layouts  227 us (32%)
  blocking collectives  167 us (23%)
  waiting for transfers between devices  150 us (21%)
  other arithmetic  61.8 us (9%)
  matrix products  44.8 us (6%)
  starting transfers between devices  31.1 us (4%)
  between operations  22.2 us (3%)
    all_to_all x3, blocking collectives, per_device(): lax.all_to_all(spectra[:, 0], 'strip', split_axis=3, concat_axis=4, tiled...  100 us
    reduce_scatter x4, waiting for transfers between devices, per_device(): lax.psum_scatter(product, 'freq', scatter_dimension=1, tiled=True)  93.5 us
    unnamed x38, local copies, waits for them, and re-layouts  93.4 us
    all_to_all x2, blocking collectives, per_device(): lax.all_to_all(turned, 'strip', split_axis=4, concat_axis=3, tiled=True)  66.7 us
    all_to_all x2, waiting for transfers between devices, per_device(): lax.all_to_all(turned, 'strip', split_axis=4, concat_axis=3, tiled=True)  32.7 us
    another operation x8, local copies, waits for them, and re-layouts  30.7 us
    all_to_all x5, local copies, waits for them, and re-layouts, per_device(): lax.all_to_all(spectra[:, 0], 'strip', split_axis=3, concat_axis=4, tiled...  26.8 us
    all_to_all x4, local copies, waits for them, and re-layouts, per_device(): lax.all_to_all(turned, 'strip', split_axis=4, concat_axis=3, tiled=True)  26.3 us
  transfers between devices with their start and end apart: 7, of which 6 were waited for; matrix products, arithmetic and copies ran while one was open for 5% of the time, Pallas kernels for 0%

commit v1 on v0

v1 whole, which is shorter than its diff:
```python
import functools
import math

import jax
import jax.numpy as jnp
import numpy as np
from jax import lax
from jax.experimental import pallas as pl
from jax.experimental.pallas import tpu as pltpu
from jax.sharding import PartitionSpec as P

DEPTHS = 4
PHASES = 8
SIZE = 2048
RADIX = 16
INNER = SIZE // RADIX
HALF = 64
ROWS = 64
VMEM_LIMIT = 40 * 1024 * 1024

grid_step = 4.0
depth_step = 8.0


def split_table(table):
    high = table.astype(jnp.bfloat16)
    low = (table - high.astype(np.float64)).astype(jnp.bfloat16)
    return high, low


def inner_dft(direction):
    index = np.arange(INNER)
    angle = direction * 2.0 * np.pi * (np.outer(index, index) % INNER) / INNER
    return np.cos(angle), np.sin(angle)


def lane_tables():
    cosine, sine = inner_dft(-1.0)
    real_columns = np.concatenate([cosine, -sine], axis=0)
    imag_columns = np.concatenate([sine, cosine], axis=0)
    forward = np.concatenate(
        [
            part[:, half * HALF : (half + 1) * HALF]
            for half in range(2)
            for part in (real_columns, imag_columns)
        ],
        axis=1,
    )
    cosine, sine = inner_dft(1.0)
    real_rows = np.concatenate([cosine, sine], axis=1)
    imag_rows = np.concatenate([-sine, cosine], axis=1)
    inverse = (
        np.concatenate(
            [
                part[half * HALF : (half + 1) * HALF]
                for half in range(2)
                for part in (real_rows, imag_rows)
            ],
            axis=0,
        )
        / SIZE
    )
    out = []
    for table in (forward, inverse):
        high, low = split_table(table)
        out.append(np.concatenate([high, low, high], axis=0))
    return out


def row_tables():
    out = []
    for direction, scale in ((-1.0, 1.0), (1.0, 1.0 / SIZE)):
        cosine, sine = inner_dft(direction)
        high, low = split_table(np.concatenate([cosine, sine], axis=0) * scale)
        out.append(np.concatenate([high, low, high], axis=1))
    return out


def twiddles():
    angle = -2.0 * np.pi * np.outer(np.arange(RADIX), np.arange(INNER)) / SIZE
    return np.cos(angle), np.sin(angle)


def lane_twiddles():
    cosine, sine = twiddles()
    return np.concatenate([cosine, sine], axis=1).astype(np.float32)


def row_twiddles():
    cosine, sine = twiddles()
    sign = np.where(np.arange(2 * HALF) < HALF, -1.0, 1.0)
    return (
        np.broadcast_to(cosine[:, :, None], (RADIX, INNER, 2 * HALF)).astype(np.float32),
        (sine[:, :, None] * sign[None, None, :]).astype(np.float32),
    )


def butterfly16(values, direction, add, sub, turn, scale_by):
    def four(a, b, c, d):
        even_sum, even_diff = add(a, c), sub(a, c)
        odd_sum, odd_diff = add(b, d), turn(sub(b, d), direction)
        return [
            add(even_sum, odd_sum),
            add(even_diff, odd_diff),
            sub(even_sum, odd_sum),
            sub(even_diff, odd_diff),
        ]

    first = [four(*[values[4 * n + m] for n in range(4)]) for m in range(4)]
    result = [None] * 16
    for k in range(4):
        column = []
        for m in range(4):
            value = first[m][k]
            power = m * k
            if power == 4:
                value = turn(value, direction)
            elif power:
                angle = direction * 2.0 * math.pi * power / 16
                value = scale_by(value, math.cos(angle), math.sin(angle))
            column.append(value)
        for m, value in enumerate(four(*column)):
            result[k + 4 * m] = value
    return result


def pair_add(a, b):
    return (a[0] + b[0], a[1] + b[1])


def pair_sub(a, b):
    return (a[0] - b[0], a[1] - b[1])


def pair_turn(a, s):
    return (-a[1], a[0]) if s > 0 else (a[1], -a[0])


def pair_scale(a, c, s):
    return (a[0] * c - a[1] * s, a[0] * s + a[1] * c)


def swap_halves(value):
    return pltpu.roll(value, HALF, 1)


def half_sign():
    lane = lax.broadcasted_iota(jnp.int32, (8, 2 * HALF), 1)
    return jnp.where(lane < HALF, -1.0, 1.0).astype(jnp.float32)


def split_value(value):
    high = value.astype(jnp.bfloat16)
    low = (value - high.astype(jnp.float32)).astype(jnp.bfloat16)
    return high, low


def sine_cosine(angle):
    turns = jnp.round(angle * (2.0 / math.pi))
    rest = angle - turns * 1.5703125
    rest = rest - turns * 4.8375129699707031e-4
    rest = rest - turns * 7.5497899548918821e-8
    square = rest * rest
    sine = rest + rest * square * (
        -1.6666654611e-1 + square * (8.3321608736e-3 - square * 1.9515295891e-4)
    )
    cosine = (
        1.0
        - 0.5 * square
        + square
        * square
        * (4.166664568298827e-2 + square * (-1.388731625493765e-3 + square * 2.443315711809948e-5))
    )
    quarter = turns.astype(jnp.int32)
    odd = (quarter & 1) == 1
    sine_out = jnp.where(odd, cosine, sine)
    cosine_out = jnp.where(odd, sine, cosine)
    sine_out = jnp.where((quarter & 2) == 2, -sine_out, sine_out)
    cosine_out = jnp.where(((quarter + 1) & 2) == 2, -cosine_out, cosine_out)
    return sine_out, cosine_out


def lanes(a):
    return slice(a * INNER, (a + 1) * INNER)


def forward_rows(wave, work, table, twiddle, out):
    @pl.loop(0, ROWS // 8)
    def _(tile):
        rows = pl.ds(tile * 8, 8)
        values = [(wave[0, rows, lanes(a)], wave[1, rows, lanes(a)]) for a in range(RADIX)]
        values = butterfly16(values, -1.0, pair_add, pair_sub, pair_turn, pair_scale)
        for k, (real, imag) in enumerate(values):
            if k:
                cosine = twiddle[k : k + 1, :INNER]
                sine = twiddle[k : k + 1, INNER:]
                real, imag = real * cosine - imag * sine, real * sine + imag * cosine
            work[k, rows, :INNER] = real
            work[k, rows, INNER:] = imag

    for group in range(0, RADIX, 4):
        value = work[group : group + 4].reshape(4 * ROWS, 2 * INNER)
        high, low = split_value(value)
        result = jnp.dot(
            jnp.concatenate([high, high, low], axis=1),
            table[...],
            preferred_element_type=jnp.float32,
        )
        result = result.reshape(4, ROWS, 2 * INNER)
        for k in range(4):
            for kind in range(2):
                for half in range(2):
                    out[(kind * RADIX + group + k) * 2 + half] = result[
                        k,
                        kind * (ROWS // 2) : (kind + 1) * (ROWS // 2),
                        half * INNER : (half + 1) * INNER,
                    ]


def inverse_rows(chunks, work, table, twiddle, wave):
    for group in range(0, RADIX, 4):
        parts = []
        for k in range(4):
            for kind in range(2):
                place = (kind * RADIX + group + k) * 2
                parts.append(jnp.concatenate([chunks[place], chunks[place + 1]], axis=1))
        high, low = split_value(jnp.concatenate(parts, axis=0))
        result = jnp.dot(
            jnp.concatenate([high, high, low], axis=1),
            table[...],
            preferred_element_type=jnp.float32,
        )
        work[group : group + 4] = result.reshape(4, ROWS, 2 * INNER)

    @pl.loop(0, ROWS // 8)
    def _(tile):
        rows = pl.ds(tile * 8, 8)
        values = []
        for k in range(RADIX):
            real, imag = work[k, rows, :INNER], work[k, rows, INNER:]
            if k:
                cosine = twiddle[k : k + 1, :INNER]
                sine = twiddle[k : k + 1, INNER:]
                real, imag = real * cosine + imag * sine, imag * cosine - real * sine
            values.append((real, imag))
        values = butterfly16(values, 1.0, pair_add, pair_sub, pair_turn, pair_scale)
        for a, (real, imag) in enumerate(values):
            wave[0, rows, lanes(a)] = real
            wave[1, rows, lanes(a)] = imag


def rotate_and_image(wave, slow, angular, image, keep):
    half_rows = ROWS // 2
    parts = image.shape[0]
    width = SIZE // parts

    @pl.loop(0, half_rows // 8)
    def _(tile):
        first = pl.ds(tile * 8, 8)
        second = pl.ds(half_rows + tile * 8, 8)
        for a in range(SIZE // 512):
            columns = slice(a * 512, (a + 1) * 512)
            sine, cosine = sine_cosine(angular * (slow[0, first, columns] - 1.0))
            turned = []
            for rows in (first, second):
                real, imag = wave[0, rows, columns], wave[1, rows, columns]
                real, imag = real * cosine - imag * sine, real * sine + imag * cosine
                if keep:
                    wave[0, rows, columns] = real
                    wave[1, rows, columns] = imag
                turned.append((real, imag))
            picture = turned[0][0] * turned[1][0] - turned[0][1] * turned[1][1]
            place = a * 512 // width
            offset = a * 512 % width
            image[place, first, offset : offset + 512] = picture * 0.25


def first_kernel(turn_ref, source, recorded, table, twiddle, out, wave, work):
    half_rows = ROWS // 2

    @pl.loop(0, half_rows // 16)
    def _(tile):
        rows = pl.ds(tile * 16, 16)
        for kind, field in enumerate((source, recorded)):
            place = pl.ds(kind * half_rows + tile * 16, 16)
            for a in range(SIZE // 512):
                columns = slice(a * 512, (a + 1) * 512)
                real_sum, imag_sum = None, None
                for shot in range(field.shape[0]):
                    real = field[shot, 0, 0, rows, columns].astype(jnp.float32)
                    imag = field[shot, 0, 1, rows, columns].astype(jnp.float32)
                    cosine, sine = turn_ref[0, shot], turn_ref[1, shot]
                    real_part = cosine * real - sine * imag
                    imag_part = cosine * imag + sine * real
                    real_sum = real_part if real_sum is None else real_sum + real_part
                    imag_sum = imag_part if imag_sum is None else imag_sum + imag_part
                wave[0, place, columns] = real_sum
                wave[1, place, columns] = imag_sum if kind == 0 else -imag_sum

    forward_rows(wave, work, table, twiddle, out)


def middle_kernel(
    index_ref, angular_ref, chunks, slow, inverse_table, table, twiddle, out, image, wave, work
):
    inverse_rows(chunks, work, inverse_table, twiddle, wave)
    rotate_and_image(wave, slow, angular_ref[0], image, True)
    forward_rows(wave, work, table, twiddle, out)


def last_kernel(index_ref, angular_ref, chunks, slow, inverse_table, twiddle, image, wave, work):
    inverse_rows(chunks, work, inverse_table, twiddle, wave)
    rotate_and_image(wave, slow, angular_ref[0], image, False)


WAVE = pltpu.VMEM((2, ROWS, SIZE), jnp.float32)
WORK = pltpu.VMEM((RADIX, ROWS, 2 * INNER), jnp.float32)
CHUNKS = jax.ShapeDtypeStruct((64, ROWS // 2, 2 * HALF), jnp.float32)


def whole():
    return pl.BlockSpec(memory_space=pltpu.VMEM)


def params():
    return pltpu.CompilerParams(vmem_limit_bytes=VMEM_LIMIT)


def first_step(turn, source, recorded, table, twiddle):
    return pl.pallas_call(
        first_kernel,
        out_shape=CHUNKS,
        in_specs=[pl.BlockSpec(memory_space=pltpu.SMEM)] + [whole()] * 4,
        out_specs=whole(),
        scratch_shapes=[WAVE, WORK],
        compiler_params=params(),
        name="encode_forward",
    )(turn, source, recorded, table, twiddle)


def space_step(slice_at, angular, chunks, slowness, tables, twiddle, parts, last):
    rows = ROWS // 2

    def fixed(shape):
        return pl.BlockSpec(shape, lambda i, *scalars: (0,) * len(shape))

    image = jax.ShapeDtypeStruct((parts, rows, SIZE // parts), jnp.float32)
    constants = [tables[1], twiddle] if last else [tables[1], tables[0], twiddle]
    out_shape = [image] if last else [CHUNKS, image]
    return pl.pallas_call(
        last_kernel if last else middle_kernel,
        out_shape=out_shape,
        grid_spec=pltpu.PrefetchScalarGridSpec(
            num_scalar_prefetch=2,
            grid=(1,),
            in_specs=[
                fixed(chunks.shape),
                pl.BlockSpec((1, rows, SIZE), lambda i, place, angle: (place[0], 0, 0)),
            ]
            + [fixed(c.shape) for c in constants],
            out_specs=[fixed(o.shape) for o in out_shape],
            scratch_shapes=[WAVE, WORK],
        ),
        compiler_params=params(),
        name="space_last" if last else "space_step",
    )(slice_at, angular, chunks, slowness, *constants)


def spectral_kernel(chunks, left, left_inverse, twiddle_cos, twiddle_sin, prop_a, prop_b, out, work):
    sign = half_sign()

    def turn(value, direction):
        return swap_halves(value) * (sign if direction > 0 else -sign)

    def scale_by(value, c, s):
        return value * c + swap_halves(value) * (sign * s)

    def add(a, b):
        return a + b

    def sub(a, b):
        return a - b

    tile_rows = 8
    per_chunk = chunks.shape[1]

    def place(a, tile):
        row = a * INNER + tile * tile_rows
        return row // per_chunk, row % per_chunk

    for tile in range(INNER // tile_rows):
        rows = slice(tile * tile_rows, (tile + 1) * tile_rows)
        values = []
        for a in range(RADIX):
            chunk, row = place(a, tile)
            values.append(chunks[chunk, row : row + tile_rows, :])
        values = butterfly16(values, -1.0, add, sub, turn, scale_by)
        for k, value in enumerate(values):
            if k:
                value = value * twiddle_cos[k, rows] + swap_halves(value) * twiddle_sin[k, rows]
            work[k, rows] = value

    wide_sign = jnp.concatenate([sign, sign], axis=1)[:1]

    def multiply(matrix, value):
        high, low = split_value(value)
        result = jnp.dot(
            matrix[...],
            jnp.concatenate([high, high, low], axis=0),
            preferred_element_type=jnp.float32,
        )
        swapped = jnp.concatenate(
            [swap_halves(result[INNER:, :INNER]), swap_halves(result[INNER:, INNER:])], axis=1
        )
        return result[:INNER] + swapped * wide_sign

    for pair in range(0, RADIX, 2):
        value = jnp.concatenate([work[pair], work[pair + 1]], axis=1)
        value = multiply(left, value)
        shifted = []
        for k in range(2):
            part = value[:, k * INNER : (k + 1) * INNER]
            shifted.append(part * prop_a[pair + k] + swap_halves(part) * prop_b[pair + k])
        value = multiply(left_inverse, jnp.concatenate(shifted, axis=1))
        work[pair] = value[:, :INNER]
        work[pair + 1] = value[:, INNER:]

    for tile in range(INNER // tile_rows):
        rows = slice(tile * tile_rows, (tile + 1) * tile_rows)
        values = []
        for k in range(RADIX):
            value = work[k, rows]
            if k:
                value = value * twiddle_cos[k, rows] - swap_halves(value) * twiddle_sin[k, rows]
            values.append(value)
        values = butterfly16(values, 1.0, add, sub, turn, scale_by)
        for a, value in enumerate(values):
            chunk, row = place(a, tile)
            out[chunk, row : row + tile_rows, :] = value


def spectral_step(chunks, left_tables, row_twiddle, propagators):
    return pl.pallas_call(
        spectral_kernel,
        out_shape=jax.ShapeDtypeStruct(chunks.shape, jnp.float32),
        in_specs=[whole()] * 7,
        out_specs=whole(),
        scratch_shapes=[pltpu.VMEM((RADIX, INNER, 2 * HALF), jnp.float32)],
        compiler_params=params(),
        name="spectral_step",
    )(chunks, *left_tables, *row_twiddle, *propagators)


def wavenumber(index):
    signed = jnp.where(index < SIZE // 2, index, index - SIZE).astype(jnp.float32)
    return signed * (2.0 * math.pi / (SIZE * grid_step))


def propagator_tables(angular, strip):
    block = strip % (2 * RADIX)
    lane = jnp.arange(2 * HALF, dtype=jnp.int32) % HALF
    column = block // 2 + RADIX * ((block % 2) * HALF + lane)
    wave_y = wavenumber(column)[None, None, :]
    row = (
        jnp.arange(RADIX, dtype=jnp.int32)[:, None]
        + RADIX * jnp.arange(INNER, dtype=jnp.int32)[None, :]
    )
    wave_x = wavenumber(row)[:, :, None]
    vertical_sq = angular * angular - wave_x * wave_x - wave_y * wave_y
    vertical = jnp.sqrt(jnp.abs(vertical_sq))
    propagating = vertical_sq > 0
    sine, cosine = sine_cosine(depth_step * vertical)
    real_part = jnp.where(propagating, cosine, jnp.exp(-depth_step * vertical))
    imag_part = jnp.where(propagating, sine, 0.0)
    sign = jnp.where(jnp.arange(2 * HALF) < HALF, -1.0, 1.0).astype(jnp.float32)
    return real_part, imag_part * sign[None, None, :]


def per_device(source_field, recorded, phase_index, slowness, slice_index):
    freq = lax.axis_index("freq")
    strip = lax.axis_index("strip")
    parts = lax.axis_size("freq")
    total_freq = source_field.shape[1] * parts
    encode_angle = lax.dynamic_slice_in_dim(phase_index, freq, 1, 2)[0, :, 0].astype(
        jnp.float32
    ) * (2.0 * math.pi / PHASES)
    turn = jnp.stack([jnp.cos(encode_angle), jnp.sin(encode_angle)])
    angular = 0.5 + 1.5 * (freq.astype(jnp.float32) + 0.5) / total_freq

    right = [jnp.asarray(t) for t in lane_tables()]
    left = [jnp.asarray(t) for t in row_tables()]
    lane_twiddle = jnp.asarray(lane_twiddles())
    row_twiddle = [jnp.asarray(t) for t in row_twiddles()]
    propagators = propagator_tables(angular, strip)

    def exchange(chunks):
        return lax.all_to_all(chunks, "strip", 0, 0, tiled=True)

    chunks = first_step(turn, source_field, recorded, right[0], lane_twiddle)
    scaled = (depth_step * angular)[None]
    pictures = []
    for descent in range(DEPTHS):
        chunks = exchange(chunks)
        chunks = spectral_step(chunks, left, row_twiddle, propagators)
        chunks = exchange(chunks)
        last = descent == DEPTHS - 1
        result = space_step(
            slice_index[descent : descent + 1],
            scaled,
            chunks,
            slowness,
            right,
            lane_twiddle,
            parts,
            last,
        )
        if last:
            image = result[0]
            pictures.append(jnp.sum(lax.all_to_all(image, "freq", 0, 0, tiled=True), axis=0))
        else:
            chunks, image = result
            pictures.append(lax.psum_scatter(image, "freq", scatter_dimension=0, tiled=False))
    return jnp.stack(pictures)


def solution(mesh):
    placed = (
        P(None, "freq", None, "strip", None),
        P(None, "freq", None, "strip", None),
        P(),
        P(None, "strip", None),
        P(),
    )
    return jax.shard_map(
        per_device, mesh=mesh, in_specs=placed, out_specs=P(None, "strip", "freq"), check_vma=False
    )
```

time: 714 us -> 412 us (0.58); the launches traced: 705 us -> 411 us
  local copies, waits for them, and re-layouts: 227 us -> 16.4 us
  other arithmetic: 61.8 us -> 4.67 us
  matrix products: 44.8 us -> 0 us
  Pallas kernels: 0 us -> 29.2 us
  blocking collectives: 167 us -> 180 us
  waiting for transfers between devices: 150 us -> 137 us
  between operations: 22.2 us -> 13.4 us
    unnamed x38 -> x46, local copies, waits for them, and re-layouts: 93.4 us -> 14.9 us
    all_to_all x9 -> x0, local copies, waits for them, and re-layouts: 53.2 us -> none  [the longest x5 26.8 us: per_device(): lax.all_to_all(spectra[:, 0], 'strip', split_axis=3, concat_axis=4, tiled...]
    another operation x12 -> x0, local copies, waits for them, and re-layouts: 52.6 us -> none
    dot_general x32 -> x0, matrix products: 44.8 us -> none  [the longest x8 14.5 us: inverse_transform(): jnp.einsum('t...kb,tuka->u...ab', turned, section_table(FACTOR, FACTOR, F...]
    all_to_all x8 -> x0, other arithmetic: 35.6 us -> none  [the longest x4 18.3 us: per_device(): lax.all_to_all(spectra[:, 0], 'strip', split_axis=3, concat_axis=4, tiled...]
    reduce_scatter x4 -> x3, waiting for transfers between devices: 93.5 us -> 64.2 us  [per_device(): lax.psum_scatter(image, 'freq', scatter_dimension=0, tiled=False)]
    pallas_call x0 -> x9, Pallas kernels: none -> 29.2 us  [the longest x4 14 us: spectral_step(): pl.pallas_call(spectral_kernel, out_shape=jax.ShapeDtypeStruct(chunks.sha...]
    div x4 -> x0, local copies, waits for them, and re-layouts: 15.7 us -> none  [inverse_transform(): return result.reshape(result.shape[:-2] + (length,)) / length]
  transfers between devices with their start and end apart: 7 -> 6, of which waited for: 6 -> 5; matrix products, arithmetic and copies ran while one was open for 5% -> 1% of each run, Pallas kernels for 0% -> 1%
where the time goes in v1:
time: 412 us; the launch traced here: 411 us
  blocking collectives  180 us (44%)
  waiting for transfers between devices  137 us (33%)
  starting transfers between devices  30.3 us (7%)
  Pallas kernels  29.2 us (7%)
  local copies, waits for them, and re-layouts  16.4 us (4%)
  between operations  13.4 us (3%)
  other arithmetic  4.67 us (1%)
    all_to_all x5, blocking collectives, exchange(): return lax.all_to_all(chunks, 'strip', 0, 0, tiled=True)  165 us
    all_to_all x3, waiting for transfers between devices, exchange(): return lax.all_to_all(chunks, 'strip', 0, 0, tiled=True)  70.6 us
    reduce_scatter x3, waiting for transfers between devices, per_device(): lax.psum_scatter(image, 'freq', scatter_dimension=0, tiled=False)  64.2 us
    all_to_all x3, starting transfers between devices, exchange(): return lax.all_to_all(chunks, 'strip', 0, 0, tiled=True)  30.1 us
    all_to_all x1, blocking collectives, per_device(): lax.all_to_all(image, 'freq', 0, 0, tiled=True)  15.4 us
    unnamed x46, local copies, waits for them, and re-layouts  14.9 us
    pallas_call x4, Pallas kernels, spectral_step(): pl.pallas_call(spectral_kernel, out_shape=jax.ShapeDtypeStruct(chunks.sha...  14 us
    pallas_call x4, Pallas kernels, space_step(): pl.pallas_call(last_kernel if last else middle_kernel, out_shape=out_shap...  12.5 us
  transfers between devices with their start and end apart: 6, of which 5 were waited for; matrix products, arithmetic and copies ran while one was open for 1% of the time, Pallas kernels for 1%

profile of v1, /device:TPU:1, one launch (start us, length us, event | category | flops | bytes accessed | tf_op | source)
XLA Modules:
  0.0 411.2 jit_solution(3367938238181925069)
XLA Ops:
  6.5 1.0 cosine_reduce_fusion
  8.6 1.0 copy-done.16
  9.6 1.0 copy-done.17
  11.4 2.7 encode_forward.1
  14.1 13.8 %all-to-all-start = ((f32[64,32,128]{2,1,0:T(8,128)}), f32[64,32,128]{2,1,0:T(8,128)}, u32[]{:S(2)}, u32[]{:S(2)}) async-start(f32[64,32,128]{2,1,0:T(8,128)} %encode_forward.1), calls=%async_computation | async-start | bytes 2097152 | tf_op jit(solution)/shard_map/all_to_all | solution.py:497
  28.1 2.0 fusion.2
  30.0 23.9 %all-to-all-done.chunks = f32[64,32,128]{2,1,0:T(8,128)} async-done(((f32[64,32,128]{2,1,0:T(8,128)}), f32[64,32,128]{2,1,0:T(8,128)}, u32[]{:S(2)}, u32[]{:S(2)}) %all-to-all-start) | async-done | bytes 1048608 | tf_op jit(solution)/shard_map/all_to_all | solution.py:497
  53.9 1.2 copy-done.4
  57.0 4.4 %spectral_step.4 = f32[64,32,128]{2,1,0:T(8,128)S(1)} custom-call(f32[64,32,128]{2,1,0:T(8,128)} %all-to-all-done.chunks, bf16[256,384]{1,0:T(8,128)(2,1)S(1)} %copy-done.14, bf16[256,384]{1,0:T(8,128)(2,1)S(1)} %copy-done.12, f32[16,128,128]{2,1,0:T(8,128)S(1)} %copy-done.4, f32[16,128,128]{2,1,0:T(8,128)S(1)} %copy-done.3, ...), custom_call_target="tpu_custom_call" | custom-call | tf_op jit(solution)/shard_map/spectral_step/pallas_call | solution.py:443
  62.4 8.2 %all-to-all-start.1 = ((f32[64,32,128]{2,1,0:T(8,128)}), f32[64,32,128]{2,1,0:T(8,128)}, u32[]{:S(2)}, u32[]{:S(2)}) async-start(f32[64,32,128]{2,1,0:T(8,128)} %copy-done.11), calls=%async_computation.1 | async-start | bytes 2097152 | tf_op jit(solution)/shard_map/all_to_all | solution.py:497
  70.6 1.5 fusion.42
  72.1 24.2 %all-to-all-done.1.chunks = f32[64,32,128]{2,1,0:T(8,128)} async-done(((f32[64,32,128]{2,1,0:T(8,128)}), f32[64,32,128]{2,1,0:T(8,128)}, u32[]{:S(2)}, u32[]{:S(2)}) %all-to-all-start.1) | async-done | bytes 1048608 | tf_op jit(solution)/shard_map/all_to_all | solution.py:497
  96.3 2.2 copy-done
  99.5 4.4 %space_step.3 = (f32[64,32,128]{2,1,0:T(8,128)S(1)}, f32[4,32,512]{2,1,0:T(8,128)S(1)}) custom-call(s32[1]{0:T(128)} %get-tuple-element.21.index_ref, f32[1]{0:T(128)} %bitcast.angular_ref, f32[64,32,128]{2,1,0:T(8,128)} %all-to-all-done.1.chunks, f32[16,32,2048]{2,1,0:T(8,128)S(1)} %copy-done, bf16[768,256]{1,0:T(8,128)(2,1)S(1)} %copy-done.6, ...), custom_call_target="tpu_custom_call" | custom-call | tf_op jit(solution)/shard_map/space_step/pallas_call | solution.py:350
  103.9 33.0 %all_to_all.45.chunks = f32[64,32,128]{2,1,0:T(8,128)S(1)} all-to-all(f32[64,32,128]{2,1,0:T(8,128)S(1)} %get-tuple-element.12), channel_id=1, replica_groups=mesh['freq'=4,'strip'=64] {'strip'}, dimensions={0} | all-to-all | bytes 2097152 | tf_op jit(solution)/shard_map/all_to_all | solution.py:497
  136.9 3.2 spectral_step.5
  140.1 33.2 %all_to_all.46.chunks = f32[64,32,128]{2,1,0:T(8,128)S(1)} all-to-all(f32[64,32,128]{2,1,0:T(8,128)S(1)} %spectral_step.5), channel_id=1, replica_groups=mesh['freq'=4,'strip'=64] {'strip'}, dimensions={0} | all-to-all | bytes 2097152 | tf_op jit(solution)/shard_map/all_to_all | solution.py:497
  173.3 3.1 space_step.4
  177.0 33.3 %all_to_all.47.chunks = f32[64,32,128]{2,1,0:T(8,128)S(1)} all-to-all(f32[64,32,128]{2,1,0:T(8,128)S(1)} %get-tuple-element.14), channel_id=1, replica_groups=mesh['freq'=4,'strip'=64] {'strip'}, dimensions={0} | all-to-all | bytes 2097152 | tf_op jit(solution)/shard_map/all_to_all | solution.py:497
  210.3 3.2 spectral_step.6
  213.5 32.7 %all_to_all.48.chunks = f32[64,32,128]{2,1,0:T(8,128)S(1)} all-to-all(f32[64,32,128]{2,1,0:T(8,128)S(1)} %spectral_step.6), channel_id=1, replica_groups=mesh['freq'=4,'strip'=64] {'strip'}, dimensions={0} | all-to-all | bytes 2097152 | tf_op jit(solution)/shard_map/all_to_all | solution.py:497
  246.2 3.0 space_step.5
  249.1 32.9 %all_to_all.49.chunks = f32[64,32,128]{2,1,0:T(8,128)S(1)} all-to-all(f32[64,32,128]{2,1,0:T(8,128)S(1)} %get-tuple-element.16), channel_id=1, replica_groups=mesh['freq'=4,'strip'=64] {'strip'}, dimensions={0} | all-to-all | bytes 2097152 | tf_op jit(solution)/shard_map/all_to_all | solution.py:497
  282.1 3.2 spectral_step.7
  286.3 8.1 %all-to-all-start.7 = ((f32[64,32,128]{2,1,0:T(8,128)}), f32[64,32,128]{2,1,0:T(8,128)S(1)}, u32[]{:S(2)}, u32[]{:S(2)}) async-start(f32[64,32,128]{2,1,0:T(8,128)} %copy-done.10), calls=%async_computation.10 | async-start | bytes 2097152 | tf_op jit(solution)/shard_map/all_to_all | solution.py:497
  296.6 22.5 %all-to-all-done.7.chunks = f32[64,32,128]{2,1,0:T(8,128)S(1)} async-done(((f32[64,32,128]{2,1,0:T(8,128)}), f32[64,32,128]{2,1,0:T(8,128)S(1)}, u32[]{:S(2)}, u32[]{:S(2)}) %all-to-all-start.7) | async-done | bytes 1048608 | tf_op jit(solution)/shard_map/all_to_all | solution.py:497
  319.1 2.2 copy-done.2
  321.3 2.1 space_last.1
  323.4 15.4 %all_to_all.50 = f32[4,32,512]{2,1,0:T(8,128)S(1)} all-to-all(f32[4,32,512]{2,1,0:T(8,128)S(1)} %space_last.1), channel_id=1, replica_groups=mesh['freq'=4,'strip'=64] {'freq'}, dimensions={0} | all-to-all | bytes 524288 | tf_op jit(solution)/shard_map/all_to_all | solution.py:519
  338.9 29.9 %reduce-scatter.6.cloned.1.call-done = f32[1,32,512]{2,1,0:T(8,128)} async-done(((f32[4,32,512]{2,1,0:T(8,128)}), f32[1,32,512]{2,1,0:T(8,128)}) %reduce-scatter.6.cloned.1.call-update) | async-done | bytes 65552 | tf_op jit(solution)/shard_map/reduce_scatter | solution.py:522
  368.8 34.3 %reduce-scatter.8.cloned.1.call-done = f32[1,32,512]{2,1,0:T(8,128)} async-done(((f32[4,32,512]{2,1,0:T(8,128)}), f32[1,32,512]{2,1,0:T(8,128)}) %reduce-scatter.8.cloned.1.call-update) | async-done | bytes 65552 | tf_op jit(solution)/shard_map/reduce_scatter | solution.py:522
  403.0 1.6 pad_maximum_fusion
  (53 shorter events, 9.5 us)
Async XLA Ops:
  6.5 47.4 %copy-start.3 = (f32[16,128,128]{2,1,0:T(8,128)S(1)}, f32[16,128,128]{2,1,0:T(8,128)}, u32[]{:S(2)}) copy-start(f32[16,128,128]{2,1,0:T(8,128)} %constant.142.clone.twiddle_sin) | copy-start | bytes 3145732
  7.6 1.0 copy-start.7
  8.6 1.0 copy-start.16
  9.6 1.0 copy-start.17
  10.7 0.7 copy-start.18
  14.1 39.8 %all-to-all-start = ((f32[64,32,128]{2,1,0:T(8,128)}), f32[64,32,128]{2,1,0:T(8,128)}, u32[]{:S(2)}, u32[]{:S(2)}) async-start(f32[64,32,128]{2,1,0:T(8,128)} %encode_forward.1), calls=%async_computation | async-start | bytes 2097152 | tf_op jit(solution)/shard_map/all_to_all | solution.py:497
  53.9 1.2 copy-start.4
  55.1 0.9 copy-start.12
  56.1 0.9 copy-start.14
  57.0 39.3 %copy-start.6 = (bf16[768,256]{1,0:T(8,128)(2,1)S(1)}, bf16[768,256]{1,0:T(8,128)(2,1)}, u32[]{:S(2)}) copy-start(bf16[768,256]{1,0:T(8,128)(2,1)} %constant.137.clone.inverse_table) | copy-start | bytes 1179652
  57.0 39.3 %copy-start.19 = (f32[16,256]{1,0:T(8,128)S(1)}, f32[16,256]{1,0:T(8,128)}, u32[]{:S(2)}) copy-start(f32[16,256]{1,0:T(8,128)} %constant.140.clone.twiddle) | copy-start | bytes 49156
  61.5 0.9 copy-start.11
  62.4 33.9 %all-to-all-start.1 = ((f32[64,32,128]{2,1,0:T(8,128)}), f32[64,32,128]{2,1,0:T(8,128)}, u32[]{:S(2)}, u32[]{:S(2)}) async-start(f32[64,32,128]{2,1,0:T(8,128)} %copy-done.11), calls=%async_computation.1 | async-start | bytes 2097152 | tf_op jit(solution)/shard_map/all_to_all | solution.py:497
  96.3 2.2 copy-start
  98.5 1.0 copy-start.8
  99.5 37.4 %copy-start.5 = (f32[16,128,128]{2,1,0:T(8,128)S(1)}, f32[16,128,128]{2,1,0:T(8,128)}, u32[]{:S(2)}) copy-start(f32[16,128,128]{2,1,0:T(8,128)} %constant.141.clone.twiddle_cos) | copy-start | bytes 3145732
  99.5 37.4 %copy-start.13 = (bf16[256,384]{1,0:T(8,128)(2,1)S(1)}, bf16[256,384]{1,0:T(8,128)(2,1)}, u32[]{:S(2)}) copy-start(bf16[256,384]{1,0:T(8,128)(2,1)} %constant.139.clone.left_inverse) | copy-start | bytes 589828
  99.5 37.4 %copy-start.15 = (bf16[256,384]{1,0:T(8,128)(2,1)S(1)}, bf16[256,384]{1,0:T(8,128)(2,1)}, u32[]{:S(2)}) copy-start(bf16[256,384]{1,0:T(8,128)(2,1)} %constant.138.clone.left) | copy-start | bytes 589828
  103.9 36.2 %copy-start.20 = (f32[4,32,512]{2,1,0:T(8,128)}, f32[4,32,512]{2,1,0:T(8,128)S(1)}, u32[]{:S(2)}) copy-start(f32[4,32,512]{2,1,0:T(8,128)S(1)} %get-tuple-element.11) | copy-start | bytes 786436
  136.9 36.4 %copy-start.1 = (f32[16,32,2048]{2,1,0:T(8,128)S(1)}, f32[16,32,2048]{2,1,0:T(8,128)}, u32[]{:S(2)}) copy-start(f32[16,32,2048]{2,1,0:T(8,128)} %slow.7) | copy-start | bytes 12582916
  136.9 36.4 %copy-start.9 = (bf16[768,256]{1,0:T(8,128)(2,1)S(1)}, bf16[768,256]{1,0:T(8,128)(2,1)}, u32[]{:S(2)}) copy-start(bf16[768,256]{1,0:T(8,128)(2,1)} %constant.136.clone.table) | copy-start | bytes 1179652
  176.3 0.7 copy-start.21
  249.1 32.9 %copy-start.22 = (f32[4,32,512]{2,1,0:T(8,128)}, f32[4,32,512]{2,1,0:T(8,128)S(1)}, u32[]{:S(2)}) copy-start(f32[4,32,512]{2,1,0:T(8,128)S(1)} %get-tuple-element.15) | copy-start | bytes 786436
  285.2 1.0 copy-start.10
  286.3 32.8 %all-to-all-start.7 = ((f32[64,32,128]{2,1,0:T(8,128)}), f32[64,32,128]{2,1,0:T(8,128)S(1)}, u32[]{:S(2)}, u32[]{:S(2)}) async-start(f32[64,32,128]{2,1,0:T(8,128)} %copy-done.10), calls=%async_computation.10 | async-start | bytes 2097152 | tf_op jit(solution)/shard_map/all_to_all | solution.py:497
  294.3 44.5 %reduce-scatter.4.cloned.1.call-start = ((), (), s32[]{:S(2)}) async-start(), calls=%async_computation.12 | async-start | bytes 327680 | tf_op jit(solution)/shard_map/reduce_scatter | solution.py:522
  295.1 73.7 %reduce-scatter.6.cloned.1.call-start = ((), (), s32[]{:S(2)}) async-start(), calls=%async_computation.13 | async-start | bytes 327680 | tf_op jit(solution)/shard_map/reduce_scatter | solution.py:522
  295.8 107.2 %reduce-scatter.8.cloned.1.call-start = ((), (), s32[]{:S(2)}) async-start(), calls=%async_computation.14 | async-start | bytes 327680 | tf_op jit(solution)/shard_map/reduce_scatter | solution.py:522
  319.1 2.2 copy-start.2
Sparse Core Ops, SparseCore 0:
  297.9 34.9 reduce-scatter.3
  335.8 32.8 reduce-scatter.5
  371.5 31.5 reduce-scatter.7

commit v2 on v1

--- a/solution.py
+++ b/solution.py
@@ -7,6 +7,7 @@
 from jax import lax
 from jax.experimental import pallas as pl
 from jax.experimental.pallas import tpu as pltpu
+from jax.sharding import Mesh
 from jax.sharding import PartitionSpec as P
 
 DEPTHS = 4
@@ -16,7 +17,7 @@
 INNER = SIZE // RADIX
 HALF = 64
 ROWS = 64
-VMEM_LIMIT = 40 * 1024 * 1024
+VMEM_LIMIT = 12 * 1024 * 1024
 
 grid_step = 4.0
 depth_step = 8.0
@@ -89,10 +90,10 @@
 def row_twiddles():
     cosine, sine = twiddles()
     sign = np.where(np.arange(2 * HALF) < HALF, -1.0, 1.0)
-    return (
-        np.broadcast_to(cosine[:, :, None], (RADIX, INNER, 2 * HALF)).astype(np.float32),
-        (sine[:, :, None] * sign[None, None, :]).astype(np.float32),
-    )
+    ones = np.ones(2 * HALF)
+    return np.stack(
+        [cosine[:, :8, None] * ones, sine[:, :8, None] * sign]
+    ).astype(np.float32)
 
 
 def butterfly16(values, direction, add, sub, turn, scale_by):
@@ -251,8 +252,7 @@
 
 def rotate_and_image(wave, slow, angular, image, keep):
     half_rows = ROWS // 2
-    parts = image.shape[0]
-    width = SIZE // parts
+    width = image.shape[3]
 
     @pl.loop(0, half_rows // 8)
     def _(tile):
@@ -260,7 +260,7 @@
         second = pl.ds(half_rows + tile * 8, 8)
         for a in range(SIZE // 512):
             columns = slice(a * 512, (a + 1) * 512)
-            sine, cosine = sine_cosine(angular * (slow[0, first, columns] - 1.0))
+            sine, cosine = sine_cosine(angular * (slow[tile, :, columns] - 1.0))
             turned = []
             for rows in (first, second):
                 real, imag = wave[0, rows, columns], wave[1, rows, columns]
@@ -272,23 +272,39 @@
             picture = turned[0][0] * turned[1][0] - turned[0][1] * turned[1][1]
             place = a * 512 // width
             offset = a * 512 % width
-            image[place, first, offset : offset + 512] = picture * 0.25
-
-
-def first_kernel(turn_ref, source, recorded, table, twiddle, out, wave, work):
+            image[tile, place, :, offset : offset + 512] = picture * (1.0 / image.shape[0])
+
+
+def fetch(pairs, semaphores):
+    copies = [
+        pltpu.make_async_copy(source, target, semaphores.at[n])
+        for n, (source, target) in enumerate(pairs)
+    ]
+    for copy in copies:
+        copy.start()
+    return copies
+
+
+def first_kernel(
+    turn_ref, source, recorded, table, twiddle, early, out, wave, work, fields, tables, semaphores
+):
     half_rows = ROWS // 2
-
-    @pl.loop(0, half_rows // 16)
-    def _(tile):
-        rows = pl.ds(tile * 16, 16)
-        for kind, field in enumerate((source, recorded)):
+    copies = fetch(
+        [(source, fields.at[0]), (recorded, fields.at[1]), (table.at[0], tables)], semaphores
+    )
+    for kind in range(2):
+        copies[kind].wait()
+
+        @pl.loop(0, half_rows // 16)
+        def _(tile):
+            rows = pl.ds(tile * 16, 16)
             place = pl.ds(kind * half_rows + tile * 16, 16)
             for a in range(SIZE // 512):
                 columns = slice(a * 512, (a + 1) * 512)
                 real_sum, imag_sum = None, None
-                for shot in range(field.shape[0]):
-                    real = field[shot, 0, 0, rows, columns].astype(jnp.float32)
-                    imag = field[shot, 0, 1, rows, columns].astype(jnp.float32)
+                for shot in range(fields.shape[1]):
+                    real = fields[kind, shot, 0, 0, rows, columns].astype(jnp.float32)
+                    imag = fields[kind, shot, 0, 1, rows, columns].astype(jnp.float32)
                     cosine, sine = turn_ref[0, shot], turn_ref[1, shot]
                     real_part = cosine * real - sine * imag
                     imag_part = cosine * imag + sine * real
@@ -297,20 +313,29 @@
                 wave[0, place, columns] = real_sum
                 wave[1, place, columns] = imag_sum if kind == 0 else -imag_sum
 
-    forward_rows(wave, work, table, twiddle, out)
-
-
-def middle_kernel(
-    index_ref, angular_ref, chunks, slow, inverse_table, table, twiddle, out, image, wave, work
+    copies[2].wait()
+    forward_rows(wave, work, tables, twiddle, out)
+
+
+def space_kernel(
+    depth, last, angular, chunks, slow, table, twiddle, early, *refs
 ):
-    inverse_rows(chunks, work, inverse_table, twiddle, wave)
-    rotate_and_image(wave, slow, angular_ref[0], image, True)
-    forward_rows(wave, work, table, twiddle, out)
-
-
-def last_kernel(index_ref, angular_ref, chunks, slow, inverse_table, twiddle, image, wave, work):
-    inverse_rows(chunks, work, inverse_table, twiddle, wave)
-    rotate_and_image(wave, slow, angular_ref[0], image, False)
+    if last:
+        image, wave, work, tables, slow_here, semaphores = refs
+    else:
+        out, image, wave, work, tables, slow_here, semaphores = refs
+    copies = fetch(
+        [(table.at[1], tables.at[1]), (slow.at[:, depth], slow_here)]
+        + ([] if last else [(table.at[0], tables.at[0])]),
+        semaphores,
+    )
+    copies[0].wait()
+    inverse_rows(chunks, work, tables.at[1], twiddle, wave)
+    copies[1].wait()
+    rotate_and_image(wave, slow_here, angular[0], image, not last)
+    if not last:
+        copies[2].wait()
+        forward_rows(wave, work, tables.at[0], twiddle, out)
 
 
 WAVE = pltpu.VMEM((2, ROWS, SIZE), jnp.float32)
@@ -322,51 +347,61 @@
     return pl.BlockSpec(memory_space=pltpu.VMEM)
 
 
+def anywhere():
+    return pl.BlockSpec(memory_space=pl.ANY)
+
+
+def scalars():
+    return pl.BlockSpec(memory_space=pltpu.SMEM)
+
+
 def params():
     return pltpu.CompilerParams(vmem_limit_bytes=VMEM_LIMIT)
 
 
-def first_step(turn, source, recorded, table, twiddle):
+def first_step(turn, source, recorded, table, twiddle, early):
     return pl.pallas_call(
         first_kernel,
         out_shape=CHUNKS,
-        in_specs=[pl.BlockSpec(memory_space=pltpu.SMEM)] + [whole()] * 4,
+        in_specs=[scalars(), anywhere(), anywhere(), anywhere(), whole(), anywhere()],
         out_specs=whole(),
-        scratch_shapes=[WAVE, WORK],
+        scratch_shapes=[
+            WAVE,
+            WORK,
+            pltpu.VMEM((2,) + source.shape, source.dtype),
+            pltpu.VMEM(table.shape[1:], table.dtype),
+            pltpu.SemaphoreType.DMA((3,)),
+        ],
         compiler_params=params(),
         name="encode_forward",
-    )(turn, source, recorded, table, twiddle)
-
-
-def space_step(slice_at, angular, chunks, slowness, tables, twiddle, parts, last):
-    rows = ROWS // 2
-
-    def fixed(shape):
-        return pl.BlockSpec(shape, lambda i, *scalars: (0,) * len(shape))
-
-    image = jax.ShapeDtypeStruct((parts, rows, SIZE // parts), jnp.float32)
-    constants = [tables[1], twiddle] if last else [tables[1], tables[0], twiddle]
+    )(turn, source, recorded, table, twiddle, early)
+
+
+def space_step(angular, chunks, slow, table, twiddle, early, depth, last):
+    parts = slow.shape[0]
+    image = jax.ShapeDtypeStruct((parts, parts, ROWS // 2 // parts, SIZE // parts), jnp.float32)
     out_shape = [image] if last else [CHUNKS, image]
     return pl.pallas_call(
-        last_kernel if last else middle_kernel,
+        functools.partial(space_kernel, depth, last),
         out_shape=out_shape,
-        grid_spec=pltpu.PrefetchScalarGridSpec(
-            num_scalar_prefetch=2,
-            grid=(1,),
-            in_specs=[
-                fixed(chunks.shape),
-                pl.BlockSpec((1, rows, SIZE), lambda i, place, angle: (place[0], 0, 0)),
-            ]
-            + [fixed(c.shape) for c in constants],
-            out_specs=[fixed(o.shape) for o in out_shape],
-            scratch_shapes=[WAVE, WORK],
-        ),
+        in_specs=[scalars(), whole(), anywhere(), anywhere(), whole(), anywhere()],
+        out_specs=[whole()] * len(out_shape),
+        scratch_shapes=[
+            WAVE,
+            WORK,
+            pltpu.VMEM(table.shape, table.dtype),
+            pltpu.VMEM((slow.shape[0],) + slow.shape[2:], slow.dtype),
+            pltpu.SemaphoreType.DMA((2 if last else 3,)),
+        ],
         compiler_params=params(),
         name="space_last" if last else "space_step",
-    )(slice_at, angular, chunks, slowness, *constants)
-
-
-def spectral_kernel(chunks, left, left_inverse, twiddle_cos, twiddle_sin, prop_a, prop_b, out, work):
+    )(angular, chunks, slow, table, twiddle, early)
+
+
+def spectral_kernel(
+    slab_in, chunks, matrices, twiddle, prop_a, prop_b, early, out, work, left, semaphores
+):
+    copies = fetch([(matrices.at[0], left.at[0]), (matrices.at[1], left.at[1])], semaphores)
     sign = half_sign()
 
     def turn(value, direction):
@@ -382,24 +417,36 @@
         return a - b
 
     tile_rows = 8
-    per_chunk = chunks.shape[1]
-
-    def place(a, tile):
-        row = a * INNER + tile * tile_rows
-        return row // per_chunk, row % per_chunk
+
+    def place(slab, a, tile):
+        strip, part = a * (INNER // 32) + tile // 4, tile % 4
+        if slab:
+            return part * 16 + strip % 16, strip // 16 * 8
+        return strip, part * 8
+
+    def turn_rows(value, k, tile, direction):
+        angle = -2.0 * math.pi * k * tile * tile_rows / SIZE
+        cosine, sine = twiddle[0, k], twiddle[1, k]
+        if tile:
+            c, s = math.cos(angle), math.sin(angle)
+            cosine, sine = cosine * c - sine * (sign * s), sine * c + cosine * (sign * s)
+        swapped = swap_halves(value) * sine
+        return value * cosine - swapped * direction
 
     for tile in range(INNER // tile_rows):
         rows = slice(tile * tile_rows, (tile + 1) * tile_rows)
         values = []
         for a in range(RADIX):
-            chunk, row = place(a, tile)
+            chunk, row = place(slab_in, a, tile)
             values.append(chunks[chunk, row : row + tile_rows, :])
         values = butterfly16(values, -1.0, add, sub, turn, scale_by)
         for k, value in enumerate(values):
             if k:
-                value = value * twiddle_cos[k, rows] + swap_halves(value) * twiddle_sin[k, rows]
+                value = turn_rows(value, k, tile, -1.0)
             work[k, rows] = value
 
+    for copy in copies:
+        copy.wait()
     wide_sign = jnp.concatenate([sign, sign], axis=1)[:1]
 
     def multiply(matrix, value):
@@ -416,12 +463,12 @@
 
     for pair in range(0, RADIX, 2):
         value = jnp.concatenate([work[pair], work[pair + 1]], axis=1)
-        value = multiply(left, value)
+        value = multiply(left.at[0], value)
         shifted = []
         for k in range(2):
             part = value[:, k * INNER : (k + 1) * INNER]
             shifted.append(part * prop_a[pair + k] + swap_halves(part) * prop_b[pair + k])
-        value = multiply(left_inverse, jnp.concatenate(shifted, axis=1))
+        value = multiply(left.at[1], jnp.concatenate(shifted, axis=1))
         work[pair] = value[:, :INNER]
         work[pair + 1] = value[:, INNER:]
 
@@ -431,24 +478,28 @@
         for k in range(RADIX):
             value = work[k, rows]
             if k:
-                value = value * twiddle_cos[k, rows] - swap_halves(value) * twiddle_sin[k, rows]
+                value = turn_rows(value, k, tile, 1.0)
             values.append(value)
         values = butterfly16(values, 1.0, add, sub, turn, scale_by)
         for a, value in enumerate(values):
-            chunk, row = place(a, tile)
+            chunk, row = place(True, a, tile)
             out[chunk, row : row + tile_rows, :] = value
 
 
-def spectral_step(chunks, left_tables, row_twiddle, propagators):
+def spectral_step(chunks, matrices, twiddle, propagators, early, slab_in):
     return pl.pallas_call(
-        spectral_kernel,
-        out_shape=jax.ShapeDtypeStruct(chunks.shape, jnp.float32),
-        in_specs=[whole()] * 7,
+        functools.partial(spectral_kernel, slab_in),
+        out_shape=CHUNKS,
+        in_specs=[whole(), anywhere(), whole(), whole(), whole(), anywhere()],
         out_specs=whole(),
-        scratch_shapes=[pltpu.VMEM((RADIX, INNER, 2 * HALF), jnp.float32)],
+        scratch_shapes=[
+            pltpu.VMEM((RADIX, INNER, 2 * HALF), jnp.float32),
+            pltpu.VMEM(matrices.shape, matrices.dtype),
+            pltpu.SemaphoreType.DMA((2,)),
+        ],
         compiler_params=params(),
         name="spectral_step",
-    )(chunks, *left_tables, *row_twiddle, *propagators)
+    )(chunks, matrices, twiddle, *propagators, early)
 
 
 def wavenumber(index):
@@ -477,60 +528,67 @@
 
 
 def per_device(source_field, recorded, phase_index, slowness, slice_index):
-    freq = lax.axis_index("freq")
-    strip = lax.axis_index("strip")
-    parts = lax.axis_size("freq")
-    total_freq = source_field.shape[1] * parts
-    encode_angle = lax.dynamic_slice_in_dim(phase_index, freq, 1, 2)[0, :, 0].astype(
+    group = lax.axis_index(("xh", "c"))
+    freq = lax.axis_index("zh")
+    freqs = lax.axis_size("zh")
+    encode_angle = lax.dynamic_slice_in_dim(phase_index, group, 1, 2)[0, :, 0].astype(
         jnp.float32
     ) * (2.0 * math.pi / PHASES)
     turn = jnp.stack([jnp.cos(encode_angle), jnp.sin(encode_angle)])
-    angular = 0.5 + 1.5 * (freq.astype(jnp.float32) + 0.5) / total_freq
-
-    right = [jnp.asarray(t) for t in lane_tables()]
-    left = [jnp.asarray(t) for t in row_tables()]
+    angular = 0.5 + 1.5 * (freq.astype(jnp.float32) + 0.5) / freqs
+
+    right = jnp.asarray(np.stack(lane_tables()))
+    left = jnp.asarray(np.stack(row_tables()))
     lane_twiddle = jnp.asarray(lane_twiddles())
-    row_twiddle = [jnp.asarray(t) for t in row_twiddles()]
-    propagators = propagator_tables(angular, strip)
-
-    def exchange(chunks):
-        return lax.all_to_all(chunks, "strip", 0, 0, tiled=True)
-
-    chunks = first_step(turn, source_field, recorded, right[0], lane_twiddle)
+    row_twiddle = jnp.asarray(row_twiddles())
+    slab = ("xh", "c", "zl", "y", "xl")
+    propagators = propagator_tables(angular, lax.axis_index(slab))
     scaled = (depth_step * angular)[None]
+
+    part_rows = ROWS // 2 // freqs
+    parts = jnp.concatenate(
+        [
+            lax.dynamic_slice(
+                slowness, (slice_index[d], group * part_rows, 0), (1, part_rows, SIZE)
+            )
+            for d in range(DEPTHS)
+        ]
+    )
+    slow = lax.all_gather(parts, "zh", axis=0, tiled=False)
+
+    chunks = first_step(turn, source_field, recorded, right, lane_twiddle, parts)
+    chunks = lax.all_to_all(chunks, ("xh", "c"), 0, 0, tiled=True)
+    chunks = lax.all_to_all(chunks, ("zh", "zl", "y", "xl"), 0, 0, tiled=True)
     pictures = []
     for descent in range(DEPTHS):
-        chunks = exchange(chunks)
-        chunks = spectral_step(chunks, left, row_twiddle, propagators)
-        chunks = exchange(chunks)
         last = descent == DEPTHS - 1
+        chunks = spectral_step(
+            chunks, left, row_twiddle, propagators, slow, descent > 0
+        )
+        chunks = lax.all_to_all(chunks, slab, 0, 0, tiled=True)
         result = space_step(
-            slice_index[descent : descent + 1],
-            scaled,
-            chunks,
-            slowness,
-            right,
-            lane_twiddle,
-            parts,
-            last,
-        )
-        if last:
-            image = result[0]
-            pictures.append(jnp.sum(lax.all_to_all(image, "freq", 0, 0, tiled=True), axis=0))
-        else:
-            chunks, image = result
-            pictures.append(lax.psum_scatter(image, "freq", scatter_dimension=0, tiled=False))
-    return jnp.stack(pictures)
+            scaled, chunks, slow, right, lane_twiddle, slow, descent, last
+        )
+        pictures.append(result[-1])
+        if not last:
+            chunks = lax.all_to_all(result[0], slab, 0, 0, tiled=True)
+    picture = jnp.stack(pictures, axis=2)
+    picture = picture.reshape((freqs * freqs,) + picture.shape[2:])
+    picture = lax.all_to_all(picture, ("zh", "xh", "c"), 0, 0, tiled=True)
+    picture = jnp.sum(picture.reshape((freqs, freqs) + picture.shape[1:]), axis=0)
+    return picture.transpose(1, 0, 2, 3).reshape(DEPTHS, ROWS // 2, SIZE // freqs)
 
 
 def solution(mesh):
+    fine = Mesh(mesh.devices.reshape(2, 2, 4, 2, 4, 2), ("xh", "c", "zh", "zl", "y", "xl"))
+    freq, strip = ("xh", "c"), ("zh", "zl", "y", "xl")
     placed = (
-        P(None, "freq", None, "strip", None),
-        P(None, "freq", None, "strip", None),
+        P(None, freq, None, strip, None),
+        P(None, freq, None, strip, None),
         P(),
-        P(None, "strip", None),
+        P(None, strip, None),
         P(),
     )
     return jax.shard_map(
-        per_device, mesh=mesh, in_specs=placed, out_specs=P(None, "strip", "freq"), check_vma=False
-    )
+        per_device, mesh=fine, in_specs=placed, out_specs=P(None, strip, freq), check_vma=False
+    )

time: 412 us -> 340 us (0.83)
  waiting for transfers between devices: 137 us -> 58.5 us
  starting transfers between devices: 30.3 us -> 19.2 us
  blocking collectives: 180 us -> 188 us
  between operations: 13.4 us -> 21.2 us
  Pallas kernels: 29.2 us -> 34.9 us
    reduce_scatter x3 -> x0, waiting for transfers between devices: 64.2 us -> none  [per_device(): lax.psum_scatter(image, 'freq', scatter_dimension=0, tiled=False)]
    all_to_all x3 -> x2, waiting for transfers between devices: 70.6 us -> 17.4 us  [the longest x1 17.4 us: per_device(): chunks = lax.all_to_all(chunks, slab, 0, 0, tiled=True)]
    all_gather x0 -> x1, waiting for transfers between devices: none -> 40.5 us  [per_device(): slow = lax.all_gather(parts, 'zh', axis=0, tiled=False)]
    all_to_all x3 -> x2, starting transfers between devices: 30.1 us -> 19.2 us  [the longest x1 11.2 us: per_device(): chunks = lax.all_to_all(chunks, ('zh', 'zl', 'y', 'xl'), 0, 0, tiled=True)]
    all_to_all x6 -> x8, blocking collectives: 180 us -> 188 us  [the longest x3 66.7 us: per_device(): chunks = lax.all_to_all(result[0], slab, 0, 0, tiled=True)]
    pallas_call x9, Pallas kernels: 29.2 us -> 34.9 us  [the longest x4 21.4 us: spectral_step(): pl.pallas_call(functools.partial(spectral_kernel, slab_in), out_shape=CHU...]
    unnamed x46 -> x32, local copies, waits for them, and re-layouts: 14.9 us -> 10.5 us
  transfers between devices with their start and end apart: 6 -> 3, of which waited for: 5 -> 2; matrix products, arithmetic and copies ran while one was open for 1% -> 1% of each run, Pallas kernels for 1% -> 0%
where the time goes in v2:
time: 340 us; the launch traced here: 339 us
  blocking collectives  188 us (55%)
  waiting for transfers between devices  58.5 us (17%)
  Pallas kernels  34.9 us (10%)
  between operations  21.2 us (6%)
  starting transfers between devices  19.2 us (6%)
  local copies, waits for them, and re-layouts  13.6 us (4%)
    all_to_all x3, blocking collectives, per_device(): chunks = lax.all_to_all(result[0], slab, 0, 0, tiled=True)  66.7 us
    all_to_all x3, blocking collectives, per_device(): chunks = lax.all_to_all(chunks, slab, 0, 0, tiled=True)  66.4 us
    all_gather x1, waiting for transfers between devices, per_device(): slow = lax.all_gather(parts, 'zh', axis=0, tiled=False)  40.5 us
    all_to_all x1, blocking collectives, per_device(): picture = lax.all_to_all(picture, ('zh', 'xh', 'c'), 0, 0, tiled=True)  33.9 us
    pallas_call x4, Pallas kernels, spectral_step(): pl.pallas_call(functools.partial(spectral_kernel, slab_in), out_shape=CHU...  21.4 us
    all_to_all x1, blocking collectives, per_device(): chunks = lax.all_to_all(chunks, ('xh', 'c'), 0, 0, tiled=True)  21.3 us
    all_to_all x1, waiting for transfers between devices, per_device(): chunks = lax.all_to_all(chunks, slab, 0, 0, tiled=True)  17.4 us
    pallas_call x4, Pallas kernels, space_step(): pl.pallas_call(functools.partial(space_kernel, depth, last), out_shape=ou...  11.4 us
  transfers between devices with their start and end apart: 3, of which 2 were waited for; matrix products, arithmetic and copies ran while one was open for 1% of the time, Pallas kernels for 0%

profile of v2, /device:TPU:1, one launch (start us, length us, event | category | flops | bytes accessed | tf_op | source)
XLA Modules:
  0.0 338.9 jit_solution(13545212300366628099)
XLA Ops:
  6.5 1.5 fusion.44
  16.5 1.0 constant_dynamic-slice_fusion.3
  17.6 1.2 copy-done.2
  18.8 1.0 copy-done.12
  19.8 1.0 copy-done.13
  21.6 2.1 encode_forward.1
  23.7 21.3 %all_to_all.50 = f32[64,32,128]{2,1,0:T(8,128)} all-to-all(f32[64,32,128]{2,1,0:T(8,128)S(1)} %encode_forward.1), channel_id=1, replica_groups=mesh['xh'=2,'c'=2,'zh'=4,'zl'=2,'y'=4,'xl'=2] {'xh','c'}, dimensions={0} | all-to-all | bytes 2097152 | tf_op jit(solution)/shard_map/all_to_all | solution.py:560
  45.0 11.2 %all-to-all-start.1 = ((f32[64,32,128]{2,1,0:T(8,128)}), f32[64,32,128]{2,1,0:T(8,128)S(1)}, u32[]{:S(2)}, u32[]{:S(2)}) async-start(f32[64,32,128]{2,1,0:T(8,128)} %all_to_all.50), calls=%async_computation.1 | async-start | bytes 2097152 | tf_op jit(solution)/shard_map/all_to_all | solution.py:561
  57.0 2.0 fusion.2
  59.0 40.5 %all-gather.3.cloned.1.call-done = f32[16,8,2048]{2,1,0:T(8,128)} async-done(((f32[4,8,2048]{2,1,0:T(8,128)}), f32[16,8,2048]{2,1,0:T(8,128)}) %all-gather.3.cloned.1.call-update) | async-done | bytes 1048592 | tf_op jit(solution)/shard_map/all_gather | solution.py:557
  99.5 1.0 copy-done.6
  100.5 1.2 copy-done
  101.7 1.2 copy-done.7
  103.8 5.4 %spectral_step.4 = f32[64,32,128]{2,1,0:T(8,128)S(1)} custom-call(f32[64,32,128]{2,1,0:T(8,128)S(1)} %copy-done.7, bf16[2,256,384]{2,1,0:T(8,128)(2,1)S(1)} %copy-done.5, f32[2,16,8,128]{3,2,1,0:T(8,128)S(1)} %copy-done.10, f32[16,128,128]{2,1,0:T(8,128)S(1)} %get-tuple-element.24.prop_a, f32[16,128,128]{2,1,0:T(8,128)S(1)} %get-tuple-element.23.prop_b, ...), custom_call_target="tpu_custom_call" | custom-call | tf_op jit(solution)/shard_map/spectral_step/pallas_call | solution.py:490
  109.2 1.0 copy-done.8
  110.2 8.0 %all-to-all-start.2 = ((f32[64,32,128]{2,1,0:T(8,128)}), f32[64,32,128]{2,1,0:T(8,128)}, u32[]{:S(2)}, u32[]{:S(2)}) async-start(f32[64,32,128]{2,1,0:T(8,128)} %copy-done.8), calls=%async_computation.2 | async-start | bytes 2097152 | tf_op jit(solution)/shard_map/all_to_all | solution.py:568
  118.2 17.4 %all-to-all-done.2.chunks = f32[64,32,128]{2,1,0:T(8,128)} async-done(((f32[64,32,128]{2,1,0:T(8,128)}), f32[64,32,128]{2,1,0:T(8,128)}, u32[]{:S(2)}, u32[]{:S(2)}) %all-to-all-start.2) | async-done | bytes 1048608 | tf_op jit(solution)/shard_map/all_to_all | solution.py:568
  135.6 1.1 copy-done.3
  136.7 4.1 %space_step.3 = (f32[64,32,128]{2,1,0:T(8,128)S(1)}, f32[4,4,8,512]{3,2,1,0:T(8,128)S(1)}) custom-call(f32[1]{0:T(128)} %bitcast.angular, f32[64,32,128]{2,1,0:T(8,128)} %all-to-all-done.2.chunks, f32[4,4,8,2048]{3,2,1,0:T(8,128)S(1)} %bitcast.27, bf16[2,768,256]{2,1,0:T(8,128)(2,1)S(1)} %copy-done.3, f32[16,256]{1,0:T(8,128)S(1)} %copy-done.15, ...), custom_call_target="tpu_custom_call" | custom-call | tf_op jit(solution)/shard_map/space_step/pallas_call | solution.py:384
  140.8 22.2 %all_to_all.51.chunks = f32[64,32,128]{2,1,0:T(8,128)S(1)} all-to-all(f32[64,32,128]{2,1,0:T(8,128)S(1)} %get-tuple-element.12), channel_id=1, replica_groups=mesh['xh'=2,'c'=2,'zh'=4,'zl'=2,'y'=4,'xl'=2] {'xh','c','zl','y','xl'}, dimensions={0} | all-to-all | bytes 2097152 | tf_op jit(solution)/shard_map/all_to_all | solution.py:574
  162.9 5.4 %spectral_step.5 = f32[64,32,128]{2,1,0:T(8,128)S(1)} custom-call(f32[64,32,128]{2,1,0:T(8,128)S(1)} %all_to_all.51.chunks, bf16[2,256,384]{2,1,0:T(8,128)(2,1)S(1)} %copy-done.5, f32[2,16,8,128]{3,2,1,0:T(8,128)S(1)} %copy-done.11, f32[16,128,128]{2,1,0:T(8,128)S(1)} %get-tuple-element.24.prop_a, f32[16,128,128]{2,1,0:T(8,128)S(1)} %get-tuple-element.23.prop_b, ...), custom_call_target="tpu_custom_call" | custom-call | tf_op jit(solution)/shard_map/spectral_step/pallas_call | solution.py:490
  168.3 22.1 %all_to_all.52.chunks = f32[64,32,128]{2,1,0:T(8,128)S(1)} all-to-all(f32[64,32,128]{2,1,0:T(8,128)S(1)} %spectral_step.5), channel_id=1, replica_groups=mesh['xh'=2,'c'=2,'zh'=4,'zl'=2,'y'=4,'xl'=2] {'xh','c','zl','y','xl'}, dimensions={0} | all-to-all | bytes 2097152 | tf_op jit(solution)/shard_map/all_to_all | solution.py:568
  190.4 2.8 space_step.4
  193.2 22.1 %all_to_all.53.chunks = f32[64,32,128]{2,1,0:T(8,128)S(1)} all-to-all(f32[64,32,128]{2,1,0:T(8,128)S(1)} %get-tuple-element.14), channel_id=1, replica_groups=mesh['xh'=2,'c'=2,'zh'=4,'zl'=2,'y'=4,'xl'=2] {'xh','c','zl','y','xl'}, dimensions={0} | all-to-all | bytes 2097152 | tf_op jit(solution)/shard_map/all_to_all | solution.py:574
  215.4 5.3 %spectral_step.6 = f32[64,32,128]{2,1,0:T(8,128)S(1)} custom-call(f32[64,32,128]{2,1,0:T(8,128)S(1)} %all_to_all.53.chunks, bf16[2,256,384]{2,1,0:T(8,128)(2,1)S(1)} %copy-done.5, f32[2,16,8,128]{3,2,1,0:T(8,128)S(1)} %copy-done.11, f32[16,128,128]{2,1,0:T(8,128)S(1)} %get-tuple-element.24.prop_a, f32[16,128,128]{2,1,0:T(8,128)S(1)} %get-tuple-element.23.prop_b, ...), custom_call_target="tpu_custom_call" | custom-call | tf_op jit(solution)/shard_map/spectral_step/pallas_call | solution.py:490
  220.7 22.1 %all_to_all.54.chunks = f32[64,32,128]{2,1,0:T(8,128)S(1)} all-to-all(f32[64,32,128]{2,1,0:T(8,128)S(1)} %spectral_step.6), channel_id=1, replica_groups=mesh['xh'=2,'c'=2,'zh'=4,'zl'=2,'y'=4,'xl'=2] {'xh','c','zl','y','xl'}, dimensions={0} | all-to-all | bytes 2097152 | tf_op jit(solution)/shard_map/all_to_all | solution.py:568
  242.9 2.8 space_step.5
  245.7 22.4 %all_to_all.55.chunks = f32[64,32,128]{2,1,0:T(8,128)S(1)} all-to-all(f32[64,32,128]{2,1,0:T(8,128)S(1)} %get-tuple-element.16), channel_id=1, replica_groups=mesh['xh'=2,'c'=2,'zh'=4,'zl'=2,'y'=4,'xl'=2] {'xh','c','zl','y','xl'}, dimensions={0} | all-to-all | bytes 2097152 | tf_op jit(solution)/shard_map/all_to_all | solution.py:574
  268.1 5.3 %spectral_step.7 = f32[64,32,128]{2,1,0:T(8,128)S(1)} custom-call(f32[64,32,128]{2,1,0:T(8,128)S(1)} %all_to_all.55.chunks, bf16[2,256,384]{2,1,0:T(8,128)(2,1)S(1)} %copy-done.5, f32[2,16,8,128]{3,2,1,0:T(8,128)S(1)} %copy-done.11, f32[16,128,128]{2,1,0:T(8,128)S(1)} %get-tuple-element.24.prop_a, f32[16,128,128]{2,1,0:T(8,128)S(1)} %get-tuple-element.23.prop_b, ...), custom_call_target="tpu_custom_call" | custom-call | tf_op jit(solution)/shard_map/spectral_step/pallas_call | solution.py:490
  273.4 22.1 %all_to_all.56.chunks = f32[64,32,128]{2,1,0:T(8,128)S(1)} all-to-all(f32[64,32,128]{2,1,0:T(8,128)S(1)} %spectral_step.7), channel_id=1, replica_groups=mesh['xh'=2,'c'=2,'zh'=4,'zl'=2,'y'=4,'xl'=2] {'xh','c','zl','y','xl'}, dimensions={0} | all-to-all | bytes 2097152 | tf_op jit(solution)/shard_map/all_to_all | solution.py:568
  295.6 1.7 space_last.1
  297.4 33.9 %all_to_all.57 = f32[16,4,8,512]{3,2,1,0:T(8,128)S(1)} all-to-all(f32[16,4,8,512]{3,2,1,0:T(8,128)S(1)} %pad_maximum_fusion), channel_id=1, replica_groups=mesh['xh'=2,'c'=2,'zh'=4,'zl'=2,'y'=4,'xl'=2] {'zh','xh','c'}, dimensions={0} | all-to-all | bytes 2097152 | tf_op jit(solution)/shard_map/all_to_all | solution.py:577
  (36 shorter events, 4.3 us)
Async XLA Ops:
  17.5 38.7 %copy-start.9 = (f32[4,8,2048]{2,1,0:T(8,128)}, f32[4,8,2048]{2,1,0:T(8,128)S(1)}, u32[]{:S(2)}) copy-start(f32[4,8,2048]{2,1,0:T(8,128)S(1)} %pad_maximum_fusion.1.early) | copy-start | bytes 786436
  17.5 1.2 copy-start.2
  18.8 1.0 copy-start.12
  19.8 1.0 copy-start.13
  20.9 0.7 copy-start.14
  21.6 78.9 %copy-start.5 = (bf16[2,256,384]{2,1,0:T(8,128)(2,1)S(1)}, bf16[2,256,384]{2,1,0:T(8,128)(2,1)}, u32[]{:S(2)}) copy-start(bf16[2,256,384]{2,1,0:T(8,128)(2,1)} %constant.148.clone.matrices) | copy-start | bytes 1179652
  45.0 54.5 %all-to-all-start.1 = ((f32[64,32,128]{2,1,0:T(8,128)}), f32[64,32,128]{2,1,0:T(8,128)S(1)}, u32[]{:S(2)}, u32[]{:S(2)}) async-start(f32[64,32,128]{2,1,0:T(8,128)} %all_to_all.50), calls=%async_computation.1 | async-start | bytes 2097152 | tf_op jit(solution)/shard_map/all_to_all | solution.py:561
  56.2 43.3 %all-gather.3.cloned.1.call-start = ((), (), s32[]{:S(2)}) async-start(), calls=%async_computation.10 | async-start | bytes 1310720 | tf_op jit(solution)/shard_map/all_gather | solution.py:557
  57.0 78.5 %copy-start.15 = (f32[16,256]{1,0:T(8,128)S(1)}, f32[16,256]{1,0:T(8,128)}, u32[]{:S(2)}) copy-start(f32[16,256]{1,0:T(8,128)} %constant.149.clone.twiddle) | copy-start | bytes 49156
  99.5 1.0 copy-start.6
  100.5 1.2 copy-start
  101.7 1.2 copy-start.7
  102.9 0.9 copy-start.10
  103.8 31.7 %copy-start.1 = (f32[16,8,2048]{2,1,0:T(8,128)S(1)}, f32[16,8,2048]{2,1,0:T(8,128)}, u32[]{:S(2)}) copy-start(f32[16,8,2048]{2,1,0:T(8,128)} %all-gather.3.cloned.1.call-done) | copy-start | bytes 3145732
  109.2 1.0 copy-start.8
  110.2 25.4 %all-to-all-start.2 = ((f32[64,32,128]{2,1,0:T(8,128)}), f32[64,32,128]{2,1,0:T(8,128)}, u32[]{:S(2)}, u32[]{:S(2)}) async-start(f32[64,32,128]{2,1,0:T(8,128)} %copy-done.8), calls=%async_computation.2 | async-start | bytes 2097152 | tf_op jit(solution)/shard_map/all_to_all | solution.py:568
  135.6 1.1 copy-start.3
  136.7 26.2 %copy-start.11 = (f32[2,16,8,128]{3,2,1,0:T(8,128)S(1)}, f32[2,16,8,128]{3,2,1,0:T(8,128)}, u32[]{:S(2)}) copy-start(f32[2,16,8,128]{3,2,1,0:T(8,128)} %constant.150.clone.twiddle) | copy-start | bytes 393220
  162.9 27.5 %copy-start.4 = (bf16[2,768,256]{2,1,0:T(8,128)(2,1)S(1)}, bf16[2,768,256]{2,1,0:T(8,128)(2,1)}, u32[]{:S(2)}) copy-start(bf16[2,768,256]{2,1,0:T(8,128)(2,1)} %constant.147.clone.table) | copy-start | bytes 2359300
Sparse Core Ops, SparseCore 0:
  58.8 40.6 all-gather.2

commit v3 on v2

--- a/solution.py
+++ b/solution.py
@@ -18,6 +18,7 @@
 HALF = 64
 ROWS = 64
 VMEM_LIMIT = 12 * 1024 * 1024
+FIRST_VMEM_LIMIT = 56 * 1024 * 1024
 
 grid_step = 4.0
 depth_step = 8.0
@@ -90,9 +91,8 @@
 def row_twiddles():
     cosine, sine = twiddles()
     sign = np.where(np.arange(2 * HALF) < HALF, -1.0, 1.0)
-    ones = np.ones(2 * HALF)
     return np.stack(
-        [cosine[:, :8, None] * ones, sine[:, :8, None] * sign]
+        [cosine[:, :, None] * np.ones(2 * HALF), sine[:, :, None] * sign]
     ).astype(np.float32)
 
 
@@ -250,17 +250,19 @@
             wave[1, rows, lanes(a)] = imag
 
 
-def rotate_and_image(wave, slow, angular, image, keep):
+def rotate_and_image(wave, slow, freq, angular, image, keep):
     half_rows = ROWS // 2
+    strips, part_rows = slow.shape[:2]
     width = image.shape[3]
 
-    @pl.loop(0, half_rows // 8)
-    def _(tile):
-        first = pl.ds(tile * 8, 8)
-        second = pl.ds(half_rows + tile * 8, 8)
+    @pl.loop(0, strips)
+    def _(turn):
+        strip = lax.rem(freq + strips - turn, strips)
+        first = pl.ds(pl.multiple_of(strip * part_rows, part_rows), part_rows)
+        second = pl.ds(pl.multiple_of(half_rows + strip * part_rows, part_rows), part_rows)
         for a in range(SIZE // 512):
             columns = slice(a * 512, (a + 1) * 512)
-            sine, cosine = sine_cosine(angular * (slow[tile, :, columns] - 1.0))
+            sine, cosine = sine_cosine(angular * (slow[turn, :, columns] - 1.0))
             turned = []
             for rows in (first, second):
                 real, imag = wave[0, rows, columns], wave[1, rows, columns]
@@ -272,7 +274,7 @@
             picture = turned[0][0] * turned[1][0] - turned[0][1] * turned[1][1]
             place = a * 512 // width
             offset = a * 512 % width
-            image[tile, place, :, offset : offset + 512] = picture * (1.0 / image.shape[0])
+            image[strip, place, :, offset : offset + 512] = picture * (1.0 / strips)
 
 
 def fetch(pairs, semaphores):
@@ -286,12 +288,40 @@
 
 
 def first_kernel(
-    turn_ref, source, recorded, table, twiddle, early, out, wave, work, fields, tables, semaphores
+    phases,
+    places,
+    turns,
+    source,
+    recorded,
+    table,
+    twiddle,
+    slowness,
+    out,
+    parts,
+    wave,
+    work,
+    fields,
+    tables,
+    factors,
+    semaphores,
 ):
     half_rows = ROWS // 2
+    group = lax.axis_index("xh") * lax.axis_size("c") + lax.axis_index("c")
+    part_rows = parts.shape[1]
+    part = pl.ds(pl.multiple_of(group * part_rows, part_rows), part_rows)
     copies = fetch(
-        [(source, fields.at[0]), (recorded, fields.at[1]), (table.at[0], tables)], semaphores
-    )
+        [
+            (source, fields.at[0]),
+            (recorded, fields.at[1]),
+            (table, tables),
+            (twiddle, factors),
+        ]
+        + [(slowness.at[places[d], part], parts.at[d]) for d in range(DEPTHS)],
+        semaphores,
+    )
+    shots = fields.shape[1]
+    levels = [phases[0, shot, group] & (PHASES - 1) for shot in range(shots)]
+    angles = [(turns[0, level], turns[1, level]) for level in levels]
     for kind in range(2):
         copies[kind].wait()
 
@@ -302,10 +332,10 @@
             for a in range(SIZE // 512):
                 columns = slice(a * 512, (a + 1) * 512)
                 real_sum, imag_sum = None, None
-                for shot in range(fields.shape[1]):
+                for shot in range(shots):
                     real = fields[kind, shot, 0, 0, rows, columns].astype(jnp.float32)
                     imag = fields[kind, shot, 0, 1, rows, columns].astype(jnp.float32)
-                    cosine, sine = turn_ref[0, shot], turn_ref[1, shot]
+                    cosine, sine = angles[shot]
                     real_part = cosine * real - sine * imag
                     imag_part = cosine * imag + sine * real
                     real_sum = real_part if real_sum is None else real_sum + real_part
@@ -313,29 +343,29 @@
                 wave[0, place, columns] = real_sum
                 wave[1, place, columns] = imag_sum if kind == 0 else -imag_sum
 
-    copies[2].wait()
-    forward_rows(wave, work, tables, twiddle, out)
-
-
-def space_kernel(
-    depth, last, angular, chunks, slow, table, twiddle, early, *refs
-):
+    for copy in copies[2:4]:
+        copy.wait()
+    forward_rows(wave, work, tables, factors, out)
+    for copy in copies[4:]:
+        copy.wait()
+
+
+def space_kernel(depth, last, chunks, inverse_table, table, twiddle, *refs):
+    strips = 4
+    slow, refs = refs[:strips], refs[strips:]
     if last:
-        image, wave, work, tables, slow_here, semaphores = refs
+        image, wave, work, slow_here, semaphores = refs
     else:
-        out, image, wave, work, tables, slow_here, semaphores = refs
-    copies = fetch(
-        [(table.at[1], tables.at[1]), (slow.at[:, depth], slow_here)]
-        + ([] if last else [(table.at[0], tables.at[0])]),
-        semaphores,
-    )
-    copies[0].wait()
-    inverse_rows(chunks, work, tables.at[1], twiddle, wave)
-    copies[1].wait()
-    rotate_and_image(wave, slow_here, angular[0], image, not last)
+        out, image, wave, work, slow_here, semaphores = refs
+    copies = fetch([(slow[n].at[depth], slow_here.at[n]) for n in range(strips)], semaphores)
+    freq = lax.axis_index("zh")
+    angular = depth_step * (0.5 + 1.5 * (freq.astype(jnp.float32) + 0.5) / strips)
+    inverse_rows(chunks, work, inverse_table, twiddle, wave)
+    for copy in copies:
+        copy.wait()
+    rotate_and_image(wave, slow_here, freq, angular, image, not last)
     if not last:
-        copies[2].wait()
-        forward_rows(wave, work, tables.at[0], twiddle, out)
+        forward_rows(wave, work, table, twiddle, out)
 
 
 WAVE = pltpu.VMEM((2, ROWS, SIZE), jnp.float32)
@@ -359,49 +389,55 @@
     return pltpu.CompilerParams(vmem_limit_bytes=VMEM_LIMIT)
 
 
-def first_step(turn, source, recorded, table, twiddle, early):
+def first_step(phases, places, source, recorded, table, twiddle, slowness):
+    angle = np.arange(PHASES) * (2.0 * np.pi / PHASES)
+    turns = jnp.asarray(np.stack([np.cos(angle), np.sin(angle)]).astype(np.float32))
+    part_rows = ROWS // 2 // phases.shape[2]
     return pl.pallas_call(
         first_kernel,
-        out_shape=CHUNKS,
-        in_specs=[scalars(), anywhere(), anywhere(), anywhere(), whole(), anywhere()],
-        out_specs=whole(),
+        out_shape=[
+            CHUNKS,
+            jax.ShapeDtypeStruct((DEPTHS, part_rows, SIZE), jnp.float32),
+        ],
+        in_specs=[scalars()] * 3 + [anywhere()] * 5,
+        out_specs=[whole(), whole()],
         scratch_shapes=[
             WAVE,
             WORK,
             pltpu.VMEM((2,) + source.shape, source.dtype),
-            pltpu.VMEM(table.shape[1:], table.dtype),
-            pltpu.SemaphoreType.DMA((3,)),
+            pltpu.VMEM(table.shape, table.dtype),
+            pltpu.VMEM(twiddle.shape, twiddle.dtype),
+            pltpu.SemaphoreType.DMA((4 + DEPTHS,)),
         ],
-        compiler_params=params(),
+        compiler_params=pltpu.CompilerParams(vmem_limit_bytes=FIRST_VMEM_LIMIT),
         name="encode_forward",
-    )(turn, source, recorded, table, twiddle, early)
-
-
-def space_step(angular, chunks, slow, table, twiddle, early, depth, last):
-    parts = slow.shape[0]
-    image = jax.ShapeDtypeStruct((parts, parts, ROWS // 2 // parts, SIZE // parts), jnp.float32)
+    )(phases, places, turns, source, recorded, table, twiddle, slowness)
+
+
+def space_step(chunks, slow, tables, twiddle, depth, last):
+    parts = len(slow)
+    part = slow[0].shape[1:]
+    image = jax.ShapeDtypeStruct((parts, parts, part[0], SIZE // parts), jnp.float32)
     out_shape = [image] if last else [CHUNKS, image]
     return pl.pallas_call(
         functools.partial(space_kernel, depth, last),
         out_shape=out_shape,
-        in_specs=[scalars(), whole(), anywhere(), anywhere(), whole(), anywhere()],
+        in_specs=[whole()] * 4 + [anywhere()] * parts,
         out_specs=[whole()] * len(out_shape),
         scratch_shapes=[
             WAVE,
             WORK,
-            pltpu.VMEM(table.shape, table.dtype),
-            pltpu.VMEM((slow.shape[0],) + slow.shape[2:], slow.dtype),
-            pltpu.SemaphoreType.DMA((2 if last else 3,)),
+            pltpu.VMEM((parts,) + part, jnp.float32),
+            pltpu.SemaphoreType.DMA((parts,)),
         ],
         compiler_params=params(),
         name="space_last" if last else "space_step",
-    )(angular, chunks, slow, table, twiddle, early)
+    )(chunks, tables[1], tables[0], twiddle, *slow)
 
 
 def spectral_kernel(
-    slab_in, chunks, matrices, twiddle, prop_a, prop_b, early, out, work, left, semaphores
+    slab_in, chunks, left, left_inverse, twiddle, prop_a, prop_b, out, work
 ):
-    copies = fetch([(matrices.at[0], left.at[0]), (matrices.at[1], left.at[1])], semaphores)
     sign = half_sign()
 
     def turn(value, direction):
@@ -424,14 +460,10 @@
             return part * 16 + strip % 16, strip // 16 * 8
         return strip, part * 8
 
-    def turn_rows(value, k, tile, direction):
-        angle = -2.0 * math.pi * k * tile * tile_rows / SIZE
-        cosine, sine = twiddle[0, k], twiddle[1, k]
-        if tile:
-            c, s = math.cos(angle), math.sin(angle)
-            cosine, sine = cosine * c - sine * (sign * s), sine * c + cosine * (sign * s)
-        swapped = swap_halves(value) * sine
-        return value * cosine - swapped * direction
+    def turn_rows(value, k, rows, direction):
+        turned = swap_halves(value) * twiddle[1, k, rows]
+        value = value * twiddle[0, k, rows]
+        return value - turned if direction > 0 else value + turned
 
     for tile in range(INNER // tile_rows):
         rows = slice(tile * tile_rows, (tile + 1) * tile_rows)
@@ -442,11 +474,9 @@
         values = butterfly16(values, -1.0, add, sub, turn, scale_by)
         for k, value in enumerate(values):
             if k:
-                value = turn_rows(value, k, tile, -1.0)
+                value = turn_rows(value, k, rows, -1.0)
             work[k, rows] = value
 
-    for copy in copies:
-        copy.wait()
     wide_sign = jnp.concatenate([sign, sign], axis=1)[:1]
 
     def multiply(matrix, value):
@@ -463,12 +493,12 @@
 
     for pair in range(0, RADIX, 2):
         value = jnp.concatenate([work[pair], work[pair + 1]], axis=1)
-        value = multiply(left.at[0], value)
+        value = multiply(left, value)
         shifted = []
         for k in range(2):
             part = value[:, k * INNER : (k + 1) * INNER]
             shifted.append(part * prop_a[pair + k] + swap_halves(part) * prop_b[pair + k])
-        value = multiply(left.at[1], jnp.concatenate(shifted, axis=1))
+        value = multiply(left_inverse, jnp.concatenate(shifted, axis=1))
         work[pair] = value[:, :INNER]
         work[pair + 1] = value[:, INNER:]
 
@@ -478,7 +508,7 @@
         for k in range(RADIX):
             value = work[k, rows]
             if k:
-                value = turn_rows(value, k, tile, 1.0)
+                value = turn_rows(value, k, rows, 1.0)
             values.append(value)
         values = butterfly16(values, 1.0, add, sub, turn, scale_by)
         for a, value in enumerate(values):
@@ -486,20 +516,16 @@
             out[chunk, row : row + tile_rows, :] = value
 
 
-def spectral_step(chunks, matrices, twiddle, propagators, early, slab_in):
+def spectral_step(chunks, matrices, twiddle, propagators, slab_in):
     return pl.pallas_call(
         functools.partial(spectral_kernel, slab_in),
         out_shape=CHUNKS,
-        in_specs=[whole(), anywhere(), whole(), whole(), whole(), anywhere()],
+        in_specs=[whole()] * 6,
         out_specs=whole(),
-        scratch_shapes=[
-            pltpu.VMEM((RADIX, INNER, 2 * HALF), jnp.float32),
-            pltpu.VMEM(matrices.shape, matrices.dtype),
-            pltpu.SemaphoreType.DMA((2,)),
-        ],
+        scratch_shapes=[pltpu.VMEM((RADIX, INNER, 2 * HALF), jnp.float32)],
         compiler_params=params(),
         name="spectral_step",
-    )(chunks, matrices, twiddle, *propagators, early)
+    )(chunks, *matrices, twiddle, *propagators)
 
 
 def wavenumber(index):
@@ -528,47 +554,32 @@
 
 
 def per_device(source_field, recorded, phase_index, slowness, slice_index):
-    group = lax.axis_index(("xh", "c"))
     freq = lax.axis_index("zh")
     freqs = lax.axis_size("zh")
-    encode_angle = lax.dynamic_slice_in_dim(phase_index, group, 1, 2)[0, :, 0].astype(
-        jnp.float32
-    ) * (2.0 * math.pi / PHASES)
-    turn = jnp.stack([jnp.cos(encode_angle), jnp.sin(encode_angle)])
     angular = 0.5 + 1.5 * (freq.astype(jnp.float32) + 0.5) / freqs
-
-    right = jnp.asarray(np.stack(lane_tables()))
-    left = jnp.asarray(np.stack(row_tables()))
+    slab = ("xh", "c", "zl", "y", "xl")
+    right = [jnp.asarray(t) for t in lane_tables()]
+    left = [jnp.asarray(t) for t in row_tables()]
     lane_twiddle = jnp.asarray(lane_twiddles())
     row_twiddle = jnp.asarray(row_twiddles())
-    slab = ("xh", "c", "zl", "y", "xl")
     propagators = propagator_tables(angular, lax.axis_index(slab))
-    scaled = (depth_step * angular)[None]
-
-    part_rows = ROWS // 2 // freqs
-    parts = jnp.concatenate(
-        [
-            lax.dynamic_slice(
-                slowness, (slice_index[d], group * part_rows, 0), (1, part_rows, SIZE)
-            )
-            for d in range(DEPTHS)
-        ]
-    )
-    slow = lax.all_gather(parts, "zh", axis=0, tiled=False)
-
-    chunks = first_step(turn, source_field, recorded, right, lane_twiddle, parts)
+
+    chunks, parts = first_step(
+        phase_index, slice_index, source_field, recorded, right[0], lane_twiddle, slowness
+    )
+    slow = [parts]
+    for step in range(1, freqs):
+        ring = [(z, (z + step) % freqs) for z in range(freqs)]
+        slow.append(lax.ppermute(parts, "zh", ring))
     chunks = lax.all_to_all(chunks, ("xh", "c"), 0, 0, tiled=True)
+    chunks, slow = lax.optimization_barrier((chunks, slow))
     chunks = lax.all_to_all(chunks, ("zh", "zl", "y", "xl"), 0, 0, tiled=True)
     pictures = []
     for descent in range(DEPTHS):
         last = descent == DEPTHS - 1
-        chunks = spectral_step(
-            chunks, left, row_twiddle, propagators, slow, descent > 0
-        )
+        chunks = spectral_step(chunks, left, row_twiddle, propagators, descent > 0)
         chunks = lax.all_to_all(chunks, slab, 0, 0, tiled=True)
-        result = space_step(
-            scaled, chunks, slow, right, lane_twiddle, slow, descent, last
-        )
+        result = space_step(chunks, slow, right, lane_twiddle, descent, last)
         pictures.append(result[-1])
         if not last:
             chunks = lax.all_to_all(result[0], slab, 0, 0, tiled=True)

time: 340 us -> 303 us (0.89)
  between operations: 21.2 us -> 0.26 us
  waiting for transfers between devices: 58.5 us -> 39.5 us
  starting transfers between devices: 19.2 us -> 31.8 us
  local copies, waits for them, and re-layouts: 13.6 us -> 3.86 us
  blocking collectives: 188 us -> 196 us
  Pallas kernels: 34.9 us -> 28.2 us
    all_gather x1 -> x0, waiting for transfers between devices: 40.5 us -> none  [per_device(): slow = lax.all_gather(parts, 'zh', axis=0, tiled=False)]
    all_to_all x3 -> x4, blocking collectives: 66.4 us -> 95 us  [per_device(): chunks = lax.all_to_all(chunks, slab, 0, 0, tiled=True)]
    all_to_all x1, waiting for transfers between devices: 0.01 us -> 23 us  [per_device(): chunks = lax.all_to_all(chunks, ('zh', 'zl', 'y', 'xl'), 0, 0, tiled=True)]
    all_to_all x1 -> x0, blocking collectives: 21.3 us -> none  [per_device(): chunks = lax.all_to_all(chunks, ('xh', 'c'), 0, 0, tiled=True)]
    all_to_all x1, waiting for transfers between devices: 17.4 us -> 0.01 us  [per_device(): chunks = lax.all_to_all(chunks, ('xh', 'c'), 0, 0, tiled=True)]
    ppermute x0 -> x3, waiting for transfers between devices: none -> 16.5 us  [per_device(): slow.append(lax.ppermute(parts, 'zh', ring))]
    ppermute x0 -> x3, starting transfers between devices: none -> 7.63 us  [per_device(): slow.append(lax.ppermute(parts, 'zh', ring))]
    pallas_call x4, Pallas kernels: 21.4 us -> 14 us  [spectral_step(): pl.pallas_call(functools.partial(spectral_kernel, slab_in), out_shape=CHU...]
  transfers between devices with their start and end apart: 3 -> 5, of which waited for: 2 -> 4; matrix products, arithmetic and copies ran while one was open for 1% -> 1% of each run, Pallas kernels for 0% -> 0%
where the time goes in v3:
time: 303 us; the launch traced here: 302 us
  blocking collectives  196 us (65%)
  waiting for transfers between devices  39.5 us (13%)
  starting transfers between devices  31.8 us (10%)
  Pallas kernels  28.2 us (9%)
  local copies, waits for them, and re-layouts  3.86 us (1%)
  other arithmetic  3.07 us (1%)
    all_to_all x4, blocking collectives, per_device(): chunks = lax.all_to_all(chunks, slab, 0, 0, tiled=True)  95 us
    all_to_all x3, blocking collectives, per_device(): chunks = lax.all_to_all(result[0], slab, 0, 0, tiled=True)  66.4 us
    all_to_all x1, blocking collectives, per_device(): picture = lax.all_to_all(picture, ('zh', 'xh', 'c'), 0, 0, tiled=True)  34.2 us
    all_to_all x1, waiting for transfers between devices, per_device(): chunks = lax.all_to_all(chunks, ('zh', 'zl', 'y', 'xl'), 0, 0, tiled=True)  23 us
    all_to_all x1, starting transfers between devices, per_device(): chunks = lax.all_to_all(chunks, ('zh', 'zl', 'y', 'xl'), 0, 0, tiled=True)  16.5 us
    ppermute x3, waiting for transfers between devices, per_device(): slow.append(lax.ppermute(parts, 'zh', ring))  16.5 us
    pallas_call x4, Pallas kernels, spectral_step(): pl.pallas_call(functools.partial(spectral_kernel, slab_in), out_shape=CHU...  14 us
    pallas_call x4, Pallas kernels, space_step(): pl.pallas_call(functools.partial(space_kernel, depth, last), out_shape=ou...  10 us
  transfers between devices with their start and end apart: 5, of which 4 were waited for; matrix products, arithmetic and copies ran while one was open for 1% of the time, Pallas kernels for 0%

profile of v3, /device:TPU:1, one launch (start us, length us, event | category | flops | bytes accessed | tf_op | source)
XLA Modules:
  0.0 302.2 jit_solution(674579061096252624)
XLA Ops:
  0.0 4.1 %encode_forward.1 = (f32[64,32,128]{2,1,0:T(8,128)}, f32[4,8,2048]{2,1,0:T(8,128)}) custom-call(s32[1,2,4]{2,1,0:T(2,128)} %phases.1, s32[4]{0:T(128)} %places.1, f32[2,8]{1,0:T(2,128)} %constant.153.clone.turns, bf16[2,1,2,32,2048]{4,3,2,1,0:T(8,128)(2,1)} %source.1, bf16[2,1,2,32,2048]{4,3,2,1,0:T(8,128)(2,1)} %recorded.1, ...), custom_call_target="tpu_custom_call" | custom-call | tf_op jit(solution)/shard_map/encode_forward/pallas_call | solution.py:396
  4.1 7.6 %all-to-all-start = ((f32[64,32,128]{2,1,0:T(8,128)}), f32[64,32,128]{2,1,0:T(8,128)}, u32[]{:S(2)}, u32[]{:S(2)}) async-start(f32[64,32,128]{2,1,0:T(8,128)} %get-tuple-element.18), calls=%async_computation | async-start | bytes 2097152 | tf_op jit(solution)/shard_map/all_to_all | solution.py:574
  11.7 4.4 %collective-permute-start.2 = (f32[4,8,2048]{2,1,0:T(8,128)}, f32[4,8,2048]{2,1,0:T(8,128)S(1)}, u32[]{:S(2)}, u32[]{:S(2)}) collective-permute-start(f32[4,8,2048]{2,1,0:T(8,128)} %get-tuple-element.21.refs_0_), channel_id=1, source_target_pairs={{0,48},{16,0},{32,16},{48,32},{1,49},{17,1},{33,17},{49,33},{2,50}... | collective-permute-start | bytes 786440 | tf_op jit(solution)/shard_map/ppermute | solution.py:573
  16.1 0.9 collective-permute-start.1
  17.0 2.4 collective-permute-start
  19.4 11.7 %collective-permute-done.2.refs_3_ = f32[4,8,2048]{2,1,0:T(8,128)S(1)} collective-permute-done((f32[4,8,2048]{2,1,0:T(8,128)}, f32[4,8,2048]{2,1,0:T(8,128)S(1)}, u32[]{:S(2)}, u32[]{:S(2)}) %collective-permute-start.2) | collective-permute-done | bytes 262176 | tf_op jit(solution)/shard_map/ppermute | solution.py:573
  31.1 2.7 collective-permute-done.1.refs_2_
  33.7 2.1 collective-permute-done.refs_1_
  35.8 16.5 %all-to-all-start.1 = ((f32[64,32,128]{2,1,0:T(8,128)}), f32[64,32,128]{2,1,0:T(8,128)}, u32[]{:S(2)}, u32[]{:S(2)}) async-start(f32[64,32,128]{2,1,0:T(8,128)} %all-to-all-done), calls=%async_computation.1 | async-start | bytes 2097152 | tf_op jit(solution)/shard_map/all_to_all | solution.py:576
  52.5 2.9 fusion.2
  55.4 23.0 %all-to-all-done.1.chunks = f32[64,32,128]{2,1,0:T(8,128)} async-done(((f32[64,32,128]{2,1,0:T(8,128)}), f32[64,32,128]{2,1,0:T(8,128)}, u32[]{:S(2)}, u32[]{:S(2)}) %all-to-all-start.1) | async-done | bytes 1048608 | tf_op jit(solution)/shard_map/all_to_all | solution.py:576
  78.4 1.2 copy-done.1
  79.6 0.9 copy-done.10
  80.6 0.9 copy-done.12
  81.5 4.5 %spectral_step.4 = f32[64,32,128]{2,1,0:T(8,128)S(1)} custom-call(f32[64,32,128]{2,1,0:T(8,128)} %all-to-all-done.1.chunks, bf16[256,384]{1,0:T(8,128)(2,1)S(1)} %copy-done.12, bf16[256,384]{1,0:T(8,128)(2,1)S(1)} %copy-done.10, f32[2,16,128,128]{3,2,1,0:T(8,128)S(1)} %copy-done, f32[16,128,128]{2,1,0:T(8,128)S(1)} %copy-done.1, ...), custom_call_target="tpu_custom_call" | custom-call | tf_op jit(solution)/shard_map/spectral_step/pallas_call | solution.py:520
  86.1 28.6 %all_to_all.50.chunks = f32[64,32,128]{2,1,0:T(8,128)S(1)} all-to-all(f32[64,32,128]{2,1,0:T(8,128)S(1)} %spectral_step.4), channel_id=1, replica_groups=mesh['xh'=2,'c'=2,'zh'=4,'zl'=2,'y'=4,'xl'=2] {'xh','c','zl','y','xl'}, dimensions={0} | all-to-all | bytes 2097152 | tf_op jit(solution)/shard_map/all_to_all | solution.py:581
  114.7 2.8 space_step.3
  117.4 22.2 %all_to_all.51.chunks = f32[64,32,128]{2,1,0:T(8,128)S(1)} all-to-all(f32[64,32,128]{2,1,0:T(8,128)S(1)} %get-tuple-element.26), channel_id=1, replica_groups=mesh['xh'=2,'c'=2,'zh'=4,'zl'=2,'y'=4,'xl'=2] {'xh','c','zl','y','xl'}, dimensions={0} | all-to-all | bytes 2097152 | tf_op jit(solution)/shard_map/all_to_all | solution.py:585
  139.6 3.2 %spectral_step.5 = f32[64,32,128]{2,1,0:T(8,128)S(1)} custom-call(f32[64,32,128]{2,1,0:T(8,128)S(1)} %all_to_all.51.chunks, bf16[256,384]{1,0:T(8,128)(2,1)S(1)} %copy-done.13, bf16[256,384]{1,0:T(8,128)(2,1)S(1)} %copy-done.11, f32[2,16,128,128]{3,2,1,0:T(8,128)S(1)} %copy-done, f32[16,128,128]{2,1,0:T(8,128)S(1)} %copy-done.2, ...), custom_call_target="tpu_custom_call" | custom-call | tf_op jit(solution)/shard_map/spectral_step/pallas_call | solution.py:520
  142.8 22.1 %all_to_all.52.chunks = f32[64,32,128]{2,1,0:T(8,128)S(1)} all-to-all(f32[64,32,128]{2,1,0:T(8,128)S(1)} %spectral_step.5), channel_id=1, replica_groups=mesh['xh'=2,'c'=2,'zh'=4,'zl'=2,'y'=4,'xl'=2] {'xh','c','zl','y','xl'}, dimensions={0} | all-to-all | bytes 2097152 | tf_op jit(solution)/shard_map/all_to_all | solution.py:581
  164.9 2.7 space_step.4
  167.7 22.1 %all_to_all.53.chunks = f32[64,32,128]{2,1,0:T(8,128)S(1)} all-to-all(f32[64,32,128]{2,1,0:T(8,128)S(1)} %get-tuple-element.28), channel_id=1, replica_groups=mesh['xh'=2,'c'=2,'zh'=4,'zl'=2,'y'=4,'xl'=2] {'xh','c','zl','y','xl'}, dimensions={0} | all-to-all | bytes 2097152 | tf_op jit(solution)/shard_map/all_to_all | solution.py:585
  189.8 3.2 %spectral_step.6 = f32[64,32,128]{2,1,0:T(8,128)S(1)} custom-call(f32[64,32,128]{2,1,0:T(8,128)S(1)} %all_to_all.53.chunks, bf16[256,384]{1,0:T(8,128)(2,1)S(1)} %copy-done.13, bf16[256,384]{1,0:T(8,128)(2,1)S(1)} %copy-done.11, f32[2,16,128,128]{3,2,1,0:T(8,128)S(1)} %copy-done, f32[16,128,128]{2,1,0:T(8,128)S(1)} %copy-done.2, ...), custom_call_target="tpu_custom_call" | custom-call | tf_op jit(solution)/shard_map/spectral_step/pallas_call | solution.py:520
  193.0 22.1 %all_to_all.54.chunks = f32[64,32,128]{2,1,0:T(8,128)S(1)} all-to-all(f32[64,32,128]{2,1,0:T(8,128)S(1)} %spectral_step.6), channel_id=1, replica_groups=mesh['xh'=2,'c'=2,'zh'=4,'zl'=2,'y'=4,'xl'=2] {'xh','c','zl','y','xl'}, dimensions={0} | all-to-all | bytes 2097152 | tf_op jit(solution)/shard_map/all_to_all | solution.py:581
  215.1 2.7 space_step.5
  217.8 22.1 %all_to_all.55.chunks = f32[64,32,128]{2,1,0:T(8,128)S(1)} all-to-all(f32[64,32,128]{2,1,0:T(8,128)S(1)} %get-tuple-element.30), channel_id=1, replica_groups=mesh['xh'=2,'c'=2,'zh'=4,'zl'=2,'y'=4,'xl'=2] {'xh','c','zl','y','xl'}, dimensions={0} | all-to-all | bytes 2097152 | tf_op jit(solution)/shard_map/all_to_all | solution.py:585
  240.0 3.2 %spectral_step.7 = f32[64,32,128]{2,1,0:T(8,128)S(1)} custom-call(f32[64,32,128]{2,1,0:T(8,128)S(1)} %all_to_all.55.chunks, bf16[256,384]{1,0:T(8,128)(2,1)S(1)} %copy-done.13, bf16[256,384]{1,0:T(8,128)(2,1)S(1)} %copy-done.11, f32[2,16,128,128]{3,2,1,0:T(8,128)S(1)} %copy-done, f32[16,128,128]{2,1,0:T(8,128)S(1)} %copy-done.2, ...), custom_call_target="tpu_custom_call" | custom-call | tf_op jit(solution)/shard_map/spectral_step/pallas_call | solution.py:520
  243.2 22.1 %all_to_all.56.chunks = f32[64,32,128]{2,1,0:T(8,128)S(1)} all-to-all(f32[64,32,128]{2,1,0:T(8,128)S(1)} %spectral_step.7), channel_id=1, replica_groups=mesh['xh'=2,'c'=2,'zh'=4,'zl'=2,'y'=4,'xl'=2] {'xh','c','zl','y','xl'}, dimensions={0} | all-to-all | bytes 2097152 | tf_op jit(solution)/shard_map/all_to_all | solution.py:581
  265.3 1.8 space_last.1
  267.2 34.2 %all_to_all.57 = f32[16,4,8,512]{3,2,1,0:T(8,128)S(1)} all-to-all(f32[16,4,8,512]{3,2,1,0:T(8,128)S(1)} %pad_maximum_fusion), channel_id=1, replica_groups=mesh['xh'=2,'c'=2,'zh'=4,'zl'=2,'y'=4,'xl'=2] {'zh','xh','c'}, dimensions={0} | all-to-all | bytes 2097152 | tf_op jit(solution)/shard_map/all_to_all | solution.py:588
  301.4 0.1 reduce_sum.9
  301.5 0.7 copy_bitcast_fusion
  (32 shorter events, 0.2 us)
Async XLA Ops:
  4.1 74.3 %copy-start = (f32[2,16,128,128]{3,2,1,0:T(8,128)S(1)}, f32[2,16,128,128]{3,2,1,0:T(8,128)}, u32[]{:S(2)}) copy-start(f32[2,16,128,128]{3,2,1,0:T(8,128)} %constant.152.clone.twiddle) | copy-start | bytes 6291460
  4.1 31.7 %all-to-all-start = ((f32[64,32,128]{2,1,0:T(8,128)}), f32[64,32,128]{2,1,0:T(8,128)}, u32[]{:S(2)}, u32[]{:S(2)}) async-start(f32[64,32,128]{2,1,0:T(8,128)} %get-tuple-element.18), calls=%async_computation | async-start | bytes 2097152 | tf_op jit(solution)/shard_map/all_to_all | solution.py:574
  11.7 19.3 %collective-permute-start.2 = (f32[4,8,2048]{2,1,0:T(8,128)}, f32[4,8,2048]{2,1,0:T(8,128)S(1)}, u32[]{:S(2)}, u32[]{:S(2)}) collective-permute-start(f32[4,8,2048]{2,1,0:T(8,128)} %get-tuple-element.21.refs_0_), channel_id=1, source_target_pairs={{0,48},{16,0},{32,16},{48,32},{1,49},{17,1},{33,17},{49,33},{2,50}... | collective-permute-start | bytes 786440 | tf_op jit(solution)/shard_map/ppermute | solution.py:573
  16.1 17.6 %collective-permute-start.1 = (f32[4,8,2048]{2,1,0:T(8,128)}, f32[4,8,2048]{2,1,0:T(8,128)S(1)}, u32[]{:S(2)}, u32[]{:S(2)}) collective-permute-start(f32[4,8,2048]{2,1,0:T(8,128)} %get-tuple-element.21.refs_0_), channel_id=1, source_target_pairs={{0,32},{16,48},{32,0},{48,16},{1,33},{17,49},{33,1},{49,17},{2,34}... | collective-permute-start | bytes 786440 | tf_op jit(solution)/shard_map/ppermute | solution.py:573
  17.0 18.8 %collective-permute-start = (f32[4,8,2048]{2,1,0:T(8,128)}, f32[4,8,2048]{2,1,0:T(8,128)S(1)}, u32[]{:S(2)}, u32[]{:S(2)}) collective-permute-start(f32[4,8,2048]{2,1,0:T(8,128)} %get-tuple-element.21.refs_0_), channel_id=1, source_target_pairs={{0,16},{16,32},{32,48},{48,0},{1,17},{17,33},{33,49},{49,1},{2,18}... | collective-permute-start | bytes 786440 | tf_op jit(solution)/shard_map/ppermute | solution.py:573
  33.7 18.8 %copy-start.6 = (f32[4,8,2048]{2,1,0:T(8,128)}, f32[4,8,2048]{2,1,0:T(8,128)S(1)}, u32[]{:S(2)}) copy-start(f32[4,8,2048]{2,1,0:T(8,128)S(1)} %collective-permute-done.1.refs_2_) | copy-start | bytes 786436
  35.8 16.7 %copy-start.8 = (f32[4,8,2048]{2,1,0:T(8,128)}, f32[4,8,2048]{2,1,0:T(8,128)S(1)}, u32[]{:S(2)}) copy-start(f32[4,8,2048]{2,1,0:T(8,128)S(1)} %collective-permute-done.refs_1_) | copy-start | bytes 786436
  35.8 42.6 %all-to-all-start.1 = ((f32[64,32,128]{2,1,0:T(8,128)}), f32[64,32,128]{2,1,0:T(8,128)}, u32[]{:S(2)}, u32[]{:S(2)}) async-start(f32[64,32,128]{2,1,0:T(8,128)} %all-to-all-done), calls=%async_computation.1 | async-start | bytes 2097152 | tf_op jit(solution)/shard_map/all_to_all | solution.py:576
  78.4 1.2 copy-start.1
  79.6 0.9 copy-start.10
  80.6 0.9 copy-start.12
  81.5 33.2 %copy-start.3 = (bf16[768,256]{1,0:T(8,128)(2,1)S(1)}, bf16[768,256]{1,0:T(8,128)(2,1)}, u32[]{:S(2)}) copy-start(bf16[768,256]{1,0:T(8,128)(2,1)} %constant.147.clone.table) | copy-start | bytes 1179652
  81.5 33.2 %copy-start.4 = (bf16[768,256]{1,0:T(8,128)(2,1)S(1)}, bf16[768,256]{1,0:T(8,128)(2,1)}, u32[]{:S(2)}) copy-start(bf16[768,256]{1,0:T(8,128)(2,1)} %constant.148.clone.inverse_table) | copy-start | bytes 1179652
  81.5 33.2 %copy-start.5 = (f32[4,8,2048]{2,1,0:T(8,128)S(1)}, f32[4,8,2048]{2,1,0:T(8,128)}, u32[]{:S(2)}) copy-start(f32[4,8,2048]{2,1,0:T(8,128)} %get-tuple-element.21.refs_0_) | copy-start | bytes 786436
  81.5 33.2 %copy-start.7 = (f32[4,8,2048]{2,1,0:T(8,128)S(1)}, f32[4,8,2048]{2,1,0:T(8,128)}, u32[]{:S(2)}) copy-start(f32[4,8,2048]{2,1,0:T(8,128)} %copy-done.6) | copy-start | bytes 786436
  81.5 33.2 %copy-start.9 = (f32[4,8,2048]{2,1,0:T(8,128)S(1)}, f32[4,8,2048]{2,1,0:T(8,128)}, u32[]{:S(2)}) copy-start(f32[4,8,2048]{2,1,0:T(8,128)} %copy-done.8) | copy-start | bytes 786436
  81.5 33.2 %copy-start.14 = (f32[16,256]{1,0:T(8,128)S(1)}, f32[16,256]{1,0:T(8,128)}, u32[]{:S(2)}) copy-start(f32[16,256]{1,0:T(8,128)} %constant.151.clone.twiddle) | copy-start | bytes 49156
  86.0 53.6 %copy-start.2 = (f32[16,128,128]{2,1,0:T(8,128)S(1)}, f32[16,128,128]{2,1,0:T(8,128)}, u32[]{:S(2)}) copy-start(f32[16,128,128]{2,1,0:T(8,128)} %get-tuple-element.32.prop_a) | copy-start | bytes 3145732
  86.0 53.6 %copy-start.11 = (bf16[256,384]{1,0:T(8,128)(2,1)S(1)}, bf16[256,384]{1,0:T(8,128)(2,1)}, u32[]{:S(2)}) copy-start(bf16[256,384]{1,0:T(8,128)(2,1)} %constant.150.clone.left_inverse) | copy-start | bytes 589828
  86.1 53.6 %copy-start.13 = (bf16[256,384]{1,0:T(8,128)(2,1)S(1)}, bf16[256,384]{1,0:T(8,128)(2,1)}, u32[]{:S(2)}) copy-start(bf16[256,384]{1,0:T(8,128)(2,1)} %constant.149.clone.left) | copy-start | bytes 589828

commit v4 on v3

--- a/solution.py
+++ b/solution.py
@@ -14,6 +14,7 @@
 PHASES = 8
 SIZE = 2048
 RADIX = 16
+HALF_RADIX = RADIX // 2
 INNER = SIZE // RADIX
 HALF = 64
 ROWS = 64
@@ -73,41 +74,72 @@
     out = []
     for direction, scale in ((-1.0, 1.0), (1.0, 1.0 / SIZE)):
         cosine, sine = inner_dft(direction)
-        high, low = split_table(np.concatenate([cosine, sine], axis=0) * scale)
+        table = np.concatenate(
+            [np.concatenate([cosine, -sine], axis=1), np.concatenate([sine, cosine], axis=1)]
+        )
+        high, low = split_table(table * scale)
         out.append(np.concatenate([high, low, high], axis=1))
     return out
 
 
-def twiddles():
+def lane_twiddles():
     angle = -2.0 * np.pi * np.outer(np.arange(RADIX), np.arange(INNER)) / SIZE
-    return np.cos(angle), np.sin(angle)
-
-
-def lane_twiddles():
-    cosine, sine = twiddles()
-    return np.concatenate([cosine, sine], axis=1).astype(np.float32)
+    factors = np.concatenate([np.cos(angle), np.sin(angle)], axis=1)
+    return np.broadcast_to(factors[:, None], (RADIX, 8, 2 * INNER)).astype(np.float32)
 
 
 def row_twiddles():
-    cosine, sine = twiddles()
-    sign = np.where(np.arange(2 * HALF) < HALF, -1.0, 1.0)
-    return np.stack(
-        [cosine[:, :, None] * np.ones(2 * HALF), sine[:, :, None] * sign]
-    ).astype(np.float32)
-
-
-def butterfly16(values, direction, add, sub, turn, scale_by):
-    def four(a, b, c, d):
-        even_sum, even_diff = add(a, c), sub(a, c)
-        odd_sum, odd_diff = add(b, d), turn(sub(b, d), direction)
-        return [
-            add(even_sum, odd_sum),
-            add(even_diff, odd_diff),
-            sub(even_sum, odd_sum),
-            sub(even_diff, odd_diff),
-        ]
-
-    first = [four(*[values[4 * n + m] for n in range(4)]) for m in range(4)]
+    odd = (np.arange(2 * HALF) >= HALF).astype(np.int64)
+    order = 2 * np.arange(HALF_RADIX)[:, None, None] + odd
+    angle = -2.0 * np.pi * (order * np.arange(INNER)[None, :, None]) / SIZE
+    return np.stack([np.cos(angle), np.sin(angle)]).astype(np.float32)
+
+
+def add(a, b):
+    return (a[0] + b[0], a[1] + b[1])
+
+
+def sub(a, b):
+    return (a[0] - b[0], a[1] - b[1])
+
+
+def turn(a, s):
+    return (-a[1], a[0]) if s > 0 else (a[1], -a[0])
+
+
+def scale(a, c, s):
+    return (a[0] * c - a[1] * s, a[0] * s + a[1] * c)
+
+
+def butterfly4(a, b, c, d, direction):
+    even_sum, even_diff = add(a, c), sub(a, c)
+    odd_sum, odd_diff = add(b, d), turn(sub(b, d), direction)
+    return [
+        add(even_sum, odd_sum),
+        add(even_diff, odd_diff),
+        sub(even_sum, odd_sum),
+        sub(even_diff, odd_diff),
+    ]
+
+
+def butterfly8(values, direction):
+    even = butterfly4(*values[0::2], direction)
+    odd = butterfly4(*values[1::2], direction)
+    root = math.sqrt(0.5)
+
+    def eighth(a):
+        if direction > 0:
+            return ((a[0] - a[1]) * root, (a[0] + a[1]) * root)
+        return ((a[0] + a[1]) * root, (a[1] - a[0]) * root)
+
+    odd[1] = eighth(odd[1])
+    odd[2] = turn(odd[2], direction)
+    odd[3] = turn(eighth(odd[3]), direction)
+    return [add(e, o) for e, o in zip(even, odd)] + [sub(e, o) for e, o in zip(even, odd)]
+
+
+def butterfly16(values, direction):
+    first = [butterfly4(*values[m::4], direction) for m in range(4)]
     result = [None] * 16
     for k in range(4):
         column = []
@@ -118,36 +150,15 @@
                 value = turn(value, direction)
             elif power:
                 angle = direction * 2.0 * math.pi * power / 16
-                value = scale_by(value, math.cos(angle), math.sin(angle))
+                value = scale(value, math.cos(angle), math.sin(angle))
             column.append(value)
-        for m, value in enumerate(four(*column)):
+        for m, value in enumerate(butterfly4(*column, direction)):
             result[k + 4 * m] = value
     return result
 
 
-def pair_add(a, b):
-    return (a[0] + b[0], a[1] + b[1])
-
-
-def pair_sub(a, b):
-    return (a[0] - b[0], a[1] - b[1])
-
-
-def pair_turn(a, s):
-    return (-a[1], a[0]) if s > 0 else (a[1], -a[0])
-
-
-def pair_scale(a, c, s):
-    return (a[0] * c - a[1] * s, a[0] * s + a[1] * c)
-
-
 def swap_halves(value):
     return pltpu.roll(value, HALF, 1)
-
-
-def half_sign():
-    lane = lax.broadcasted_iota(jnp.int32, (8, 2 * HALF), 1)
-    return jnp.where(lane < HALF, -1.0, 1.0).astype(jnp.float32)
 
 
 def split_value(value):
@@ -190,11 +201,11 @@
     def _(tile):
         rows = pl.ds(tile * 8, 8)
         values = [(wave[0, rows, lanes(a)], wave[1, rows, lanes(a)]) for a in range(RADIX)]
-        values = butterfly16(values, -1.0, pair_add, pair_sub, pair_turn, pair_scale)
+        values = butterfly16(values, -1.0)
         for k, (real, imag) in enumerate(values):
             if k:
-                cosine = twiddle[k : k + 1, :INNER]
-                sine = twiddle[k : k + 1, INNER:]
+                cosine = twiddle[k, :, :INNER]
+                sine = twiddle[k, :, INNER:]
                 real, imag = real * cosine - imag * sine, real * sine + imag * cosine
             work[k, rows, :INNER] = real
             work[k, rows, INNER:] = imag
@@ -240,11 +251,11 @@
         for k in range(RADIX):
             real, imag = work[k, rows, :INNER], work[k, rows, INNER:]
             if k:
-                cosine = twiddle[k : k + 1, :INNER]
-                sine = twiddle[k : k + 1, INNER:]
+                cosine = twiddle[k, :, :INNER]
+                sine = twiddle[k, :, INNER:]
                 real, imag = real * cosine + imag * sine, imag * cosine - real * sine
             values.append((real, imag))
-        values = butterfly16(values, 1.0, pair_add, pair_sub, pair_turn, pair_scale)
+        values = butterfly16(values, 1.0)
         for a, (real, imag) in enumerate(values):
             wave[0, rows, lanes(a)] = real
             wave[1, rows, lanes(a)] = imag
@@ -350,14 +361,14 @@
         copy.wait()
 
 
-def space_kernel(depth, last, chunks, inverse_table, table, twiddle, *refs):
+def space_kernel(places, last, chunks, inverse_table, table, twiddle, *refs):
     strips = 4
     slow, refs = refs[:strips], refs[strips:]
     if last:
         image, wave, work, slow_here, semaphores = refs
     else:
         out, image, wave, work, slow_here, semaphores = refs
-    copies = fetch([(slow[n].at[depth], slow_here.at[n]) for n in range(strips)], semaphores)
+    copies = fetch([(slow[n].at[places[n]], slow_here.at[n]) for n in range(strips)], semaphores)
     freq = lax.axis_index("zh")
     angular = depth_step * (0.5 + 1.5 * (freq.astype(jnp.float32) + 0.5) / strips)
     inverse_rows(chunks, work, inverse_table, twiddle, wave)
@@ -414,13 +425,14 @@
     )(phases, places, turns, source, recorded, table, twiddle, slowness)
 
 
-def space_step(chunks, slow, tables, twiddle, depth, last):
+def space_step(chunks, slow, tables, twiddle, last):
+    slow, places = zip(*slow)
     parts = len(slow)
     part = slow[0].shape[1:]
     image = jax.ShapeDtypeStruct((parts, parts, part[0], SIZE // parts), jnp.float32)
     out_shape = [image] if last else [CHUNKS, image]
     return pl.pallas_call(
-        functools.partial(space_kernel, depth, last),
+        functools.partial(space_kernel, places, last),
         out_shape=out_shape,
         in_specs=[whole()] * 4 + [anywhere()] * parts,
         out_specs=[whole()] * len(out_shape),
@@ -436,84 +448,82 @@
 
 
 def spectral_kernel(
-    slab_in, chunks, left, left_inverse, twiddle, prop_a, prop_b, out, work
+    slab_in, chunks, left, left_inverse, twiddle, prop_real, prop_imag, out, work
 ):
-    sign = half_sign()
-
-    def turn(value, direction):
-        return swap_halves(value) * (sign if direction > 0 else -sign)
-
-    def scale_by(value, c, s):
-        return value * c + swap_halves(value) * (sign * s)
-
-    def add(a, b):
-        return a + b
-
-    def sub(a, b):
-        return a - b
-
     tile_rows = 8
-
-    def place(slab, a, tile):
-        strip, part = a * (INNER // 32) + tile // 4, tile % 4
+    tiles = INNER // tile_rows
+    low_half = lax.broadcasted_iota(jnp.int32, (tile_rows, 2 * HALF), 1) < HALF
+
+    def place(slab, tile):
+        strip, part = tile // 4, tile % 4
         if slab:
-            return part * 16 + strip % 16, strip // 16 * 8
-        return strip, part * 8
-
-    def turn_rows(value, k, rows, direction):
-        turned = swap_halves(value) * twiddle[1, k, rows]
-        value = value * twiddle[0, k, rows]
-        return value - turned if direction > 0 else value + turned
-
-    for tile in range(INNER // tile_rows):
+            return part * 16 + strip % 16, strip // 16 * tile_rows
+        return strip, part * tile_rows
+
+    def odd_factor(a):
+        angle = -2.0 * math.pi * a / RADIX
+        return (
+            jnp.where(low_half, 1.0, math.cos(angle)).astype(jnp.float32),
+            jnp.where(low_half, 0.0, math.sin(angle)).astype(jnp.float32),
+        )
+
+    factors = [odd_factor(a) for a in range(HALF_RADIX)]
+
+    for tile in range(tiles):
         rows = slice(tile * tile_rows, (tile + 1) * tile_rows)
+        imag_rows = slice(INNER + tile * tile_rows, INNER + (tile + 1) * tile_rows)
         values = []
-        for a in range(RADIX):
-            chunk, row = place(slab_in, a, tile)
-            values.append(chunks[chunk, row : row + tile_rows, :])
-        values = butterfly16(values, -1.0, add, sub, turn, scale_by)
-        for k, value in enumerate(values):
-            if k:
-                value = turn_rows(value, k, rows, -1.0)
-            work[k, rows] = value
-
-    wide_sign = jnp.concatenate([sign, sign], axis=1)[:1]
+        for a in range(HALF_RADIX):
+            pair = []
+            for half in range(2):
+                chunk, row = place(slab_in, (half * HALF_RADIX + a) * tiles + tile)
+                pair.append(chunks[chunk, row : row + tile_rows, :])
+            total, rest = pair[0] + pair[1], pair[0] - pair[1]
+            value = (
+                jnp.where(low_half, total, swap_halves(rest)),
+                jnp.where(low_half, swap_halves(total), rest),
+            )
+            values.append(scale(value, *factors[a]) if a else value)
+        for k, value in enumerate(butterfly8(values, -1.0)):
+            real, imag = scale(value, twiddle[0, k, rows], twiddle[1, k, rows])
+            work[k, rows] = real
+            work[k, imag_rows] = imag
 
     def multiply(matrix, value):
         high, low = split_value(value)
-        result = jnp.dot(
+        return jnp.dot(
             matrix[...],
             jnp.concatenate([high, high, low], axis=0),
             preferred_element_type=jnp.float32,
         )
-        swapped = jnp.concatenate(
-            [swap_halves(result[INNER:, :INNER]), swap_halves(result[INNER:, INNER:])], axis=1
-        )
-        return result[:INNER] + swapped * wide_sign
-
-    for pair in range(0, RADIX, 2):
-        value = jnp.concatenate([work[pair], work[pair + 1]], axis=1)
-        value = multiply(left, value)
-        shifted = []
-        for k in range(2):
-            part = value[:, k * INNER : (k + 1) * INNER]
-            shifted.append(part * prop_a[pair + k] + swap_halves(part) * prop_b[pair + k])
-        value = multiply(left_inverse, jnp.concatenate(shifted, axis=1))
+
+    for pair in range(0, HALF_RADIX, 2):
+        value = multiply(left, jnp.concatenate([work[pair], work[pair + 1]], axis=1))
+        factor = [
+            jnp.concatenate([table[pair], table[pair + 1]], axis=1)
+            for table in (prop_real, prop_imag)
+        ]
+        value = jnp.concatenate(scale((value[:INNER], value[INNER:]), *factor), axis=0)
+        value = multiply(left_inverse, value)
         work[pair] = value[:, :INNER]
         work[pair + 1] = value[:, INNER:]
 
-    for tile in range(INNER // tile_rows):
+    for tile in range(tiles):
         rows = slice(tile * tile_rows, (tile + 1) * tile_rows)
-        values = []
-        for k in range(RADIX):
-            value = work[k, rows]
-            if k:
-                value = turn_rows(value, k, rows, 1.0)
-            values.append(value)
-        values = butterfly16(values, 1.0, add, sub, turn, scale_by)
-        for a, value in enumerate(values):
-            chunk, row = place(True, a, tile)
-            out[chunk, row : row + tile_rows, :] = value
+        imag_rows = slice(INNER + tile * tile_rows, INNER + (tile + 1) * tile_rows)
+        values = [
+            scale((work[k, rows], work[k, imag_rows]), twiddle[0, k, rows], -twiddle[1, k, rows])
+            for k in range(HALF_RADIX)
+        ]
+        for a, value in enumerate(butterfly8(values, 1.0)):
+            if a:
+                value = scale(value, factors[a][0], -factors[a][1])
+            real, imag = value
+            total = jnp.where(low_half, real, swap_halves(imag))
+            rest = jnp.where(low_half, swap_halves(real), imag)
+            for half, result in enumerate((total + rest, total - rest)):
+                chunk, row = place(True, (half * HALF_RADIX + a) * tiles + tile)
+                out[chunk, row : row + tile_rows, :] = result
 
 
 def spectral_step(chunks, matrices, twiddle, propagators, slab_in):
@@ -522,7 +532,7 @@
         out_shape=CHUNKS,
         in_specs=[whole()] * 6,
         out_specs=whole(),
-        scratch_shapes=[pltpu.VMEM((RADIX, INNER, 2 * HALF), jnp.float32)],
+        scratch_shapes=[pltpu.VMEM((HALF_RADIX, 2 * INNER, 2 * HALF), jnp.float32)],
         compiler_params=params(),
         name="spectral_step",
     )(chunks, *matrices, twiddle, *propagators)
@@ -533,24 +543,22 @@
     return signed * (2.0 * math.pi / (SIZE * grid_step))
 
 
-def propagator_tables(angular, strip):
-    block = strip % (2 * RADIX)
-    lane = jnp.arange(2 * HALF, dtype=jnp.int32) % HALF
-    column = block // 2 + RADIX * ((block % 2) * HALF + lane)
+def propagator_tables(angular, block):
+    lane = jnp.arange(2 * HALF, dtype=jnp.int32)
+    column = block // 2 + RADIX * ((block % 2) * HALF + lane % HALF)
     wave_y = wavenumber(column)[None, None, :]
     row = (
-        jnp.arange(RADIX, dtype=jnp.int32)[:, None]
-        + RADIX * jnp.arange(INNER, dtype=jnp.int32)[None, :]
-    )
-    wave_x = wavenumber(row)[:, :, None]
+        jnp.arange(HALF_RADIX, dtype=jnp.int32)[:, None, None]
+        + HALF_RADIX * jnp.arange(INNER, dtype=jnp.int32)[None, :, None]
+    )
+    wave_x = wavenumber(2 * row + lane // HALF)
     vertical_sq = angular * angular - wave_x * wave_x - wave_y * wave_y
     vertical = jnp.sqrt(jnp.abs(vertical_sq))
     propagating = vertical_sq > 0
     sine, cosine = sine_cosine(depth_step * vertical)
     real_part = jnp.where(propagating, cosine, jnp.exp(-depth_step * vertical))
     imag_part = jnp.where(propagating, sine, 0.0)
-    sign = jnp.where(jnp.arange(2 * HALF) < HALF, -1.0, 1.0).astype(jnp.float32)
-    return real_part, imag_part * sign[None, None, :]
+    return real_part, imag_part
 
 
 def per_device(source_field, recorded, phase_index, slowness, slice_index):
@@ -562,24 +570,32 @@
     left = [jnp.asarray(t) for t in row_tables()]
     lane_twiddle = jnp.asarray(lane_twiddles())
     row_twiddle = jnp.asarray(row_twiddles())
-    propagators = propagator_tables(angular, lax.axis_index(slab))
+    propagators = propagator_tables(angular, lax.axis_index(slab) % (2 * RADIX))
 
     chunks, parts = first_step(
         phase_index, slice_index, source_field, recorded, right[0], lane_twiddle, slowness
     )
-    slow = [parts]
-    for step in range(1, freqs):
-        ring = [(z, (z + step) % freqs) for z in range(freqs)]
-        slow.append(lax.ppermute(parts, "zh", ring))
+    up = [(z, (z + 1) % freqs) for z in range(freqs)]
+    down = [(z, (z - 1) % freqs) for z in range(freqs)]
+    middle = DEPTHS // 2
+    below = lax.ppermute(parts, "zh", up)
+    above = lax.ppermute(parts, "zh", down)
     chunks = lax.all_to_all(chunks, ("xh", "c"), 0, 0, tiled=True)
-    chunks, slow = lax.optimization_barrier((chunks, slow))
+    chunks, below, above = lax.optimization_barrier((chunks, below, above))
+    far = [
+        lax.ppermute(below[:middle], "zh", up),
+        lax.ppermute(above[middle:], "zh", down),
+    ]
     chunks = lax.all_to_all(chunks, ("zh", "zl", "y", "xl"), 0, 0, tiled=True)
+    chunks, far = lax.optimization_barrier((chunks, far))
     pictures = []
     for descent in range(DEPTHS):
         last = descent == DEPTHS - 1
         chunks = spectral_step(chunks, left, row_twiddle, propagators, descent > 0)
         chunks = lax.all_to_all(chunks, slab, 0, 0, tiled=True)
-        result = space_step(chunks, slow, right, lane_twiddle, descent, last)
+        late, at = divmod(descent, middle)
+        slow = [(parts, descent), (below, descent), (far[late], at), (above, descent)]
+        result = space_step(chunks, slow, right, lane_twiddle, last)
         pictures.append(result[-1])
         if not last:
             chunks = lax.all_to_all(result[0], slab, 0, 0, tiled=True)

time: 303 us -> 287 us (0.947)
  starting transfers between devices: 31.8 us -> 26.7 us
  Pallas kernels: 28.2 us -> 24.4 us
  waiting for transfers between devices: 39.5 us -> 35.9 us
    all_to_all x1, waiting for transfers between devices: 23 us -> 0.01 us  [per_device(): chunks = lax.all_to_all(chunks, ('zh', 'zl', 'y', 'xl'), 0, 0, tiled=True)]
    ppermute x3 -> x4, waiting for transfers between devices: 16.5 us -> 35.9 us  [the longest x1 24.6 us: per_device(): lax.ppermute(above[middle:], 'zh', down)]
    all_to_all x1, starting transfers between devices: 16.5 us -> 11.4 us  [per_device(): chunks = lax.all_to_all(chunks, ('zh', 'zl', 'y', 'xl'), 0, 0, tiled=True)]
    pallas_call x4, Pallas kernels: 14 us -> 10.3 us  [spectral_step(): pl.pallas_call(functools.partial(spectral_kernel, slab_in), out_shape=CHU...]
    ppermute x3 -> x4, starting transfers between devices: 7.63 us -> 7.72 us  [the longest x1 4.38 us: per_device(): above = lax.ppermute(parts, 'zh', down)]
  transfers between devices with their start and end apart: 5 -> 6, of which waited for: 4 -> 3; matrix products, arithmetic and copies ran while one was open for 1% -> 0% of each run, Pallas kernels for 0% -> 0%
where the time goes in v4:
time: 287 us; the launch traced here: 286 us
  blocking collectives  196 us (68%)
  waiting for transfers between devices  35.9 us (13%)
  starting transfers between devices  26.7 us (9%)
  Pallas kernels  24.4 us (9%)
    all_to_all x4, blocking collectives, per_device(): chunks = lax.all_to_all(chunks, slab, 0, 0, tiled=True)  94.3 us
    all_to_all x3, blocking collectives, per_device(): chunks = lax.all_to_all(result[0], slab, 0, 0, tiled=True)  66.5 us
    all_to_all x1, blocking collectives, per_device(): picture = lax.all_to_all(picture, ('zh', 'xh', 'c'), 0, 0, tiled=True)  34.7 us
    ppermute x1, waiting for transfers between devices, per_device(): lax.ppermute(above[middle:], 'zh', down)  24.6 us
    all_to_all x1, starting transfers between devices, per_device(): chunks = lax.all_to_all(chunks, ('zh', 'zl', 'y', 'xl'), 0, 0, tiled=True)  11.4 us
    ppermute x1, waiting for transfers between devices, per_device(): above = lax.ppermute(parts, 'zh', down)  10.4 us
    pallas_call x4, Pallas kernels, spectral_step(): pl.pallas_call(functools.partial(spectral_kernel, slab_in), out_shape=CHU...  10.3 us
    pallas_call x4, Pallas kernels, space_step(): pl.pallas_call(functools.partial(space_kernel, places, last), out_shape=o...  10 us
  transfers between devices with their start and end apart: 6, of which 3 were waited for; matrix products, arithmetic and copies ran while one was open for 0% of the time, Pallas kernels for 0%

profile of v4, /device:TPU:1, one launch (start us, length us, event | category | flops | bytes accessed | tf_op | source)
XLA Modules:
  0.0 286.3 jit_solution(15808202753487840495)
XLA Ops:
  0.0 4.1 %encode_forward.1 = (f32[64,32,128]{2,1,0:T(8,128)}, f32[4,8,2048]{2,1,0:T(8,128)}) custom-call(s32[1,2,4]{2,1,0:T(2,128)} %phases.1, s32[4]{0:T(128)} %places.1, f32[2,8]{1,0:T(2,128)} %constant.163.clone.turns, bf16[2,1,2,32,2048]{4,3,2,1,0:T(8,128)(2,1)} %source.1, bf16[2,1,2,32,2048]{4,3,2,1,0:T(8,128)(2,1)} %recorded.1, ...), custom_call_target="tpu_custom_call" | custom-call | tf_op jit(solution)/shard_map/encode_forward/pallas_call | solution.py:407
  4.1 0.0 copy-start
  4.1 0.0 copy-start.2
  4.2 7.6 %all-to-all-start = ((f32[64,32,128]{2,1,0:T(8,128)}), f32[64,32,128]{2,1,0:T(8,128)}, u32[]{:S(2)}, u32[]{:S(2)}) async-start(f32[64,32,128]{2,1,0:T(8,128)} %get-tuple-element.19), calls=%async_computation | async-start | bytes 2097152 | tf_op jit(solution)/shard_map/all_to_all | solution.py:583
  11.7 4.4 %collective-permute-start.1 = (f32[4,8,2048]{2,1,0:T(8,128)}, f32[4,8,2048]{2,1,0:T(8,128)S(1)}, u32[]{:S(2)}, u32[]{:S(2)}) collective-permute-start(f32[4,8,2048]{2,1,0:T(8,128)} %get-tuple-element.20.refs_0_), channel_id=1, source_target_pairs={{0,48},{16,0},{32,16},{48,32},{1,49},{17,1},{33,17},{49,33},{2,50}... | collective-permute-start | bytes 786440 | tf_op jit(solution)/shard_map/ppermute | solution.py:582
  16.1 10.4 %collective-permute-done.1.refs_3_ = f32[4,8,2048]{2,1,0:T(8,128)S(1)} collective-permute-done((f32[4,8,2048]{2,1,0:T(8,128)}, f32[4,8,2048]{2,1,0:T(8,128)S(1)}, u32[]{:S(2)}, u32[]{:S(2)}) %collective-permute-start.1) | collective-permute-done | bytes 262176 | tf_op jit(solution)/shard_map/ppermute | solution.py:582
  26.5 0.9 collective-permute-done.refs_1_
  27.4 11.4 %all-to-all-start.1 = ((f32[64,32,128]{2,1,0:T(8,128)}), f32[64,32,128]{2,1,0:T(8,128)}, u32[]{:S(2)}, u32[]{:S(2)}) async-start(f32[64,32,128]{2,1,0:T(8,128)} %all-to-all-done), calls=%async_computation.1 | async-start | bytes 2097152 | tf_op jit(solution)/shard_map/all_to_all | solution.py:589
  39.0 3.3 %collective-permute-start.3 = (f32[2,8,2048]{2,1,0:T(8,128)S(1)}, f32[2,8,2048]{2,1,0:T(8,128)S(1)}, u32[]{:S(2)}, u32[]{:S(2)}) collective-permute-start(f32[2,8,2048]{2,1,0:T(8,128)S(1)} %slice.7), channel_id=1, source_target_pairs={{0,48},{16,0},{32,16},{48,32},{1,49},{17,1},{33,17},{49,33},{2,50}... | collective-permute-start | bytes 393224 | tf_op jit(solution)/shard_map/ppermute | solution.py:587
  42.3 1.1 fusion.10
  43.5 24.6 %collective-permute-done.3.refs_2_ = f32[2,8,2048]{2,1,0:T(8,128)S(1)} collective-permute-done((f32[2,8,2048]{2,1,0:T(8,128)S(1)}, f32[2,8,2048]{2,1,0:T(8,128)S(1)}, u32[]{:S(2)}, u32[]{:S(2)}) %collective-permute-start.3) | collective-permute-done | bytes 131104 | tf_op jit(solution)/shard_map/ppermute | solution.py:587
  68.1 0.7 copy-done.9
  68.7 0.6 copy-done.11
  69.4 3.6 %spectral_step.4 = f32[64,32,128]{2,1,0:T(8,128)S(1)} custom-call(f32[64,32,128]{2,1,0:T(8,128)} %all-to-all-done.1.chunks, bf16[256,768]{1,0:T(8,128)(2,1)S(1)} %copy-done.3, bf16[256,768]{1,0:T(8,128)(2,1)S(1)} %copy-done.2, f32[2,8,128,128]{3,2,1,0:T(8,128)S(1)} %copy-done, f32[8,128,128]{2,1,0:T(8,128)S(1)} %get-tuple-element.34.prop_real, ...), custom_call_target="tpu_custom_call" | custom-call | tf_op jit(solution)/shard_map/spectral_step/pallas_call | solution.py:530
  73.0 27.9 %all_to_all.50.chunks = f32[64,32,128]{2,1,0:T(8,128)S(1)} all-to-all(f32[64,32,128]{2,1,0:T(8,128)S(1)} %spectral_step.4), channel_id=1, replica_groups=mesh['xh'=2,'c'=2,'zh'=4,'zl'=2,'y'=4,'xl'=2] {'xh','c','zl','y','xl'}, dimensions={0} | all-to-all | bytes 2097152 | tf_op jit(solution)/shard_map/all_to_all | solution.py:595
  100.9 2.8 space_step.3
  103.7 22.1 %all_to_all.51.chunks = f32[64,32,128]{2,1,0:T(8,128)S(1)} all-to-all(f32[64,32,128]{2,1,0:T(8,128)S(1)} %get-tuple-element.27), channel_id=1, replica_groups=mesh['xh'=2,'c'=2,'zh'=4,'zl'=2,'y'=4,'xl'=2] {'xh','c','zl','y','xl'}, dimensions={0} | all-to-all | bytes 2097152 | tf_op jit(solution)/shard_map/all_to_all | solution.py:601
  125.8 2.2 spectral_step.5
  128.1 22.1 %all_to_all.52.chunks = f32[64,32,128]{2,1,0:T(8,128)S(1)} all-to-all(f32[64,32,128]{2,1,0:T(8,128)S(1)} %spectral_step.5), channel_id=1, replica_groups=mesh['xh'=2,'c'=2,'zh'=4,'zl'=2,'y'=4,'xl'=2] {'xh','c','zl','y','xl'}, dimensions={0} | all-to-all | bytes 2097152 | tf_op jit(solution)/shard_map/all_to_all | solution.py:595
  150.2 2.7 space_step.4
  153.0 22.3 %all_to_all.53.chunks = f32[64,32,128]{2,1,0:T(8,128)S(1)} all-to-all(f32[64,32,128]{2,1,0:T(8,128)S(1)} %get-tuple-element.29), channel_id=1, replica_groups=mesh['xh'=2,'c'=2,'zh'=4,'zl'=2,'y'=4,'xl'=2] {'xh','c','zl','y','xl'}, dimensions={0} | all-to-all | bytes 2097152 | tf_op jit(solution)/shard_map/all_to_all | solution.py:601
  175.2 2.2 spectral_step.6
  177.5 22.1 %all_to_all.54.chunks = f32[64,32,128]{2,1,0:T(8,128)S(1)} all-to-all(f32[64,32,128]{2,1,0:T(8,128)S(1)} %spectral_step.6), channel_id=1, replica_groups=mesh['xh'=2,'c'=2,'zh'=4,'zl'=2,'y'=4,'xl'=2] {'xh','c','zl','y','xl'}, dimensions={0} | all-to-all | bytes 2097152 | tf_op jit(solution)/shard_map/all_to_all | solution.py:595
  199.6 2.7 space_step.5
  202.4 22.1 %all_to_all.55.chunks = f32[64,32,128]{2,1,0:T(8,128)S(1)} all-to-all(f32[64,32,128]{2,1,0:T(8,128)S(1)} %get-tuple-element.32), channel_id=1, replica_groups=mesh['xh'=2,'c'=2,'zh'=4,'zl'=2,'y'=4,'xl'=2] {'xh','c','zl','y','xl'}, dimensions={0} | all-to-all | bytes 2097152 | tf_op jit(solution)/shard_map/all_to_all | solution.py:601
  224.5 2.2 spectral_step.7
  226.8 22.1 %all_to_all.56.chunks = f32[64,32,128]{2,1,0:T(8,128)S(1)} all-to-all(f32[64,32,128]{2,1,0:T(8,128)S(1)} %spectral_step.7), channel_id=1, replica_groups=mesh['xh'=2,'c'=2,'zh'=4,'zl'=2,'y'=4,'xl'=2] {'xh','c','zl','y','xl'}, dimensions={0} | all-to-all | bytes 2097152 | tf_op jit(solution)/shard_map/all_to_all | solution.py:595
  248.9 1.8 space_last.1
  250.7 0.1 pad_maximum_fusion
  250.8 34.7 %all_to_all.57 = f32[16,4,8,512]{3,2,1,0:T(8,128)S(1)} all-to-all(f32[16,4,8,512]{3,2,1,0:T(8,128)S(1)} %pad_maximum_fusion), channel_id=1, replica_groups=mesh['xh'=2,'c'=2,'zh'=4,'zl'=2,'y'=4,'xl'=2] {'zh','xh','c'}, dimensions={0} | all-to-all | bytes 2097152 | tf_op jit(solution)/shard_map/all_to_all | solution.py:604
  285.5 0.1 reduce_sum.9
  285.6 0.7 copy_bitcast_fusion
  (33 shorter events, 0.1 us)
Async XLA Ops:
  4.1 65.3 %copy-start = (f32[2,8,128,128]{3,2,1,0:T(8,128)S(1)}, f32[2,8,128,128]{3,2,1,0:T(8,128)}, u32[]{:S(2)}) copy-start(f32[2,8,128,128]{3,2,1,0:T(8,128)} %constant.162.clone.twiddle) | copy-start | bytes 3145732
  4.1 65.3 %copy-start.2 = (bf16[256,768]{1,0:T(8,128)(2,1)S(1)}, bf16[256,768]{1,0:T(8,128)(2,1)}, u32[]{:S(2)}) copy-start(bf16[256,768]{1,0:T(8,128)(2,1)} %constant.160.clone.left_inverse) | copy-start | bytes 1179652
  4.2 65.3 %copy-start.3 = (bf16[256,768]{1,0:T(8,128)(2,1)S(1)}, bf16[256,768]{1,0:T(8,128)(2,1)}, u32[]{:S(2)}) copy-start(bf16[256,768]{1,0:T(8,128)(2,1)} %constant.159.clone.left) | copy-start | bytes 1179652
  4.2 23.3 %all-to-all-start = ((f32[64,32,128]{2,1,0:T(8,128)}), f32[64,32,128]{2,1,0:T(8,128)}, u32[]{:S(2)}, u32[]{:S(2)}) async-start(f32[64,32,128]{2,1,0:T(8,128)} %get-tuple-element.19), calls=%async_computation | async-start | bytes 2097152 | tf_op jit(solution)/shard_map/all_to_all | solution.py:583
  11.7 14.8 %collective-permute-start.1 = (f32[4,8,2048]{2,1,0:T(8,128)}, f32[4,8,2048]{2,1,0:T(8,128)S(1)}, u32[]{:S(2)}, u32[]{:S(2)}) collective-permute-start(f32[4,8,2048]{2,1,0:T(8,128)} %get-tuple-element.20.refs_0_), channel_id=1, source_target_pairs={{0,48},{16,0},{32,16},{48,32},{1,49},{17,1},{33,17},{49,33},{2,50}... | collective-permute-start | bytes 786440 | tf_op jit(solution)/shard_map/ppermute | solution.py:582
  16.1 11.3 %collective-permute-start = (f32[4,8,2048]{2,1,0:T(8,128)}, f32[4,8,2048]{2,1,0:T(8,128)S(1)}, u32[]{:S(2)}, u32[]{:S(2)}) collective-permute-start(f32[4,8,2048]{2,1,0:T(8,128)} %get-tuple-element.20.refs_0_), channel_id=1, source_target_pairs={{0,16},{16,32},{32,48},{48,0},{1,17},{17,33},{33,49},{49,1},{2,18}... | collective-permute-start | bytes 786440 | tf_op jit(solution)/shard_map/ppermute | solution.py:581
  27.4 14.9 %copy-start.5 = (f32[4,8,2048]{2,1,0:T(8,128)}, f32[4,8,2048]{2,1,0:T(8,128)S(1)}, u32[]{:S(2)}) copy-start(f32[4,8,2048]{2,1,0:T(8,128)S(1)} %collective-permute-done.refs_1_) | copy-start | bytes 786436
  27.4 41.9 %all-to-all-start.1 = ((f32[64,32,128]{2,1,0:T(8,128)}), f32[64,32,128]{2,1,0:T(8,128)}, u32[]{:S(2)}, u32[]{:S(2)}) async-start(f32[64,32,128]{2,1,0:T(8,128)} %all-to-all-done), calls=%async_computation.1 | async-start | bytes 2097152 | tf_op jit(solution)/shard_map/all_to_all | solution.py:589
  39.0 61.9 %copy-start.1 = (bf16[768,256]{1,0:T(8,128)(2,1)S(1)}, bf16[768,256]{1,0:T(8,128)(2,1)}, u32[]{:S(2)}) copy-start(bf16[768,256]{1,0:T(8,128)(2,1)} %constant.157.clone.table) | copy-start | bytes 1179652
  39.0 29.1 %collective-permute-start.3 = (f32[2,8,2048]{2,1,0:T(8,128)S(1)}, f32[2,8,2048]{2,1,0:T(8,128)S(1)}, u32[]{:S(2)}, u32[]{:S(2)}) collective-permute-start(f32[2,8,2048]{2,1,0:T(8,128)S(1)} %slice.7), channel_id=1, source_target_pairs={{0,48},{16,0},{32,16},{48,32},{1,49},{17,1},{33,17},{49,33},{2,50}... | collective-permute-start | bytes 393224 | tf_op jit(solution)/shard_map/ppermute | solution.py:587
  42.3 26.4 %collective-permute-start.2 = (f32[2,8,2048]{2,1,0:T(8,128)S(1)}, f32[2,8,2048]{2,1,0:T(8,128)S(1)}, u32[]{:S(2)}, u32[]{:S(2)}) collective-permute-start(f32[2,8,2048]{2,1,0:T(8,128)S(1)} %slice.6), channel_id=1, source_target_pairs={{0,16},{16,32},{32,48},{48,0},{1,17},{17,33},{33,49},{49,1},{2,18}... | collective-permute-start | bytes 393224 | tf_op jit(solution)/shard_map/ppermute | solution.py:586
  68.1 0.7 copy-start.9
  68.7 0.6 copy-start.11
  69.4 31.5 %copy-start.4 = (bf16[768,256]{1,0:T(8,128)(2,1)S(1)}, bf16[768,256]{1,0:T(8,128)(2,1)}, u32[]{:S(2)}) copy-start(bf16[768,256]{1,0:T(8,128)(2,1)} %constant.158.clone.inverse_table) | copy-start | bytes 1179652
  69.4 31.5 %copy-start.6 = (f32[4,8,2048]{2,1,0:T(8,128)S(1)}, f32[4,8,2048]{2,1,0:T(8,128)}, u32[]{:S(2)}) copy-start(f32[4,8,2048]{2,1,0:T(8,128)} %copy-done.5) | copy-start | bytes 786436
  69.4 31.5 %copy-start.7 = (f32[4,8,2048]{2,1,0:T(8,128)S(1)}, f32[4,8,2048]{2,1,0:T(8,128)}, u32[]{:S(2)}) copy-start(f32[4,8,2048]{2,1,0:T(8,128)} %get-tuple-element.20.refs_0_) | copy-start | bytes 786436
  69.4 31.5 %copy-start.8 = (f32[16,8,256]{2,1,0:T(8,128)S(1)}, f32[16,8,256]{2,1,0:T(8,128)}, u32[]{:S(2)}) copy-start(f32[16,8,256]{2,1,0:T(8,128)} %constant.161.clone.twiddle) | copy-start | bytes 393220
  69.4 31.5 %copy-start.12 = (f32[2,8,2048]{2,1,0:T(8,128)S(1)}, f32[2,8,2048]{2,1,0:T(8,128)}, u32[]{:S(2)}) copy-start(f32[2,8,2048]{2,1,0:T(8,128)} %copy-done.11) | copy-start | bytes 393220
  153.0 46.7 %copy-start.10 = (f32[2,8,2048]{2,1,0:T(8,128)S(1)}, f32[2,8,2048]{2,1,0:T(8,128)}, u32[]{:S(2)}) copy-start(f32[2,8,2048]{2,1,0:T(8,128)} %copy-done.9) | copy-start | bytes 393220

commit v5 on v4

--- a/solution.py
+++ b/solution.py
@@ -197,9 +197,8 @@
 
 
 def forward_rows(wave, work, table, twiddle, out):
-    @pl.loop(0, ROWS // 8)
-    def _(tile):
-        rows = pl.ds(tile * 8, 8)
+    for tile in range(ROWS // 8):
+        rows = slice(tile * 8, tile * 8 + 8)
         values = [(wave[0, rows, lanes(a)], wave[1, rows, lanes(a)]) for a in range(RADIX)]
         values = butterfly16(values, -1.0)
         for k, (real, imag) in enumerate(values):
@@ -244,9 +243,8 @@
         )
         work[group : group + 4] = result.reshape(4, ROWS, 2 * INNER)
 
-    @pl.loop(0, ROWS // 8)
-    def _(tile):
-        rows = pl.ds(tile * 8, 8)
+    for tile in range(ROWS // 8):
+        rows = slice(tile * 8, tile * 8 + 8)
         values = []
         for k in range(RADIX):
             real, imag = work[k, rows, :INNER], work[k, rows, INNER:]
@@ -261,19 +259,18 @@
             wave[1, rows, lanes(a)] = imag
 
 
-def rotate_and_image(wave, slow, freq, angular, image, keep):
+def rotate_and_image(wave, slow, places, freq, angular, image, keep):
     half_rows = ROWS // 2
-    strips, part_rows = slow.shape[:2]
+    strips, part_rows = image.shape[0], image.shape[2]
     width = image.shape[3]
 
-    @pl.loop(0, strips)
-    def _(turn):
+    for turn in range(strips):
         strip = lax.rem(freq + strips - turn, strips)
         first = pl.ds(pl.multiple_of(strip * part_rows, part_rows), part_rows)
         second = pl.ds(pl.multiple_of(half_rows + strip * part_rows, part_rows), part_rows)
         for a in range(SIZE // 512):
             columns = slice(a * 512, (a + 1) * 512)
-            sine, cosine = sine_cosine(angular * (slow[turn, :, columns] - 1.0))
+            sine, cosine = sine_cosine(angular * (slow[turn][places[turn], :, columns] - 1.0))
             turned = []
             for rows in (first, second):
                 real, imag = wave[0, rows, columns], wave[1, rows, columns]
@@ -336,10 +333,9 @@
     for kind in range(2):
         copies[kind].wait()
 
-        @pl.loop(0, half_rows // 16)
-        def _(tile):
-            rows = pl.ds(tile * 16, 16)
-            place = pl.ds(kind * half_rows + tile * 16, 16)
+        for tile in range(half_rows // 16):
+            rows = slice(tile * 16, tile * 16 + 16)
+            place = slice(kind * half_rows + tile * 16, kind * half_rows + tile * 16 + 16)
             for a in range(SIZE // 512):
                 columns = slice(a * 512, (a + 1) * 512)
                 real_sum, imag_sum = None, None
@@ -362,19 +358,16 @@
 
 
 def space_kernel(places, last, chunks, inverse_table, table, twiddle, *refs):
-    strips = 4
+    strips = len(places)
     slow, refs = refs[:strips], refs[strips:]
     if last:
-        image, wave, work, slow_here, semaphores = refs
+        image, wave, work = refs
     else:
-        out, image, wave, work, slow_here, semaphores = refs
-    copies = fetch([(slow[n].at[places[n]], slow_here.at[n]) for n in range(strips)], semaphores)
+        out, image, wave, work = refs
     freq = lax.axis_index("zh")
     angular = depth_step * (0.5 + 1.5 * (freq.astype(jnp.float32) + 0.5) / strips)
     inverse_rows(chunks, work, inverse_table, twiddle, wave)
-    for copy in copies:
-        copy.wait()
-    rotate_and_image(wave, slow_here, freq, angular, image, not last)
+    rotate_and_image(wave, slow, places, freq, angular, image, not last)
     if not last:
         forward_rows(wave, work, table, twiddle, out)
 
@@ -434,13 +427,11 @@
     return pl.pallas_call(
         functools.partial(space_kernel, places, last),
         out_shape=out_shape,
-        in_specs=[whole()] * 4 + [anywhere()] * parts,
+        in_specs=[whole()] * (4 + parts),
         out_specs=[whole()] * len(out_shape),
         scratch_shapes=[
             WAVE,
             WORK,
-            pltpu.VMEM((parts,) + part, jnp.float32),
-            pltpu.SemaphoreType.DMA((parts,)),
         ],
         compiler_params=params(),
         name="space_last" if last else "space_step",

time: 287 us -> 284 us (0.990)
  no operation moved by 1% of the time
where the time goes in v5:
time: 284 us
  blocking collectives  196 us (69%)
  waiting for transfers between devices  35.9 us (13%)
  starting transfers between devices  26.7 us (9%)
  Pallas kernels  21.7 us (8%)
    all_to_all x4, blocking collectives, per_device(): chunks = lax.all_to_all(chunks, slab, 0, 0, tiled=True)  94.3 us
    all_to_all x3, blocking collectives, per_device(): chunks = lax.all_to_all(result[0], slab, 0, 0, tiled=True)  66.9 us
    all_to_all x1, blocking collectives, per_device(): picture = lax.all_to_all(picture, ('zh', 'xh', 'c'), 0, 0, tiled=True)  34.7 us
    ppermute x1, waiting for transfers between devices, per_device(): lax.ppermute(above[middle:], 'zh', down)  24.6 us
    all_to_all x1, starting transfers between devices, per_device(): chunks = lax.all_to_all(chunks, ('zh', 'zl', 'y', 'xl'), 0, 0, tiled=True)  11.4 us
    ppermute x1, waiting for transfers between devices, per_device(): above = lax.ppermute(parts, 'zh', down)  10.4 us
    pallas_call x4, Pallas kernels, spectral_step(): pl.pallas_call(functools.partial(spectral_kernel, slab_in), out_shape=CHU...  10.3 us
    all_to_all x1, starting transfers between devices, per_device(): chunks = lax.all_to_all(chunks, ('xh', 'c'), 0, 0, tiled=True)  7.58 us
  transfers between devices with their start and end apart: 6, of which 3 were waited for; matrix products, arithmetic and copies ran while one was open for 0% of the time, Pallas kernels for 0%

profile of v5, /device:TPU:1, one launch (start us, length us, event | category | flops | bytes accessed | tf_op | source)
XLA Modules:
  0.0 283.8 jit_solution(3246863423568172106)
XLA Ops:
  0.0 4.0 %encode_forward.1 = (f32[64,32,128]{2,1,0:T(8,128)}, f32[4,8,2048]{2,1,0:T(8,128)}) custom-call(s32[1,2,4]{2,1,0:T(2,128)} %phases.1, s32[4]{0:T(128)} %places.1, f32[2,8]{1,0:T(2,128)} %constant.163.clone.turns, bf16[2,1,2,32,2048]{4,3,2,1,0:T(8,128)(2,1)} %source.1, bf16[2,1,2,32,2048]{4,3,2,1,0:T(8,128)(2,1)} %recorded.1, ...), custom_call_target="tpu_custom_call" | custom-call | tf_op jit(solution)/shard_map/encode_forward/pallas_call | solution.py:400
  4.0 0.0 copy-start
  4.0 0.0 copy-start.2
  4.0 7.6 %all-to-all-start = ((f32[64,32,128]{2,1,0:T(8,128)}), f32[64,32,128]{2,1,0:T(8,128)}, u32[]{:S(2)}, u32[]{:S(2)}) async-start(f32[64,32,128]{2,1,0:T(8,128)} %get-tuple-element.19), calls=%async_computation | async-start | bytes 2097152 | tf_op jit(solution)/shard_map/all_to_all | solution.py:574
  11.6 4.4 %collective-permute-start.1 = (f32[4,8,2048]{2,1,0:T(8,128)}, f32[4,8,2048]{2,1,0:T(8,128)S(1)}, u32[]{:S(2)}, u32[]{:S(2)}) collective-permute-start(f32[4,8,2048]{2,1,0:T(8,128)} %get-tuple-element.20.refs_0_), channel_id=1, source_target_pairs={{0,48},{16,0},{32,16},{48,32},{1,49},{17,1},{33,17},{49,33},{2,50}... | collective-permute-start | bytes 786440 | tf_op jit(solution)/shard_map/ppermute | solution.py:573
  16.0 10.4 %collective-permute-done.1.refs_3_ = f32[4,8,2048]{2,1,0:T(8,128)S(1)} collective-permute-done((f32[4,8,2048]{2,1,0:T(8,128)}, f32[4,8,2048]{2,1,0:T(8,128)S(1)}, u32[]{:S(2)}, u32[]{:S(2)}) %collective-permute-start.1) | collective-permute-done | bytes 262176 | tf_op jit(solution)/shard_map/ppermute | solution.py:573
  26.4 0.9 collective-permute-done.refs_1_
  27.3 11.4 %all-to-all-start.1 = ((f32[64,32,128]{2,1,0:T(8,128)}), f32[64,32,128]{2,1,0:T(8,128)}, u32[]{:S(2)}, u32[]{:S(2)}) async-start(f32[64,32,128]{2,1,0:T(8,128)} %all-to-all-done), calls=%async_computation.1 | async-start | bytes 2097152 | tf_op jit(solution)/shard_map/all_to_all | solution.py:580
  38.9 3.3 %collective-permute-start.3 = (f32[2,8,2048]{2,1,0:T(8,128)S(1)}, f32[2,8,2048]{2,1,0:T(8,128)S(1)}, u32[]{:S(2)}, u32[]{:S(2)}) collective-permute-start(f32[2,8,2048]{2,1,0:T(8,128)S(1)} %slice.7), channel_id=1, source_target_pairs={{0,48},{16,0},{32,16},{48,32},{1,49},{17,1},{33,17},{49,33},{2,50}... | collective-permute-start | bytes 393224 | tf_op jit(solution)/shard_map/ppermute | solution.py:578
  42.2 1.1 fusion.10
  43.4 24.6 %collective-permute-done.3.refs_2_ = f32[2,8,2048]{2,1,0:T(8,128)S(1)} collective-permute-done((f32[2,8,2048]{2,1,0:T(8,128)S(1)}, f32[2,8,2048]{2,1,0:T(8,128)S(1)}, u32[]{:S(2)}, u32[]{:S(2)}) %collective-permute-start.3) | collective-permute-done | bytes 131104 | tf_op jit(solution)/shard_map/ppermute | solution.py:578
  67.9 0.7 copy-done.9
  68.6 0.6 copy-done.11
  69.3 3.6 %spectral_step.4 = f32[64,32,128]{2,1,0:T(8,128)S(1)} custom-call(f32[64,32,128]{2,1,0:T(8,128)} %all-to-all-done.1.chunks, bf16[256,768]{1,0:T(8,128)(2,1)S(1)} %copy-done.3, bf16[256,768]{1,0:T(8,128)(2,1)S(1)} %copy-done.2, f32[2,8,128,128]{3,2,1,0:T(8,128)S(1)} %copy-done, f32[8,128,128]{2,1,0:T(8,128)S(1)} %get-tuple-element.34.prop_real, ...), custom_call_target="tpu_custom_call" | custom-call | tf_op jit(solution)/shard_map/spectral_step/pallas_call | solution.py:521
  72.9 27.9 %all_to_all.50.chunks = f32[64,32,128]{2,1,0:T(8,128)S(1)} all-to-all(f32[64,32,128]{2,1,0:T(8,128)S(1)} %spectral_step.4), channel_id=1, replica_groups=mesh['xh'=2,'c'=2,'zh'=4,'zl'=2,'y'=4,'xl'=2] {'xh','c','zl','y','xl'}, dimensions={0} | all-to-all | bytes 2097152 | tf_op jit(solution)/shard_map/all_to_all | solution.py:586
  100.8 2.0 space_step.3
  102.9 22.3 %all_to_all.51.chunks = f32[64,32,128]{2,1,0:T(8,128)S(1)} all-to-all(f32[64,32,128]{2,1,0:T(8,128)S(1)} %get-tuple-element.27), channel_id=1, replica_groups=mesh['xh'=2,'c'=2,'zh'=4,'zl'=2,'y'=4,'xl'=2] {'xh','c','zl','y','xl'}, dimensions={0} | all-to-all | bytes 2097152 | tf_op jit(solution)/shard_map/all_to_all | solution.py:592
  125.2 2.2 spectral_step.5
  127.4 22.1 %all_to_all.52.chunks = f32[64,32,128]{2,1,0:T(8,128)S(1)} all-to-all(f32[64,32,128]{2,1,0:T(8,128)S(1)} %spectral_step.5), channel_id=1, replica_groups=mesh['xh'=2,'c'=2,'zh'=4,'zl'=2,'y'=4,'xl'=2] {'xh','c','zl','y','xl'}, dimensions={0} | all-to-all | bytes 2097152 | tf_op jit(solution)/shard_map/all_to_all | solution.py:586
  149.6 2.0 space_step.4
  151.6 22.3 %all_to_all.53.chunks = f32[64,32,128]{2,1,0:T(8,128)S(1)} all-to-all(f32[64,32,128]{2,1,0:T(8,128)S(1)} %get-tuple-element.29), channel_id=1, replica_groups=mesh['xh'=2,'c'=2,'zh'=4,'zl'=2,'y'=4,'xl'=2] {'xh','c','zl','y','xl'}, dimensions={0} | all-to-all | bytes 2097152 | tf_op jit(solution)/shard_map/all_to_all | solution.py:592
  173.9 2.2 spectral_step.6
  176.1 22.1 %all_to_all.54.chunks = f32[64,32,128]{2,1,0:T(8,128)S(1)} all-to-all(f32[64,32,128]{2,1,0:T(8,128)S(1)} %spectral_step.6), channel_id=1, replica_groups=mesh['xh'=2,'c'=2,'zh'=4,'zl'=2,'y'=4,'xl'=2] {'xh','c','zl','y','xl'}, dimensions={0} | all-to-all | bytes 2097152 | tf_op jit(solution)/shard_map/all_to_all | solution.py:586
  198.3 2.0 space_step.5
  200.3 22.3 %all_to_all.55.chunks = f32[64,32,128]{2,1,0:T(8,128)S(1)} all-to-all(f32[64,32,128]{2,1,0:T(8,128)S(1)} %get-tuple-element.32), channel_id=1, replica_groups=mesh['xh'=2,'c'=2,'zh'=4,'zl'=2,'y'=4,'xl'=2] {'xh','c','zl','y','xl'}, dimensions={0} | all-to-all | bytes 2097152 | tf_op jit(solution)/shard_map/all_to_all | solution.py:592
  222.6 2.2 spectral_step.7
  224.9 22.1 %all_to_all.56.chunks = f32[64,32,128]{2,1,0:T(8,128)S(1)} all-to-all(f32[64,32,128]{2,1,0:T(8,128)S(1)} %spectral_step.7), channel_id=1, replica_groups=mesh['xh'=2,'c'=2,'zh'=4,'zl'=2,'y'=4,'xl'=2] {'xh','c','zl','y','xl'}, dimensions={0} | all-to-all | bytes 2097152 | tf_op jit(solution)/shard_map/all_to_all | solution.py:586
  247.0 1.3 space_last.1
  248.3 0.1 pad_maximum_fusion
  248.4 34.7 %all_to_all.57 = f32[16,4,8,512]{3,2,1,0:T(8,128)S(1)} all-to-all(f32[16,4,8,512]{3,2,1,0:T(8,128)S(1)} %pad_maximum_fusion), channel_id=1, replica_groups=mesh['xh'=2,'c'=2,'zh'=4,'zl'=2,'y'=4,'xl'=2] {'zh','xh','c'}, dimensions={0} | all-to-all | bytes 2097152 | tf_op jit(solution)/shard_map/all_to_all | solution.py:595
  283.0 0.1 reduce_sum.9
  283.1 0.7 copy_bitcast_fusion
  (33 shorter events, 0.1 us)
Async XLA Ops:
  4.0 65.3 %copy-start = (f32[2,8,128,128]{3,2,1,0:T(8,128)S(1)}, f32[2,8,128,128]{3,2,1,0:T(8,128)}, u32[]{:S(2)}) copy-start(f32[2,8,128,128]{3,2,1,0:T(8,128)} %constant.162.clone.twiddle) | copy-start | bytes 3145732
  4.0 65.3 %copy-start.2 = (bf16[256,768]{1,0:T(8,128)(2,1)S(1)}, bf16[256,768]{1,0:T(8,128)(2,1)}, u32[]{:S(2)}) copy-start(bf16[256,768]{1,0:T(8,128)(2,1)} %constant.160.clone.left_inverse) | copy-start | bytes 1179652
  4.0 65.3 %copy-start.3 = (bf16[256,768]{1,0:T(8,128)(2,1)S(1)}, bf16[256,768]{1,0:T(8,128)(2,1)}, u32[]{:S(2)}) copy-start(bf16[256,768]{1,0:T(8,128)(2,1)} %constant.159.clone.left) | copy-start | bytes 1179652
  4.0 23.3 %all-to-all-start = ((f32[64,32,128]{2,1,0:T(8,128)}), f32[64,32,128]{2,1,0:T(8,128)}, u32[]{:S(2)}, u32[]{:S(2)}) async-start(f32[64,32,128]{2,1,0:T(8,128)} %get-tuple-element.19), calls=%async_computation | async-start | bytes 2097152 | tf_op jit(solution)/shard_map/all_to_all | solution.py:574
  11.6 14.8 %collective-permute-start.1 = (f32[4,8,2048]{2,1,0:T(8,128)}, f32[4,8,2048]{2,1,0:T(8,128)S(1)}, u32[]{:S(2)}, u32[]{:S(2)}) collective-permute-start(f32[4,8,2048]{2,1,0:T(8,128)} %get-tuple-element.20.refs_0_), channel_id=1, source_target_pairs={{0,48},{16,0},{32,16},{48,32},{1,49},{17,1},{33,17},{49,33},{2,50}... | collective-permute-start | bytes 786440 | tf_op jit(solution)/shard_map/ppermute | solution.py:573
  16.0 11.3 %collective-permute-start = (f32[4,8,2048]{2,1,0:T(8,128)}, f32[4,8,2048]{2,1,0:T(8,128)S(1)}, u32[]{:S(2)}, u32[]{:S(2)}) collective-permute-start(f32[4,8,2048]{2,1,0:T(8,128)} %get-tuple-element.20.refs_0_), channel_id=1, source_target_pairs={{0,16},{16,32},{32,48},{48,0},{1,17},{17,33},{33,49},{49,1},{2,18}... | collective-permute-start | bytes 786440 | tf_op jit(solution)/shard_map/ppermute | solution.py:572
  27.3 14.9 %copy-start.5 = (f32[4,8,2048]{2,1,0:T(8,128)}, f32[4,8,2048]{2,1,0:T(8,128)S(1)}, u32[]{:S(2)}) copy-start(f32[4,8,2048]{2,1,0:T(8,128)S(1)} %collective-permute-done.refs_1_) | copy-start | bytes 786436
  27.3 41.9 %all-to-all-start.1 = ((f32[64,32,128]{2,1,0:T(8,128)}), f32[64,32,128]{2,1,0:T(8,128)}, u32[]{:S(2)}, u32[]{:S(2)}) async-start(f32[64,32,128]{2,1,0:T(8,128)} %all-to-all-done), calls=%async_computation.1 | async-start | bytes 2097152 | tf_op jit(solution)/shard_map/all_to_all | solution.py:580
  38.8 61.9 %copy-start.1 = (bf16[768,256]{1,0:T(8,128)(2,1)S(1)}, bf16[768,256]{1,0:T(8,128)(2,1)}, u32[]{:S(2)}) copy-start(bf16[768,256]{1,0:T(8,128)(2,1)} %constant.157.clone.table) | copy-start | bytes 1179652
  38.9 29.1 %collective-permute-start.3 = (f32[2,8,2048]{2,1,0:T(8,128)S(1)}, f32[2,8,2048]{2,1,0:T(8,128)S(1)}, u32[]{:S(2)}, u32[]{:S(2)}) collective-permute-start(f32[2,8,2048]{2,1,0:T(8,128)S(1)} %slice.7), channel_id=1, source_target_pairs={{0,48},{16,0},{32,16},{48,32},{1,49},{17,1},{33,17},{49,33},{2,50}... | collective-permute-start | bytes 393224 | tf_op jit(solution)/shard_map/ppermute | solution.py:578
  42.2 26.4 %collective-permute-start.2 = (f32[2,8,2048]{2,1,0:T(8,128)S(1)}, f32[2,8,2048]{2,1,0:T(8,128)S(1)}, u32[]{:S(2)}, u32[]{:S(2)}) collective-permute-start(f32[2,8,2048]{2,1,0:T(8,128)S(1)} %slice.6), channel_id=1, source_target_pairs={{0,16},{16,32},{32,48},{48,0},{1,17},{17,33},{33,49},{49,1},{2,18}... | collective-permute-start | bytes 393224 | tf_op jit(solution)/shard_map/ppermute | solution.py:577
  67.9 0.7 copy-start.9
  68.6 0.6 copy-start.11
  69.3 31.5 %copy-start.4 = (bf16[768,256]{1,0:T(8,128)(2,1)S(1)}, bf16[768,256]{1,0:T(8,128)(2,1)}, u32[]{:S(2)}) copy-start(bf16[768,256]{1,0:T(8,128)(2,1)} %constant.158.clone.inverse_table) | copy-start | bytes 1179652
  69.3 31.5 %copy-start.6 = (f32[4,8,2048]{2,1,0:T(8,128)S(1)}, f32[4,8,2048]{2,1,0:T(8,128)}, u32[]{:S(2)}) copy-start(f32[4,8,2048]{2,1,0:T(8,128)} %copy-done.5) | copy-start | bytes 786436
  69.3 31.5 %copy-start.7 = (f32[4,8,2048]{2,1,0:T(8,128)S(1)}, f32[4,8,2048]{2,1,0:T(8,128)}, u32[]{:S(2)}) copy-start(f32[4,8,2048]{2,1,0:T(8,128)} %get-tuple-element.20.refs_0_) | copy-start | bytes 786436
  69.3 31.5 %copy-start.8 = (f32[16,8,256]{2,1,0:T(8,128)S(1)}, f32[16,8,256]{2,1,0:T(8,128)}, u32[]{:S(2)}) copy-start(f32[16,8,256]{2,1,0:T(8,128)} %constant.161.clone.twiddle) | copy-start | bytes 393220
  69.3 31.5 %copy-start.12 = (f32[2,8,2048]{2,1,0:T(8,128)S(1)}, f32[2,8,2048]{2,1,0:T(8,128)}, u32[]{:S(2)}) copy-start(f32[2,8,2048]{2,1,0:T(8,128)} %copy-done.11) | copy-start | bytes 393220
  151.6 46.7 %copy-start.10 = (f32[2,8,2048]{2,1,0:T(8,128)S(1)}, f32[2,8,2048]{2,1,0:T(8,128)}, u32[]{:S(2)}) copy-start(f32[2,8,2048]{2,1,0:T(8,128)} %copy-done.9) | copy-start | bytes 393220

commit v6 on v5

--- a/solution.py
+++ b/solution.py
@@ -192,6 +192,18 @@
     return sine_out, cosine_out
 
 
+def rotation(half_angle):
+    square = half_angle * half_angle
+    sine = 1.0 / 120.0 + square * (-1.0 / 5040.0 + square * (1.0 / 362880.0 - square * (1.0 / 39916800.0)))
+    sine = half_angle * (1.0 + square * (-1.0 / 6.0 + square * sine))
+    cosine = -1.0 / 720.0 + square * (
+        1.0 / 40320.0 + square * (-1.0 / 3628800.0 + square * (1.0 / 479001600.0))
+    )
+    cosine = 1.0 + square * (-0.5 + square * (1.0 / 24.0 + square * cosine))
+    double = sine + sine
+    return double * cosine, 1.0 - double * sine
+
+
 def lanes(a):
     return slice(a * INNER, (a + 1) * INNER)
 
@@ -263,6 +275,7 @@
     half_rows = ROWS // 2
     strips, part_rows = image.shape[0], image.shape[2]
     width = image.shape[3]
+    half_angular = 0.5 * angular
 
     for turn in range(strips):
         strip = lax.rem(freq + strips - turn, strips)
@@ -270,7 +283,7 @@
         second = pl.ds(pl.multiple_of(half_rows + strip * part_rows, part_rows), part_rows)
         for a in range(SIZE // 512):
             columns = slice(a * 512, (a + 1) * 512)
-            sine, cosine = sine_cosine(angular * (slow[turn][places[turn], :, columns] - 1.0))
+            sine, cosine = rotation(half_angular * (slow[turn][places[turn], :, columns] - 1.0))
             turned = []
             for rows in (first, second):
                 real, imag = wave[0, rows, columns], wave[1, rows, columns]

time: 284 us -> 284 us (level)
  no operation moved by 1% of the time
where the time goes in v6:
time: 284 us; the launch traced here: 283 us
  blocking collectives  196 us (69%)
  waiting for transfers between devices  35.9 us (13%)
  starting transfers between devices  26.7 us (9%)
  Pallas kernels  21.3 us (8%)
    all_to_all x4, blocking collectives, per_device(): chunks = lax.all_to_all(chunks, slab, 0, 0, tiled=True)  94.3 us
    all_to_all x3, blocking collectives, per_device(): chunks = lax.all_to_all(result[0], slab, 0, 0, tiled=True)  66.8 us
    all_to_all x1, blocking collectives, per_device(): picture = lax.all_to_all(picture, ('zh', 'xh', 'c'), 0, 0, tiled=True)  34.7 us
    ppermute x1, waiting for transfers between devices, per_device(): lax.ppermute(above[middle:], 'zh', down)  24.6 us
    all_to_all x1, starting transfers between devices, per_device(): chunks = lax.all_to_all(chunks, ('zh', 'zl', 'y', 'xl'), 0, 0, tiled=True)  11.4 us
    ppermute x1, waiting for transfers between devices, per_device(): above = lax.ppermute(parts, 'zh', down)  10.4 us
    pallas_call x4, Pallas kernels, spectral_step(): pl.pallas_call(functools.partial(spectral_kernel, slab_in), out_shape=CHU...  10.3 us
    all_to_all x1, starting transfers between devices, per_device(): chunks = lax.all_to_all(chunks, ('xh', 'c'), 0, 0, tiled=True)  7.58 us
  transfers between devices with their start and end apart: 6, of which 3 were waited for; matrix products, arithmetic and copies ran while one was open for 0% of the time, Pallas kernels for 0%

profile of v6, /device:TPU:1, one launch (start us, length us, event | category | flops | bytes accessed | tf_op | source)
XLA Modules:
  0.0 283.5 jit_solution(16759405165885898169)
XLA Ops:
  0.0 4.0 %encode_forward.1 = (f32[64,32,128]{2,1,0:T(8,128)}, f32[4,8,2048]{2,1,0:T(8,128)}) custom-call(s32[1,2,4]{2,1,0:T(2,128)} %phases.1, s32[4]{0:T(128)} %places.1, f32[2,8]{1,0:T(2,128)} %constant.163.clone.turns, bf16[2,1,2,32,2048]{4,3,2,1,0:T(8,128)(2,1)} %source.1, bf16[2,1,2,32,2048]{4,3,2,1,0:T(8,128)(2,1)} %recorded.1, ...), custom_call_target="tpu_custom_call" | custom-call | tf_op jit(solution)/shard_map/encode_forward/pallas_call | solution.py:413
  4.0 0.0 copy-start
  4.0 0.0 copy-start.2
  4.0 7.6 %all-to-all-start = ((f32[64,32,128]{2,1,0:T(8,128)}), f32[64,32,128]{2,1,0:T(8,128)}, u32[]{:S(2)}, u32[]{:S(2)}) async-start(f32[64,32,128]{2,1,0:T(8,128)} %get-tuple-element.19), calls=%async_computation | async-start | bytes 2097152 | tf_op jit(solution)/shard_map/all_to_all | solution.py:587
  11.6 4.4 %collective-permute-start.1 = (f32[4,8,2048]{2,1,0:T(8,128)}, f32[4,8,2048]{2,1,0:T(8,128)S(1)}, u32[]{:S(2)}, u32[]{:S(2)}) collective-permute-start(f32[4,8,2048]{2,1,0:T(8,128)} %get-tuple-element.20.refs_0_), channel_id=1, source_target_pairs={{0,48},{16,0},{32,16},{48,32},{1,49},{17,1},{33,17},{49,33},{2,50}... | collective-permute-start | bytes 786440 | tf_op jit(solution)/shard_map/ppermute | solution.py:586
  16.0 10.4 %collective-permute-done.1.refs_3_ = f32[4,8,2048]{2,1,0:T(8,128)S(1)} collective-permute-done((f32[4,8,2048]{2,1,0:T(8,128)}, f32[4,8,2048]{2,1,0:T(8,128)S(1)}, u32[]{:S(2)}, u32[]{:S(2)}) %collective-permute-start.1) | collective-permute-done | bytes 262176 | tf_op jit(solution)/shard_map/ppermute | solution.py:586
  26.4 0.9 collective-permute-done.refs_1_
  27.3 11.4 %all-to-all-start.1 = ((f32[64,32,128]{2,1,0:T(8,128)}), f32[64,32,128]{2,1,0:T(8,128)}, u32[]{:S(2)}, u32[]{:S(2)}) async-start(f32[64,32,128]{2,1,0:T(8,128)} %all-to-all-done), calls=%async_computation.1 | async-start | bytes 2097152 | tf_op jit(solution)/shard_map/all_to_all | solution.py:593
  38.9 3.3 %collective-permute-start.3 = (f32[2,8,2048]{2,1,0:T(8,128)S(1)}, f32[2,8,2048]{2,1,0:T(8,128)S(1)}, u32[]{:S(2)}, u32[]{:S(2)}) collective-permute-start(f32[2,8,2048]{2,1,0:T(8,128)S(1)} %slice.7), channel_id=1, source_target_pairs={{0,48},{16,0},{32,16},{48,32},{1,49},{17,1},{33,17},{49,33},{2,50}... | collective-permute-start | bytes 393224 | tf_op jit(solution)/shard_map/ppermute | solution.py:591
  42.2 1.1 fusion.10
  43.4 24.6 %collective-permute-done.3.refs_2_ = f32[2,8,2048]{2,1,0:T(8,128)S(1)} collective-permute-done((f32[2,8,2048]{2,1,0:T(8,128)S(1)}, f32[2,8,2048]{2,1,0:T(8,128)S(1)}, u32[]{:S(2)}, u32[]{:S(2)}) %collective-permute-start.3) | collective-permute-done | bytes 131104 | tf_op jit(solution)/shard_map/ppermute | solution.py:591
  67.9 0.7 copy-done.9
  68.6 0.6 copy-done.11
  69.3 3.6 %spectral_step.4 = f32[64,32,128]{2,1,0:T(8,128)S(1)} custom-call(f32[64,32,128]{2,1,0:T(8,128)} %all-to-all-done.1.chunks, bf16[256,768]{1,0:T(8,128)(2,1)S(1)} %copy-done.3, bf16[256,768]{1,0:T(8,128)(2,1)S(1)} %copy-done.2, f32[2,8,128,128]{3,2,1,0:T(8,128)S(1)} %copy-done, f32[8,128,128]{2,1,0:T(8,128)S(1)} %get-tuple-element.34.prop_real, ...), custom_call_target="tpu_custom_call" | custom-call | tf_op jit(solution)/shard_map/spectral_step/pallas_call | solution.py:534
  72.9 27.9 %all_to_all.50.chunks = f32[64,32,128]{2,1,0:T(8,128)S(1)} all-to-all(f32[64,32,128]{2,1,0:T(8,128)S(1)} %spectral_step.4), channel_id=1, replica_groups=mesh['xh'=2,'c'=2,'zh'=4,'zl'=2,'y'=4,'xl'=2] {'xh','c','zl','y','xl'}, dimensions={0} | all-to-all | bytes 2097152 | tf_op jit(solution)/shard_map/all_to_all | solution.py:599
  100.8 2.0 space_step.3
  102.8 22.3 %all_to_all.51.chunks = f32[64,32,128]{2,1,0:T(8,128)S(1)} all-to-all(f32[64,32,128]{2,1,0:T(8,128)S(1)} %get-tuple-element.27), channel_id=1, replica_groups=mesh['xh'=2,'c'=2,'zh'=4,'zl'=2,'y'=4,'xl'=2] {'xh','c','zl','y','xl'}, dimensions={0} | all-to-all | bytes 2097152 | tf_op jit(solution)/shard_map/all_to_all | solution.py:605
  125.0 2.2 spectral_step.5
  127.3 22.1 %all_to_all.52.chunks = f32[64,32,128]{2,1,0:T(8,128)S(1)} all-to-all(f32[64,32,128]{2,1,0:T(8,128)S(1)} %spectral_step.5), channel_id=1, replica_groups=mesh['xh'=2,'c'=2,'zh'=4,'zl'=2,'y'=4,'xl'=2] {'xh','c','zl','y','xl'}, dimensions={0} | all-to-all | bytes 2097152 | tf_op jit(solution)/shard_map/all_to_all | solution.py:599
  149.4 2.0 space_step.4
  151.4 22.3 %all_to_all.53.chunks = f32[64,32,128]{2,1,0:T(8,128)S(1)} all-to-all(f32[64,32,128]{2,1,0:T(8,128)S(1)} %get-tuple-element.29), channel_id=1, replica_groups=mesh['xh'=2,'c'=2,'zh'=4,'zl'=2,'y'=4,'xl'=2] {'xh','c','zl','y','xl'}, dimensions={0} | all-to-all | bytes 2097152 | tf_op jit(solution)/shard_map/all_to_all | solution.py:605
  173.7 2.2 spectral_step.6
  175.9 22.1 %all_to_all.54.chunks = f32[64,32,128]{2,1,0:T(8,128)S(1)} all-to-all(f32[64,32,128]{2,1,0:T(8,128)S(1)} %spectral_step.6), channel_id=1, replica_groups=mesh['xh'=2,'c'=2,'zh'=4,'zl'=2,'y'=4,'xl'=2] {'xh','c','zl','y','xl'}, dimensions={0} | all-to-all | bytes 2097152 | tf_op jit(solution)/shard_map/all_to_all | solution.py:599
  198.0 2.0 space_step.5
  200.0 22.3 %all_to_all.55.chunks = f32[64,32,128]{2,1,0:T(8,128)S(1)} all-to-all(f32[64,32,128]{2,1,0:T(8,128)S(1)} %get-tuple-element.32), channel_id=1, replica_groups=mesh['xh'=2,'c'=2,'zh'=4,'zl'=2,'y'=4,'xl'=2] {'xh','c','zl','y','xl'}, dimensions={0} | all-to-all | bytes 2097152 | tf_op jit(solution)/shard_map/all_to_all | solution.py:605
  222.3 2.2 spectral_step.7
  224.5 22.1 %all_to_all.56.chunks = f32[64,32,128]{2,1,0:T(8,128)S(1)} all-to-all(f32[64,32,128]{2,1,0:T(8,128)S(1)} %spectral_step.7), channel_id=1, replica_groups=mesh['xh'=2,'c'=2,'zh'=4,'zl'=2,'y'=4,'xl'=2] {'xh','c','zl','y','xl'}, dimensions={0} | all-to-all | bytes 2097152 | tf_op jit(solution)/shard_map/all_to_all | solution.py:599
  246.7 1.2 space_last.1
  247.9 0.1 pad_maximum_fusion
  248.0 34.7 %all_to_all.57 = f32[16,4,8,512]{3,2,1,0:T(8,128)S(1)} all-to-all(f32[16,4,8,512]{3,2,1,0:T(8,128)S(1)} %pad_maximum_fusion), channel_id=1, replica_groups=mesh['xh'=2,'c'=2,'zh'=4,'zl'=2,'y'=4,'xl'=2] {'zh','xh','c'}, dimensions={0} | all-to-all | bytes 2097152 | tf_op jit(solution)/shard_map/all_to_all | solution.py:608
  282.7 0.1 reduce_sum.9
  282.8 0.7 copy_bitcast_fusion
  (33 shorter events, 0.1 us)
Async XLA Ops:
  4.0 65.3 %copy-start = (f32[2,8,128,128]{3,2,1,0:T(8,128)S(1)}, f32[2,8,128,128]{3,2,1,0:T(8,128)}, u32[]{:S(2)}) copy-start(f32[2,8,128,128]{3,2,1,0:T(8,128)} %constant.162.clone.twiddle) | copy-start | bytes 3145732
  4.0 65.3 %copy-start.2 = (bf16[256,768]{1,0:T(8,128)(2,1)S(1)}, bf16[256,768]{1,0:T(8,128)(2,1)}, u32[]{:S(2)}) copy-start(bf16[256,768]{1,0:T(8,128)(2,1)} %constant.160.clone.left_inverse) | copy-start | bytes 1179652
  4.0 65.3 %copy-start.3 = (bf16[256,768]{1,0:T(8,128)(2,1)S(1)}, bf16[256,768]{1,0:T(8,128)(2,1)}, u32[]{:S(2)}) copy-start(bf16[256,768]{1,0:T(8,128)(2,1)} %constant.159.clone.left) | copy-start | bytes 1179652
  4.0 23.3 %all-to-all-start = ((f32[64,32,128]{2,1,0:T(8,128)}), f32[64,32,128]{2,1,0:T(8,128)}, u32[]{:S(2)}, u32[]{:S(2)}) async-start(f32[64,32,128]{2,1,0:T(8,128)} %get-tuple-element.19), calls=%async_computation | async-start | bytes 2097152 | tf_op jit(solution)/shard_map/all_to_all | solution.py:587
  11.6 14.8 %collective-permute-start.1 = (f32[4,8,2048]{2,1,0:T(8,128)}, f32[4,8,2048]{2,1,0:T(8,128)S(1)}, u32[]{:S(2)}, u32[]{:S(2)}) collective-permute-start(f32[4,8,2048]{2,1,0:T(8,128)} %get-tuple-element.20.refs_0_), channel_id=1, source_target_pairs={{0,48},{16,0},{32,16},{48,32},{1,49},{17,1},{33,17},{49,33},{2,50}... | collective-permute-start | bytes 786440 | tf_op jit(solution)/shard_map/ppermute | solution.py:586
  16.0 11.3 %collective-permute-start = (f32[4,8,2048]{2,1,0:T(8,128)}, f32[4,8,2048]{2,1,0:T(8,128)S(1)}, u32[]{:S(2)}, u32[]{:S(2)}) collective-permute-start(f32[4,8,2048]{2,1,0:T(8,128)} %get-tuple-element.20.refs_0_), channel_id=1, source_target_pairs={{0,16},{16,32},{32,48},{48,0},{1,17},{17,33},{33,49},{49,1},{2,18}... | collective-permute-start | bytes 786440 | tf_op jit(solution)/shard_map/ppermute | solution.py:585
  27.3 14.9 %copy-start.5 = (f32[4,8,2048]{2,1,0:T(8,128)}, f32[4,8,2048]{2,1,0:T(8,128)S(1)}, u32[]{:S(2)}) copy-start(f32[4,8,2048]{2,1,0:T(8,128)S(1)} %collective-permute-done.refs_1_) | copy-start | bytes 786436
  27.3 41.9 %all-to-all-start.1 = ((f32[64,32,128]{2,1,0:T(8,128)}), f32[64,32,128]{2,1,0:T(8,128)}, u32[]{:S(2)}, u32[]{:S(2)}) async-start(f32[64,32,128]{2,1,0:T(8,128)} %all-to-all-done), calls=%async_computation.1 | async-start | bytes 2097152 | tf_op jit(solution)/shard_map/all_to_all | solution.py:593
  38.8 61.9 %copy-start.1 = (bf16[768,256]{1,0:T(8,128)(2,1)S(1)}, bf16[768,256]{1,0:T(8,128)(2,1)}, u32[]{:S(2)}) copy-start(bf16[768,256]{1,0:T(8,128)(2,1)} %constant.157.clone.table) | copy-start | bytes 1179652
  38.9 29.1 %collective-permute-start.3 = (f32[2,8,2048]{2,1,0:T(8,128)S(1)}, f32[2,8,2048]{2,1,0:T(8,128)S(1)}, u32[]{:S(2)}, u32[]{:S(2)}) collective-permute-start(f32[2,8,2048]{2,1,0:T(8,128)S(1)} %slice.7), channel_id=1, source_target_pairs={{0,48},{16,0},{32,16},{48,32},{1,49},{17,1},{33,17},{49,33},{2,50}... | collective-permute-start | bytes 393224 | tf_op jit(solution)/shard_map/ppermute | solution.py:591
  42.2 26.4 %collective-permute-start.2 = (f32[2,8,2048]{2,1,0:T(8,128)S(1)}, f32[2,8,2048]{2,1,0:T(8,128)S(1)}, u32[]{:S(2)}, u32[]{:S(2)}) collective-permute-start(f32[2,8,2048]{2,1,0:T(8,128)S(1)} %slice.6), channel_id=1, source_target_pairs={{0,16},{16,32},{32,48},{48,0},{1,17},{17,33},{33,49},{49,1},{2,18}... | collective-permute-start | bytes 393224 | tf_op jit(solution)/shard_map/ppermute | solution.py:590
  67.9 0.7 copy-start.9
  68.6 0.6 copy-start.11
  69.3 31.5 %copy-start.4 = (bf16[768,256]{1,0:T(8,128)(2,1)S(1)}, bf16[768,256]{1,0:T(8,128)(2,1)}, u32[]{:S(2)}) copy-start(bf16[768,256]{1,0:T(8,128)(2,1)} %constant.158.clone.inverse_table) | copy-start | bytes 1179652
  69.3 31.5 %copy-start.6 = (f32[4,8,2048]{2,1,0:T(8,128)S(1)}, f32[4,8,2048]{2,1,0:T(8,128)}, u32[]{:S(2)}) copy-start(f32[4,8,2048]{2,1,0:T(8,128)} %copy-done.5) | copy-start | bytes 786436
  69.3 31.5 %copy-start.7 = (f32[4,8,2048]{2,1,0:T(8,128)S(1)}, f32[4,8,2048]{2,1,0:T(8,128)}, u32[]{:S(2)}) copy-start(f32[4,8,2048]{2,1,0:T(8,128)} %get-tuple-element.20.refs_0_) | copy-start | bytes 786436
  69.3 31.5 %copy-start.8 = (f32[16,8,256]{2,1,0:T(8,128)S(1)}, f32[16,8,256]{2,1,0:T(8,128)}, u32[]{:S(2)}) copy-start(f32[16,8,256]{2,1,0:T(8,128)} %constant.161.clone.twiddle) | copy-start | bytes 393220
  69.3 31.5 %copy-start.12 = (f32[2,8,2048]{2,1,0:T(8,128)S(1)}, f32[2,8,2048]{2,1,0:T(8,128)}, u32[]{:S(2)}) copy-start(f32[2,8,2048]{2,1,0:T(8,128)} %copy-done.11) | copy-start | bytes 393220
  151.4 46.7 %copy-start.10 = (f32[2,8,2048]{2,1,0:T(8,128)S(1)}, f32[2,8,2048]{2,1,0:T(8,128)}, u32[]{:S(2)}) copy-start(f32[2,8,2048]{2,1,0:T(8,128)} %copy-done.9) | copy-start | bytes 393220

commit v7 on v5

--- a/solution.py
+++ b/solution.py
@@ -282,7 +282,7 @@
             picture = turned[0][0] * turned[1][0] - turned[0][1] * turned[1][1]
             place = a * 512 // width
             offset = a * 512 % width
-            image[strip, place, :, offset : offset + 512] = picture * (1.0 / strips)
+            image[place, strip, :, offset : offset + 512] = picture * (1.0 / strips)
 
 
 def fetch(pairs, semaphores):
@@ -592,8 +592,8 @@
             chunks = lax.all_to_all(result[0], slab, 0, 0, tiled=True)
     picture = jnp.stack(pictures, axis=2)
     picture = picture.reshape((freqs * freqs,) + picture.shape[2:])
-    picture = lax.all_to_all(picture, ("zh", "xh", "c"), 0, 0, tiled=True)
-    picture = jnp.sum(picture.reshape((freqs, freqs) + picture.shape[1:]), axis=0)
+    picture = lax.all_to_all(picture, ("xh", "c", "zh"), 0, 0, tiled=True)
+    picture = jnp.sum(picture.reshape((freqs, freqs) + picture.shape[1:]), axis=1)
     return picture.transpose(1, 0, 2, 3).reshape(DEPTHS, ROWS // 2, SIZE // freqs)
 
 

time: 284 us -> 284 us (level)
  no operation moved by 1% of the time
where the time goes in v7:
time: 284 us; the launch traced here: 283 us
  blocking collectives  195 us (69%)
  waiting for transfers between devices  35.9 us (13%)
  starting transfers between devices  26.7 us (9%)
  Pallas kernels  21.7 us (8%)
    all_to_all x4, blocking collectives, per_device(): chunks = lax.all_to_all(chunks, slab, 0, 0, tiled=True)  94.3 us
    all_to_all x3, blocking collectives, per_device(): chunks = lax.all_to_all(result[0], slab, 0, 0, tiled=True)  66.9 us
    all_to_all x1, blocking collectives, per_device(): picture = lax.all_to_all(picture, ('xh', 'c', 'zh'), 0, 0, tiled=True)  33.9 us
    ppermute x1, waiting for transfers between devices, per_device(): lax.ppermute(above[middle:], 'zh', down)  24.6 us
    all_to_all x1, starting transfers between devices, per_device(): chunks = lax.all_to_all(chunks, ('zh', 'zl', 'y', 'xl'), 0, 0, tiled=True)  11.4 us
    ppermute x1, waiting for transfers between devices, per_device(): above = lax.ppermute(parts, 'zh', down)  10.4 us
    pallas_call x4, Pallas kernels, spectral_step(): pl.pallas_call(functools.partial(spectral_kernel, slab_in), out_shape=CHU...  10.3 us
    all_to_all x1, starting transfers between devices, per_device(): chunks = lax.all_to_all(chunks, ('xh', 'c'), 0, 0, tiled=True)  7.58 us
  transfers between devices with their start and end apart: 6, of which 3 were waited for; matrix products, arithmetic and copies ran while one was open for 0% of the time, Pallas kernels for 0%

profile of v7, /device:TPU:1, one launch (start us, length us, event | category | flops | bytes accessed | tf_op | source)
XLA Modules:
  0.0 283.0 jit_solution(4661102224200689769)
XLA Ops:
  0.0 4.0 %encode_forward.1 = (f32[64,32,128]{2,1,0:T(8,128)}, f32[4,8,2048]{2,1,0:T(8,128)}) custom-call(s32[1,2,4]{2,1,0:T(2,128)} %phases.1, s32[4]{0:T(128)} %places.1, f32[2,8]{1,0:T(2,128)} %constant.163.clone.turns, bf16[2,1,2,32,2048]{4,3,2,1,0:T(8,128)(2,1)} %source.1, bf16[2,1,2,32,2048]{4,3,2,1,0:T(8,128)(2,1)} %recorded.1, ...), custom_call_target="tpu_custom_call" | custom-call | tf_op jit(solution)/shard_map/encode_forward/pallas_call | solution.py:400
  4.0 0.0 copy-start
  4.0 0.0 copy-start.2
  4.0 7.6 %all-to-all-start = ((f32[64,32,128]{2,1,0:T(8,128)}), f32[64,32,128]{2,1,0:T(8,128)}, u32[]{:S(2)}, u32[]{:S(2)}) async-start(f32[64,32,128]{2,1,0:T(8,128)} %get-tuple-element.19), calls=%async_computation | async-start | bytes 2097152 | tf_op jit(solution)/shard_map/all_to_all | solution.py:574
  11.6 4.4 %collective-permute-start.1 = (f32[4,8,2048]{2,1,0:T(8,128)}, f32[4,8,2048]{2,1,0:T(8,128)S(1)}, u32[]{:S(2)}, u32[]{:S(2)}) collective-permute-start(f32[4,8,2048]{2,1,0:T(8,128)} %get-tuple-element.20.refs_0_), channel_id=1, source_target_pairs={{0,48},{16,0},{32,16},{48,32},{1,49},{17,1},{33,17},{49,33},{2,50}... | collective-permute-start | bytes 786440 | tf_op jit(solution)/shard_map/ppermute | solution.py:573
  16.0 10.4 %collective-permute-done.1.refs_3_ = f32[4,8,2048]{2,1,0:T(8,128)S(1)} collective-permute-done((f32[4,8,2048]{2,1,0:T(8,128)}, f32[4,8,2048]{2,1,0:T(8,128)S(1)}, u32[]{:S(2)}, u32[]{:S(2)}) %collective-permute-start.1) | collective-permute-done | bytes 262176 | tf_op jit(solution)/shard_map/ppermute | solution.py:573
  26.4 0.9 collective-permute-done.refs_1_
  27.3 11.4 %all-to-all-start.1 = ((f32[64,32,128]{2,1,0:T(8,128)}), f32[64,32,128]{2,1,0:T(8,128)}, u32[]{:S(2)}, u32[]{:S(2)}) async-start(f32[64,32,128]{2,1,0:T(8,128)} %all-to-all-done), calls=%async_computation.1 | async-start | bytes 2097152 | tf_op jit(solution)/shard_map/all_to_all | solution.py:580
  38.9 3.3 %collective-permute-start.3 = (f32[2,8,2048]{2,1,0:T(8,128)S(1)}, f32[2,8,2048]{2,1,0:T(8,128)S(1)}, u32[]{:S(2)}, u32[]{:S(2)}) collective-permute-start(f32[2,8,2048]{2,1,0:T(8,128)S(1)} %slice.7), channel_id=1, source_target_pairs={{0,48},{16,0},{32,16},{48,32},{1,49},{17,1},{33,17},{49,33},{2,50}... | collective-permute-start | bytes 393224 | tf_op jit(solution)/shard_map/ppermute | solution.py:578
  42.2 1.1 fusion.10
  43.4 24.6 %collective-permute-done.3.refs_2_ = f32[2,8,2048]{2,1,0:T(8,128)S(1)} collective-permute-done((f32[2,8,2048]{2,1,0:T(8,128)S(1)}, f32[2,8,2048]{2,1,0:T(8,128)S(1)}, u32[]{:S(2)}, u32[]{:S(2)}) %collective-permute-start.3) | collective-permute-done | bytes 131104 | tf_op jit(solution)/shard_map/ppermute | solution.py:578
  67.9 0.7 copy-done.9
  68.6 0.6 copy-done.11
  69.3 3.6 %spectral_step.4 = f32[64,32,128]{2,1,0:T(8,128)S(1)} custom-call(f32[64,32,128]{2,1,0:T(8,128)} %all-to-all-done.1.chunks, bf16[256,768]{1,0:T(8,128)(2,1)S(1)} %copy-done.3, bf16[256,768]{1,0:T(8,128)(2,1)S(1)} %copy-done.2, f32[2,8,128,128]{3,2,1,0:T(8,128)S(1)} %copy-done, f32[8,128,128]{2,1,0:T(8,128)S(1)} %get-tuple-element.34.prop_real, ...), custom_call_target="tpu_custom_call" | custom-call | tf_op jit(solution)/shard_map/spectral_step/pallas_call | solution.py:521
  72.9 27.9 %all_to_all.50.chunks = f32[64,32,128]{2,1,0:T(8,128)S(1)} all-to-all(f32[64,32,128]{2,1,0:T(8,128)S(1)} %spectral_step.4), channel_id=1, replica_groups=mesh['xh'=2,'c'=2,'zh'=4,'zl'=2,'y'=4,'xl'=2] {'xh','c','zl','y','xl'}, dimensions={0} | all-to-all | bytes 2097152 | tf_op jit(solution)/shard_map/all_to_all | solution.py:586
  100.8 2.0 space_step.3
  102.9 22.3 %all_to_all.51.chunks = f32[64,32,128]{2,1,0:T(8,128)S(1)} all-to-all(f32[64,32,128]{2,1,0:T(8,128)S(1)} %get-tuple-element.27), channel_id=1, replica_groups=mesh['xh'=2,'c'=2,'zh'=4,'zl'=2,'y'=4,'xl'=2] {'xh','c','zl','y','xl'}, dimensions={0} | all-to-all | bytes 2097152 | tf_op jit(solution)/shard_map/all_to_all | solution.py:592
  125.2 2.2 spectral_step.5
  127.4 22.1 %all_to_all.52.chunks = f32[64,32,128]{2,1,0:T(8,128)S(1)} all-to-all(f32[64,32,128]{2,1,0:T(8,128)S(1)} %spectral_step.5), channel_id=1, replica_groups=mesh['xh'=2,'c'=2,'zh'=4,'zl'=2,'y'=4,'xl'=2] {'xh','c','zl','y','xl'}, dimensions={0} | all-to-all | bytes 2097152 | tf_op jit(solution)/shard_map/all_to_all | solution.py:586
  149.6 2.0 space_step.4
  151.6 22.3 %all_to_all.53.chunks = f32[64,32,128]{2,1,0:T(8,128)S(1)} all-to-all(f32[64,32,128]{2,1,0:T(8,128)S(1)} %get-tuple-element.29), channel_id=1, replica_groups=mesh['xh'=2,'c'=2,'zh'=4,'zl'=2,'y'=4,'xl'=2] {'xh','c','zl','y','xl'}, dimensions={0} | all-to-all | bytes 2097152 | tf_op jit(solution)/shard_map/all_to_all | solution.py:592
  173.9 2.2 spectral_step.6
  176.1 22.1 %all_to_all.54.chunks = f32[64,32,128]{2,1,0:T(8,128)S(1)} all-to-all(f32[64,32,128]{2,1,0:T(8,128)S(1)} %spectral_step.6), channel_id=1, replica_groups=mesh['xh'=2,'c'=2,'zh'=4,'zl'=2,'y'=4,'xl'=2] {'xh','c','zl','y','xl'}, dimensions={0} | all-to-all | bytes 2097152 | tf_op jit(solution)/shard_map/all_to_all | solution.py:586
  198.3 2.0 space_step.5
  200.3 22.3 %all_to_all.55.chunks = f32[64,32,128]{2,1,0:T(8,128)S(1)} all-to-all(f32[64,32,128]{2,1,0:T(8,128)S(1)} %get-tuple-element.32), channel_id=1, replica_groups=mesh['xh'=2,'c'=2,'zh'=4,'zl'=2,'y'=4,'xl'=2] {'xh','c','zl','y','xl'}, dimensions={0} | all-to-all | bytes 2097152 | tf_op jit(solution)/shard_map/all_to_all | solution.py:592
  222.6 2.2 spectral_step.7
  224.9 22.1 %all_to_all.56.chunks = f32[64,32,128]{2,1,0:T(8,128)S(1)} all-to-all(f32[64,32,128]{2,1,0:T(8,128)S(1)} %spectral_step.7), channel_id=1, replica_groups=mesh['xh'=2,'c'=2,'zh'=4,'zl'=2,'y'=4,'xl'=2] {'xh','c','zl','y','xl'}, dimensions={0} | all-to-all | bytes 2097152 | tf_op jit(solution)/shard_map/all_to_all | solution.py:586
  247.0 1.3 space_last.1
  248.3 0.1 pad_maximum_fusion
  248.4 33.9 %all_to_all.57 = f32[16,4,8,512]{3,2,1,0:T(8,128)S(1)} all-to-all(f32[16,4,8,512]{3,2,1,0:T(8,128)S(1)} %pad_maximum_fusion), channel_id=1, replica_groups=mesh['xh'=2,'c'=2,'zh'=4,'zl'=2,'y'=4,'xl'=2] {'xh','c','zh'}, dimensions={0} | all-to-all | bytes 2097152 | tf_op jit(solution)/shard_map/all_to_all | solution.py:595
  282.2 0.1 bitcast_reduce_fusion
  282.3 0.7 copy_bitcast_fusion
  (33 shorter events, 0.1 us)
Async XLA Ops:
  4.0 65.3 %copy-start = (f32[2,8,128,128]{3,2,1,0:T(8,128)S(1)}, f32[2,8,128,128]{3,2,1,0:T(8,128)}, u32[]{:S(2)}) copy-start(f32[2,8,128,128]{3,2,1,0:T(8,128)} %constant.162.clone.twiddle) | copy-start | bytes 3145732
  4.0 65.3 %copy-start.2 = (bf16[256,768]{1,0:T(8,128)(2,1)S(1)}, bf16[256,768]{1,0:T(8,128)(2,1)}, u32[]{:S(2)}) copy-start(bf16[256,768]{1,0:T(8,128)(2,1)} %constant.160.clone.left_inverse) | copy-start | bytes 1179652
  4.0 65.3 %copy-start.3 = (bf16[256,768]{1,0:T(8,128)(2,1)S(1)}, bf16[256,768]{1,0:T(8,128)(2,1)}, u32[]{:S(2)}) copy-start(bf16[256,768]{1,0:T(8,128)(2,1)} %constant.159.clone.left) | copy-start | bytes 1179652
  4.0 23.3 %all-to-all-start = ((f32[64,32,128]{2,1,0:T(8,128)}), f32[64,32,128]{2,1,0:T(8,128)}, u32[]{:S(2)}, u32[]{:S(2)}) async-start(f32[64,32,128]{2,1,0:T(8,128)} %get-tuple-element.19), calls=%async_computation | async-start | bytes 2097152 | tf_op jit(solution)/shard_map/all_to_all | solution.py:574
  11.6 14.8 %collective-permute-start.1 = (f32[4,8,2048]{2,1,0:T(8,128)}, f32[4,8,2048]{2,1,0:T(8,128)S(1)}, u32[]{:S(2)}, u32[]{:S(2)}) collective-permute-start(f32[4,8,2048]{2,1,0:T(8,128)} %get-tuple-element.20.refs_0_), channel_id=1, source_target_pairs={{0,48},{16,0},{32,16},{48,32},{1,49},{17,1},{33,17},{49,33},{2,50}... | collective-permute-start | bytes 786440 | tf_op jit(solution)/shard_map/ppermute | solution.py:573
  16.0 11.3 %collective-permute-start = (f32[4,8,2048]{2,1,0:T(8,128)}, f32[4,8,2048]{2,1,0:T(8,128)S(1)}, u32[]{:S(2)}, u32[]{:S(2)}) collective-permute-start(f32[4,8,2048]{2,1,0:T(8,128)} %get-tuple-element.20.refs_0_), channel_id=1, source_target_pairs={{0,16},{16,32},{32,48},{48,0},{1,17},{17,33},{33,49},{49,1},{2,18}... | collective-permute-start | bytes 786440 | tf_op jit(solution)/shard_map/ppermute | solution.py:572
  27.3 14.9 %copy-start.5 = (f32[4,8,2048]{2,1,0:T(8,128)}, f32[4,8,2048]{2,1,0:T(8,128)S(1)}, u32[]{:S(2)}) copy-start(f32[4,8,2048]{2,1,0:T(8,128)S(1)} %collective-permute-done.refs_1_) | copy-start | bytes 786436
  27.3 41.9 %all-to-all-start.1 = ((f32[64,32,128]{2,1,0:T(8,128)}), f32[64,32,128]{2,1,0:T(8,128)}, u32[]{:S(2)}, u32[]{:S(2)}) async-start(f32[64,32,128]{2,1,0:T(8,128)} %all-to-all-done), calls=%async_computation.1 | async-start | bytes 2097152 | tf_op jit(solution)/shard_map/all_to_all | solution.py:580
  38.8 61.9 %copy-start.1 = (bf16[768,256]{1,0:T(8,128)(2,1)S(1)}, bf16[768,256]{1,0:T(8,128)(2,1)}, u32[]{:S(2)}) copy-start(bf16[768,256]{1,0:T(8,128)(2,1)} %constant.157.clone.table) | copy-start | bytes 1179652
  38.9 29.1 %collective-permute-start.3 = (f32[2,8,2048]{2,1,0:T(8,128)S(1)}, f32[2,8,2048]{2,1,0:T(8,128)S(1)}, u32[]{:S(2)}, u32[]{:S(2)}) collective-permute-start(f32[2,8,2048]{2,1,0:T(8,128)S(1)} %slice.7), channel_id=1, source_target_pairs={{0,48},{16,0},{32,16},{48,32},{1,49},{17,1},{33,17},{49,33},{2,50}... | collective-permute-start | bytes 393224 | tf_op jit(solution)/shard_map/ppermute | solution.py:578
  42.2 26.4 %collective-permute-start.2 = (f32[2,8,2048]{2,1,0:T(8,128)S(1)}, f32[2,8,2048]{2,1,0:T(8,128)S(1)}, u32[]{:S(2)}, u32[]{:S(2)}) collective-permute-start(f32[2,8,2048]{2,1,0:T(8,128)S(1)} %slice.6), channel_id=1, source_target_pairs={{0,16},{16,32},{32,48},{48,0},{1,17},{17,33},{33,49},{49,1},{2,18}... | collective-permute-start | bytes 393224 | tf_op jit(solution)/shard_map/ppermute | solution.py:577
  67.9 0.7 copy-start.9
  68.6 0.6 copy-start.11
  69.3 31.5 %copy-start.4 = (bf16[768,256]{1,0:T(8,128)(2,1)S(1)}, bf16[768,256]{1,0:T(8,128)(2,1)}, u32[]{:S(2)}) copy-start(bf16[768,256]{1,0:T(8,128)(2,1)} %constant.158.clone.inverse_table) | copy-start | bytes 1179652
  69.3 31.5 %copy-start.6 = (f32[4,8,2048]{2,1,0:T(8,128)S(1)}, f32[4,8,2048]{2,1,0:T(8,128)}, u32[]{:S(2)}) copy-start(f32[4,8,2048]{2,1,0:T(8,128)} %copy-done.5) | copy-start | bytes 786436
  69.3 31.5 %copy-start.7 = (f32[4,8,2048]{2,1,0:T(8,128)S(1)}, f32[4,8,2048]{2,1,0:T(8,128)}, u32[]{:S(2)}) copy-start(f32[4,8,2048]{2,1,0:T(8,128)} %get-tuple-element.20.refs_0_) | copy-start | bytes 786436
  69.3 31.5 %copy-start.8 = (f32[16,8,256]{2,1,0:T(8,128)S(1)}, f32[16,8,256]{2,1,0:T(8,128)}, u32[]{:S(2)}) copy-start(f32[16,8,256]{2,1,0:T(8,128)} %constant.161.clone.twiddle) | copy-start | bytes 393220
  69.3 31.5 %copy-start.12 = (f32[2,8,2048]{2,1,0:T(8,128)S(1)}, f32[2,8,2048]{2,1,0:T(8,128)}, u32[]{:S(2)}) copy-start(f32[2,8,2048]{2,1,0:T(8,128)} %copy-done.11) | copy-start | bytes 393220
  151.6 46.7 %copy-start.10 = (f32[2,8,2048]{2,1,0:T(8,128)S(1)}, f32[2,8,2048]{2,1,0:T(8,128)}, u32[]{:S(2)}) copy-start(f32[2,8,2048]{2,1,0:T(8,128)} %copy-done.9) | copy-start | bytes 393220
